TPU v7x, 32 devices: a whole 2x2x4 slice. The times are simulated.
32 devices in a mesh: table: 4 (over y, core), rows: 8 (over z, x).
Axes of the slice: x: 2, y: 2, z: 4, core: 2. Of those that a mesh axis runs over, the one named last changes fastest.
Arguments:
- cells: bfloat16 [4, 512, 119, 192], P('table', 'rows'), may hold values from -6 to 6
- cotangent: bfloat16 [4, 512, 119, 192], P('table', 'rows'), may hold values from -6 to 6
- train_count: int32 [4], P('table'), may hold values from 8 to 32
- key_mask: int32 [4, 32], P('table', 'rows'), may hold values 0 or 1
- train_order: int32 [4, 32], P('table', 'rows'), may hold values from 0 to 31, each once within a row
- proj_weights: float32 [6, 192, 192], replicated, may hold values from -0.4375 to 0.4375
- out_weights: float32 [2, 192, 192], replicated
- mlp_in: float32 [192, 768], replicated, may hold values from -0.4375 to 0.4375
- mlp_out: float32 [768, 192], replicated, may hold values from -0.21875 to 0.21875
- norm_params: float32 [6, 192], replicated
- square_rows: float32 [8, 192], replicated, may hold values from 2437.12 to 9748.48
- square_cols: float32 [8, 192], replicated, may hold values from 2437.12 to 9748.48
- mlp_model_stats: float32 [2, 192], replicated, may hold values from 24371.2 to 97484.8
- mlp_hidden_stats: float32 [2, 768], replicated, may hold values from 24371.2 to 97484.8
- norm_second: float32 [6, 192], replicated, may hold values from 24371.2 to 97484.8
Outputs:
- out_cells: bfloat16 [4, 512, 119, 192], P('table', 'rows')
- cells_grad: float32 [4, 512, 119, 192], P('table', 'rows')
- proj_grad: float32 [6, 192, 192], replicated
- out_grad: float32 [2, 192, 192], replicated
- mlp_in_grad: float32 [192, 768], replicated
- mlp_out_grad: float32 [768, 192], replicated
- norm_grad: float32 [6, 192], replicated
- proj_new: float32 [6, 192, 192], replicated
- out_new: float32 [2, 192, 192], replicated
- mlp_in_new: float32 [192, 768], replicated
- mlp_out_new: float32 [768, 192], replicated
- norm_new: float32 [6, 192], replicated
- square_rows_new: float32 [8, 192], replicated
- square_cols_new: float32 [8, 192], replicated
- mlp_model_new: float32 [2, 192], replicated
- mlp_hidden_new: float32 [2, 768], replicated
- norm_second_new: float32 [6, 192], replicated
All inputs are finite; a program needn't handle non-finite values. No bound on the sum of `key_mask` on one device may be relied on, other than what follows from the above.
Results may differ from a plain program's by a relative error of at most 0.024.
Values may be sent and summed in bfloat16 or wider, within the bound.
No kernel may reach another device: no remote copies, remote signals or barrier semaphores. Data moves between devices by JAX's collectives and lax.ppermute only.
A program may use at most 768 MiB of HBM per device.

v0:
```python
import functools

import jax
import jax.numpy as jnp
import numpy as np
from jax import lax
from jax.experimental import pallas as pl
from jax.experimental.pallas import tpu as pltpu
from jax.sharding import PartitionSpec as P

BF, F32 = jnp.bfloat16, jnp.float32
D, DP = 192, 256
H, E = 6, 32
F, FP = 119, 128
FS = 120
FF = 768
STEP = 3
CLIP = 0.3
RATE = 0.5
FB = 8
SCALE = E**-0.5
SCALE2 = SCALE * 1.4426950408889634
C0 = 0.7978845608028654
C1 = 0.044715
NT = (((1,), (1,)), ((), ()))
TN = (((0,), (0,)), ((), ()))
PAIR = 576
TAIL = 2 * PAIR + 8
MID = 2 * 6 * D + 2 * PAIR + 8


def mm(a, b):
    return jnp.dot(a, b, preferred_element_type=F32)


def mm_nt(a, b):
    return lax.dot_general(a, b, NT, preferred_element_type=F32)


def mm_tn(a, b):
    return lax.dot_general(a, b, TN, preferred_element_type=F32)


def lanes():
    return lax.broadcasted_iota(jnp.int32, (1, DP), 1)


def whole(a):
    nd = len(a.shape)
    return pl.BlockSpec(a.shape, lambda *i: (0,) * nd)


def half_masks():
    lane = lax.broadcasted_iota(jnp.int32, (1, 128), 1)
    return [jnp.where((lane >= E * h) & (lane < E * (h + 1)), 1.0, 0.0).astype(BF) for h in range(4)]


def spread_halves(w, masks):
    z = jnp.zeros((w.shape[0], 128), BF)
    lo, hi = w[:, 0:128], w[:, 128:256]
    return jnp.concatenate(
        [jnp.concatenate([lo * masks[h], z], 1) for h in range(4)]
        + [jnp.concatenate([z, hi * masks[h]], 1) for h in range(2)], 0)


def mean0(a): return jnp.sum(a, 0, keepdims=True) * (1.0 / D)


def norm_t(a):
    c = a - mean0(a)
    rc = lax.rsqrt(mean0(c * c) + 1e-5)
    return c * rc, rc


def norm_back_t(g, n, rc, gain):
    dn = g * gain
    return (dn - mean0(dn) - n * mean0(dn * n)) * rc


def tall(a):
    return jnp.concatenate([a, jnp.zeros((DP - D, a.shape[1]), a.dtype)], 0)


def gelu_parts(u):
    uu = u * u
    th = jnp.tanh(u * (BF(C0) + BF(C0 * C1) * uu))
    half = BF(0.5) + BF(0.5) * th
    act = u * half
    slope = half + act * (BF(1.0) - th) * (BF(C0) + BF(3.0 * C0 * C1) * uu)
    return act, slope


def weave(streams):
    live=[[g,s,p] for g,s,p in streams]
    turn=0
    while live:
        for it in list(live):
            if turn>=it[1]:
                for _ in range(it[2]):
                    try: next(it[0])
                    except StopIteration:
                        live.remove(it); break
        turn+=1

def shape(s, t=BF):
    return jax.ShapeDtypeStruct(s, t)


def params(mib=58):
    return pltpu.CompilerParams(vmem_limit_bytes=mib << 20)


def cost(us):
    return pl.CostEstimate(flops=int(us * 1.1e9), bytes_accessed=int(us * 1e6), transcendentals=0)


def perm_matrix():
    place = np.zeros((256, 256), np.float32)
    for f in range(16):
        for r in range(16):
            place[f * 16 + r, r * 16 + f] = 1
    return jnp.asarray(place, BF)


def prep_kernel(
    proj, outw, w_in, w_outT, norms, wqkvT, wqkvI, wo, woT, wkv2, wkv2T, wq2, wq2T, wo2I, wo2, w1T, w1, w2T, w2, vec, nrow
):
    zc = jnp.zeros((D, DP - D), F32)
    zr = jnp.zeros((DP - D, DP), BF)
    row = lax.broadcasted_iota(jnp.int32, (D, DP), 0)
    eye = jnp.where(row == lax.broadcasted_iota(jnp.int32, (D, DP), 1), 1.0, 0.0).astype(BF)

    def square(w):
        a = jnp.concatenate([w, zc], 1)
        a = jnp.concatenate([a.astype(BF), zr], 0)
        return a, a.T

    for i in range(3):
        a, t = square(proj[i])
        wqkvT[i * D : (i + 1) * D, :] = t[0:D]
    wqkvI[...] = jnp.concatenate([proj[0], proj[1], proj[2], eye[:, 0:D].astype(F32)], 1).astype(BF)
    a, t = square(outw[0])
    wo[...] = a[0:D]
    woT[...] = t[0:D]
    a, t = square(proj[3])
    wq2[...] = a
    wq2T[...] = t
    a, t = square(outw[1])
    wo2[...] = a[0:D]
    wo2I[:, 0:DP] = t[0:D]
    wo2I[:, DP : 2 * DP] = eye
    for i in range(2):
        a, t = square(proj[4 + i])
        wkv2[:, i * DP : (i + 1) * DP] = a
        wkv2T[i * DP : (i + 1) * DP, :] = t
    zw = jnp.zeros((DP - D, FF), BF)
    a = w_in[...].astype(BF)
    w1[...] = a
    w1T[...] = jnp.concatenate([a, zw], 0).T
    a = w_outT[...].astype(BF)
    w2T[...] = a
    w2[...] = jnp.concatenate([a, zw], 0).T
    nrow[...] = jnp.zeros((8, DP), F32)
    nrow[0:6, 0:D] = norms[...]
    for i in range(6):
        vec[i] = jnp.broadcast_to(nrow[i : i + 1, :], (128, DP)).T[0:D]


def prepare(proj, outw, w_in, w_outT, norms):
    sq, half = shape((DP, DP)), shape((D, DP))
    outs = [shape((3 * D, DP)), shape((D, 4 * D)), half, half, shape((DP, 2 * DP)), shape((2 * DP, DP)), sq, sq]
    outs += [shape((D, 2 * DP)), half, shape((FF, DP)), shape((D, FF)), shape((D, FF)), shape((FF, DP))]
    outs += [shape((6, D, 128), F32)]
    return pl.pallas_call(
        prep_kernel,
        out_shape=outs,
        scratch_shapes=[pltpu.VMEM((8, DP), F32)],
        compiler_params=params(),
        cost_estimate=cost(4),
        name="weights",
    )(proj, outw, w_in, w_outT, norms)


def two_heads(a, b):
    z = jnp.zeros(a.shape, a.dtype)
    return jnp.concatenate([jnp.concatenate([a, z], 1), jnp.concatenate([z, b], 1)], 0)


def feature_pair(x, wqkvT_ref, woT_ref, keep, out):
    qkv = mm(wqkvT_ref[...], x)
    q = (qkv[0:D] * SCALE2).astype(BF)
    k = qkv[D : 2 * D].astype(BF)
    v = qkv[2 * D : 3 * D].astype(BF)
    yield
    row = lax.broadcasted_iota(jnp.int32, (8, 1), 0)
    outs = []
    for u in range(2):
        own = slice(u * FP, (u + 1) * FP)
        keep("qkv", u, (q[:, own], k[:, own], v[:, own]))
        ot = []
        for j in range(H // 2):
            hs = slice(64 * j, 64 * j + 64)
            qm = two_heads(q[64 * j : 64 * j + 32, own], q[64 * j + 32 : 64 * j + 64, own])
            st = mm(k[hs, own].T, qm)
            yield
            last = jnp.where(row < F - FS + 8, st[FS - 8 : FS], -1e30)
            mx = jnp.maximum(jnp.max(st[0 : FS - 8], 0, keepdims=True), jnp.max(last, 0, keepdims=True))
            e = jnp.exp2(st[0 : FS - 8] - mx)
            last = jnp.exp2(last - mx)
            inv = 1.0 / (jnp.sum(e, 0, keepdims=True) + jnp.sum(last, 0, keepdims=True))
            e = jnp.concatenate([e, last, jnp.zeros((FP - FS, 2 * FP), F32)], 0).astype(BF)
            keep("p", (u, j), (e, inv))
            yield
            t = mm(v[hs, own], e)
            ot.append(t[0:32, 0:128] * inv[:, 0:128])
            ot.append(t[32:64, 128:256] * inv[:, 128:256])
            yield
        ot = jnp.concatenate(ot, 0).astype(BF)
        keep("o", u, ot)
        outs.append(ot)
    a = mm(woT_ref[...], tall(jnp.concatenate(outs, 1)))
    yield
    for u in range(2):
        own = slice(u * FP, (u + 1) * FP)
        out.append(norm_t(x[0:D, own].astype(F32) + a[:, own]))
        yield


def slots_kernel(SL, count_ref, mask_ref, order_ref, x_ref, wqkvT_ref, woT_ref, vec_ref, out_ref, xs):
    xs[...] = jnp.zeros_like(xs)
    row = lax.broadcasted_iota(jnp.int32, (FS, 1), 0)
    lane = lax.broadcasted_iota(jnp.int32, (1, 2 * D), 1)

    def flag(r):
        order = order_ref[0, r]
        usable = (order < count_ref[0]) & ((mask_ref[0, r] == 1) | (order == 0))
        return jnp.where(usable, 1.0, 0.0)

    def pair(c):
        for u in range(2):
            xs[c, 0:D, u * FP : u * FP + F] = x_ref[2 * c + u]
        out = []
        yield from feature_pair(xs[c], wqkvT_ref, woT_ref, lambda *a: None, out)
        both = jnp.concatenate([(n * vec_ref[0] + vec_ref[1]).astype(BF) for n, _ in out], 0)
        flags = jnp.where(lane < D, flag(2 * c), flag(2 * c + 1))
        both = jnp.where(row < F, both.T[0:FS].astype(F32), flags).astype(BF)
        for i in range(out_ref.shape[0]):
            out_ref[i, c] = both
        yield

    weave([(pair(c), 0, 1) for c in range(SL // 2)])


def slot_rows(shards, count, mask, order, cells, wqkvT, woT, vec):
    SL = mask.shape[1]
    smem = pl.BlockSpec(memory_space=pltpu.SMEM)
    sent = shape((shards, SL // 2, FS, 2 * D))
    return pl.pallas_call(
        functools.partial(slots_kernel, SL),
        grid=(1,),
        in_specs=[smem, smem, smem, pl.BlockSpec((SL, D, F), lambda i: (0, 0, 0))]
        + [whole(a) for a in (wqkvT, woT, vec)],
        out_specs=whole(sent),
        out_shape=sent,
        scratch_shapes=[pltpu.VMEM((SL // 2, DP, 2 * FP), BF)],
        compiler_params=params(),
        cost_estimate=cost(5),
        name="slot_rows",
    )(count, mask, order, cells, wqkvT, woT, vec)


def turn_block(perm_ref, block, R):
    return mm(perm_ref[...], block.reshape(256, block.shape[-1])).astype(BF).reshape(16, R, block.shape[-1])


def forward_kernel(
    R, OFF, x_ref, c_ref, wqkvT_ref, woT_ref, vec_ref, perm_ref, ht_ref, ct_ref, n_ref, qkv_ref, p_ref, l_ref, of_ref, xs, hs, cp, cs
):
    @pl.when(pl.program_id(0) == 0)
    def _():
        xs[...] = jnp.zeros_like(xs)
        cp[...] = jnp.zeros_like(cp)

    def pair(c):
        for u in range(2):
            xs[c, 0:D, u * FP : u * FP + F] = x_ref[2 * c + u]

        def keep(what, at, val):
            if what == "qkv":
                for i in range(3):
                    qkv_ref[2 * c + at, i * D : (i + 1) * D, :] = val[i]
            elif what == "p":
                u, j = at
                p_ref[2 * c + u, :, 256 * j : 256 * j + 256] = val[0]
                l_ref[2 * c + u, j : j + 1, :] = val[1]
            else:
                of_ref[2 * c + at] = val

        out = []
        yield from feature_pair(xs[c], wqkvT_ref, woT_ref, keep, out)
        for u in range(2):
            r = 2 * c + u
            n, rc = out[u]
            n_ref[r, 0:D, :] = n.astype(BF)
            n_ref[r, D : D + 16, :] = jnp.broadcast_to(rc, (16, FP)).astype(BF)
            h = tall((n * vec_ref[0] + vec_ref[1]).astype(BF))
            hs[r] = h.T
            yield

    def cotangents():
        for r in range(R):
            cp[r % 4, 0:D, 0:F] = c_ref[r]
            cs[r] = cp[r % 4].T
            yield
        for j in range(FP // 16):
            ct_ref[16 * j : 16 * j + 16] = turn_block(perm_ref, cs[:, 16 * j : 16 * j + 16, :], R)
            yield

    weave([(pair(c), c * OFF, 1) for c in range(R // 2)] + [(cotangents(), 4, 1)])
    for j in range(FP // 16):
        ht_ref[16 * j : 16 * j + 16] = turn_block(perm_ref, hs[:, 16 * j : 16 * j + 16, :], R)


def feature_forward(cells, cot, ws, R=16, OFF=6):
    rows = cells.shape[0]
    nat = lambda a, b: pl.BlockSpec((R, a, b), lambda i: (i, 0, 0))
    turned = pl.BlockSpec((FP, R, DP), lambda i: (0, i, 0))
    sizes = [(D + 16, FP), (3 * D, FP), (FP, H * FP), (8, 2 * FP), (D, FP)]
    kinds = [BF, BF, BF, F32, BF]
    return pl.pallas_call(
        functools.partial(forward_kernel, R, OFF),
        grid=(rows // R,),
        in_specs=[nat(D, F), nat(D, F)] + [whole(a) for a in ws],
        out_specs=[turned, turned] + [nat(*a) for a in sizes],
        out_shape=[shape((FP, rows, DP))] * 2 + [shape((rows,) + a, t) for a, t in zip(sizes, kinds)],
        scratch_shapes=[
            pltpu.VMEM((R // 2, DP, 2 * FP), BF),
            pltpu.VMEM((R, FP, DP), BF),
            pltpu.VMEM((4, DP, FP), BF),
            pltpu.VMEM((R, FP, DP), BF),
        ],
        compiler_params=params(),
        cost_estimate=cost(9 * rows // R),
        name="feature_forward",
    )(cells, cot, *ws)


def pack_pair(ref, at, a, b):
    ref[at : at + D] = a[0:D, 0:128].astype(BF)
    ref[at + D : at + 2 * D] = b[0:D, 0:128].astype(BF)
    ref[at + 2 * D : at + 3 * D] = jnp.concatenate([a[0:D, 128:D], b[0:D, 128:D]], 1).astype(BF)


def pack_norms(ref, at, sums):
    rows = []
    for s in sums:
        if s.shape[0] == D:
            s = jnp.concatenate([s, jnp.zeros((DP - D, 128), F32)], 0).T
        v = jnp.sum(s, 0, keepdims=True)
        rows += [v[:, 0:128], v[:, 128:256]]
    rows.append(jnp.zeros((ref.shape[0] - at - len(rows), 128), F32))
    ref[at:] = jnp.concatenate(rows, 0).astype(BF)


def item_kernel(
    RW, keys, OFF, WP, CC, WC, ht_ref, ct_ref, slot_ref, perm_ref, wq_ref, wqT_ref, woI_ref, wo_ref, w1T_ref, w1_ref, w2T_ref, w2_ref,
    wkv_ref, wkvT_ref, vec_ref, y_ref, g1_ref, back_ref, pack_ref, dwq, dwo, dw1, dw2, dnp, dwkv, bias_ref, hk_ref, bk_ref,
    dk_ref, dv_ref, hbTs, ois, hb2Ts, actss, dbTs, duss, dabTs, dqss, slp,
):
    step = pl.program_id(0)
    blocks = [(s, b, min(16, FS - b)) for s in range(0, keys, 16) for b in range(0, FS, 16)]

    @pl.when(step == 0)
    def _():
        for ref in (dwq, dwo, dw1, dw2, dnp, dwkv):
            ref[...] = jnp.zeros_like(ref)
        for ref in (hbTs, ois, hb2Ts, actss, dbTs, duss, dabTs, dqss):
            ref[1] = jnp.zeros_like(ref[1])
        hk_ref[:, :, D:DP] = jnp.zeros((FS, keys, DP - D), BF)
        for s, b, n in blocks:
            own = slot_ref[s // 2 : s // 2 + 8, b : b + n, :]
            own = jnp.concatenate([own[:, :, 0:D], own[:, :, D : 2 * D]], 0)
            if n < 16:
                own = jnp.concatenate([own, jnp.zeros((16, 16 - n, D), BF)], 1)
            hk_ref[b : b + n, s : s + 16, 0:D] = turn_block(perm_ref, own, 16)[0:n]
        for s in range(0, keys, 16):
            flag = slot_ref[s // 2 : s // 2 + 8, F, :].astype(F32)
            for i, at in enumerate((0, DP)):
                bias_ref[s + 8 * i : s + 8 * i + 8] = jnp.where(flag[:, at : at + 128] > 0.5, 0.0, -1e30)

    cur = step % 2
    masks = half_masks()
    LW = 2 * RW
    left = lax.broadcasted_iota(jnp.int32, (1, LW), 1) < RW
    HK = H * keys
    hbT, oi, hb2T, acts, dbT, dus, dabT, dqs = [r.at[cur] for r in (hbTs, ois, hb2Ts, actss, dbTs, duss, dabTs, dqss)]
    hk = hk_ref[pl.ds(pl.multiple_of(step * FB, FB), FB)].reshape(FB * keys, DP)
    kvs = [mm(hk, wkv_ref[...]).astype(BF)]

    def attend(j, out):
        h = ht_ref[2 * j:2 * j + 2].reshape(LW, DP)
        q = (mm(h, wq_ref[...]) * SCALE2).astype(BF)
        yield
        ks = [spread_halves(kvs[0][(2 * j + c) * keys : (2 * j + c + 1) * keys, 0:DP], masks) for c in range(2)]
        hbT[:, j * LW:(j + 1) * LW] = h.T[0:D]
        yield
        st = jnp.where(left, mm_nt(ks[0], q), mm_nt(ks[1], q))
        yield
        vs = [spread_halves(kvs[0][(2 * j + c) * keys : (2 * j + c + 1) * keys, DP:], masks) for c in range(2)]
        pbs = []
        for hh in range(H):
            s = st[hh * keys:(hh + 1) * keys] + bias_ref[...]
            e = jnp.exp2(s - jnp.max(s, 0, keepdims=True))
            pbs.append((e * (1.0 / jnp.sum(e, 0, keepdims=True))).astype(BF))
            if hh % 2: yield
        pb = jnp.concatenate(pbs, 0)
        pt = pb.T
        yield
        o = jnp.concatenate([mm(pt[:RW], vs[0]), mm(pt[RW:], vs[1])], 0).astype(BF)
        oi[j * LW:(j + 1) * LW] = o
        out.extend([q, pb, ks, vs, o])
        yield
    def dense(i, os, out):
        c0 = i * 2 * LW
        g1v, b1v, g2v, b2v = [vec_ref[i] for i in range(2, 6)]
        h = ht_ref[4 * i:4 * i + 4].reshape(2 * LW, DP)
        o = jnp.concatenate(os, 0)
        aT = mm_nt(woI_ref[...], jnp.concatenate([o, h], 1))
        yield
        n2, rc2, h2, hb2 = [], [], [], []
        for t in range(2):
            n, rc = norm_t(aT[:, t * LW:(t + 1) * LW])
            hh = n * g1v + b1v
            n2.append(n.astype(BF)); rc2.append(rc); hb2.append(hh.astype(BF))
            yield
        hb2 = jnp.concatenate(hb2, 1)
        hb2T[:, c0:c0 + 2 * LW] = hb2
        hb2 = tall(hb2)
        C = CC
        u = mm(w1T_ref[0:C], hb2)
        for c in range(FF // C):
            un = mm(w1T_ref[C * c + C:C * c + 2 * C], hb2) if c + 1 < FF // C else None
            act, slope = gelu_parts(u.astype(BF))
            acts[C * c:C * c + C, c0:c0 + 2 * LW] = act
            slp[C * c:C * c + C, c0:c0 + 2 * LW] = slope
            u = un
            yield
        gT = ct_ref[4 * i:4 * i + 4].reshape(2 * LW, DP).T[0:D].astype(F32)
        z = mm(w2T_ref[...], acts[:, c0:c0 + 2 * LW])
        yield
        dbs, d3s = [], []
        ys = []
        for t in range(2):
            sl = slice(t * LW, (t + 1) * LW)
            n3, rc3 = norm_t(hb2[0:D, sl].astype(F32) + z[:, sl])
            ys.append((n3 * g2v + b2v).astype(BF))
            yield
            g = gT[:, sl]
            dnp[2] += g * n3
            dnp[3] += g
            d3 = norm_back_t(g, n3, rc3, g2v)
            dbs.append(d3.astype(BF))
            yield
        db = jnp.concatenate(dbs, 1)
        dbT[:, c0:c0 + 2 * LW] = db
        db = tall(db)
        w = mm(w2_ref[0:C], db)
        for c in range(FF // C):
            wn = mm(w2_ref[C * c + C:C * c + 2 * C], db) if c + 1 < FF // C else None
            dus[C * c:C * c + C, c0:c0 + 2 * LW] = w.astype(BF) * slp[C * c:C * c + C, c0:c0 + 2 * LW]
            w = wn
            yield
        dh = mm(w1_ref[...], dus[:, c0:c0 + 2 * LW])
        yT = tall(jnp.concatenate(ys, 1))
        y_ref[4 * i:4 * i + 4] = yT.T.reshape(4, RW, DP)
        yield
        dabs = []
        for t in range(2):
            dh2 = dbs[t].astype(F32) + dh[:, t * LW:(t + 1) * LW]
            n2f = n2[t].astype(F32)
            dnp[0] += dh2 * n2f
            dnp[1] += dh2
            dabs.append(norm_back_t(dh2, n2f, rc2[t], g1v).astype(BF))
            yield
        dab = jnp.concatenate(dabs, 1)
        dabT[:, c0:c0 + 2 * LW] = dab
        doT = mm(wo_ref[...], tall(dab)).astype(BF)
        out.extend([dab, doT])
        yield
    def back(j, at, doT, out):
        q, pb, ks, vs, _ = at
        do = tall(doT)
        don = do.T
        dp = jnp.where(left, mm(vs[0], do), mm(vs[1], do))
        yield
        slot_sums(dv_ref, j, pb, don, None)
        yield
        dss = []
        for hh in range(H):
            sl = slice(hh * keys, (hh + 1) * keys)
            p, d = pb[sl].astype(F32), dp[sl]
            dss.append((p * (d - jnp.sum(p * d, 0, keepdims=True))).astype(BF))
            if hh % 2: yield
        ds = jnp.concatenate(dss, 0)
        dst = ds.T
        yield
        slot_sums(dk_ref, j, ds, q, 0.6931471805599453)
        yield
        dq = jnp.concatenate([mm(dst[:RW], ks[0]), mm(dst[RW:], ks[1])], 0) * SCALE
        dq = dq.astype(BF)
        dqs[j * LW:(j + 1) * LW] = dq
        out.append(dq)
        yield
    lane = lax.broadcasted_iota(jnp.int32, (1, 128), 1)
    zq = jnp.zeros((RW, 128), BF)
    def slot_sums(ref, j, w, rows, scale):
        out = [[], []]
        for t, heads in ((0, 4), (1, 2)):
            r = rows[:, 128 * t:128 * t + 128]
            both = jnp.concatenate([jnp.concatenate([r[:RW], zq], 0), jnp.concatenate([zq, r[RW:]], 0)], 1)
            full = mm(w[4 * t * keys:(4 * t + heads) * keys], both)
            for c in range(2):
                col = full[:, 128 * c:128 * c + 128]
                v = col[0:keys]
                for hh in range(1, heads):
                    v = jnp.where(lane >= E * hh, col[hh * keys:(hh + 1) * keys], v)
                out[c].append(v)
        for c in range(2):
            v = jnp.concatenate(out[c], 1)
            ref[2 * j + c] = (v if scale is None else v * scale).astype(BF)
    def finish(i, dqv, dab):
        dq = jnp.concatenate(dqv, 0)
        g1 = mm(dq, wqT_ref[...]) + tall(dab).T.astype(F32)
        g1_ref[4 * i:4 * i + 4] = g1.astype(BF).reshape(4, RW, DP)
        yield
    def chunk(i):
        at = [[], []]
        ga, gb = attend(2 * i, at[0]), attend(2 * i + 1, at[1])
        for _ in zip(ga, gb): yield
        for _ in ga: yield
        for _ in gb: yield
        out = []
        yield from dense(i, [at[0][4], at[1][4]], out)
        dab, doT = out
        dq = []
        for t in range(2):
            yield from back(2 * i + t, at[t], doT[:, t * LW:(t + 1) * LW], dq)
        yield from finish(i, dq, dab)
    def wgrad(b):
        dwq[...] += mm(hbTs[b], dqss[b])
        yield
        dwo[...] += mm(dabTs[b], ois[b])
        yield
        for c in range(0, FF, WC):
            dw1[c:c + WC] += mm_nt(duss[b, c:c + WC], hb2Ts[b])
            yield
        for c in range(0, FF, WC):
            dw2[c:c + WC] += mm_nt(actss[b, c:c + WC], dbTs[b])
            yield
    NC = FB // 4
    weave([(chunk(i), i * OFF, 1) for i in range(NC)] + [(wgrad(1 - cur), WP, 1)])
    dkv = jnp.concatenate([r[...].reshape(FB * keys, DP) for r in (dk_ref, dv_ref)], 1)
    dwkv[...] += mm_tn(hk, dkv)
    bk_ref[pl.ds(pl.multiple_of(step * FB, FB), FB)] = mm(dkv, wkvT_ref[...]).astype(BF).reshape(FB, keys, DP)

    @pl.when(step == pl.num_programs(0) - 1)
    def _():
        for _ in wgrad(cur):
            pass
        for s, b, n in blocks:
            own = bk_ref[b : b + n, s : s + 16, :]
            if n < 16:
                own = jnp.concatenate([own, jnp.zeros((16 - n, 16, DP), BF)], 0)
            own = turn_block(perm_ref, own, 16)[:, 0:n, 0:D]
            back_ref[s // 2 : s // 2 + 8, b : b + n, :] = jnp.concatenate([own[0:8], own[8:16]], 2)
        at = 0
        for ref in (dw1, dw2):
            t = ref[...].T
            for j in range(FF // 128):
                pack_ref[at : at + D] = t[:, 128 * j : 128 * j + 128].astype(BF)
                at += D
        pack_pair(pack_ref, at, dwq, tall(dwo[...]).T)
        pack_pair(pack_ref, at + PAIR, dwkv[:, 0:DP], dwkv[:, DP:])
        pack_norms(pack_ref, at + 2 * PAIR, [dnp[i] for i in range(4)])


def item_and_dense(ht, ct, slots, perm, ws, vec, packed, OFF=0, WP=20, CC=384, WC=384):
    RW = ht.shape[1]
    keys = 2 * slots.shape[0]
    M = FB * RW
    cells = pl.BlockSpec((FB, RW, DP), lambda i: (i, 0, 0))
    accs = [(D, DP), (D, DP), (FF, D), (FF, D), (4, D, 128), (DP, 2 * DP), (keys, 128)]
    kept = [(D, M), (M, DP), (D, M), (FF, M), (D, M), (FF, M), (D, M), (M, DP)]
    flat = [slots, perm, *ws, vec]
    outs = [shape((FS, RW, DP))] * 2 + [shape(slots.shape), shape((packed, 128))]
    return pl.pallas_call(
        functools.partial(item_kernel, RW, keys, OFF, WP, CC, WC),
        grid=(FS // FB,),
        in_specs=[cells, cells] + [whole(a) for a in flat],
        out_specs=[cells, cells] + [whole(a) for a in outs[2:]],
        out_shape=outs,
        scratch_shapes=[pltpu.VMEM(a, F32) for a in accs]
        + [pltpu.VMEM((FS, keys, DP), BF)] * 2
        + [pltpu.VMEM((FB, keys, DP), BF)] * 2
        + [pltpu.VMEM((2,) + a, BF) for a in kept]
        + [pltpu.VMEM((FF, M), BF)],
        compiler_params=params(),
        cost_estimate=cost(66),
        name="item_and_dense",
    )(ht, ct, *flat)


def backward_kernel(R, OFF, SL, x_ref, n_ref, qkv_ref, p_ref, l_ref, of_ref, g1t_ref, yt_ref, *rest):
    if SL:
        (dsl_ref, wqkvI_ref, wo_ref, vec_ref, perm_ref, iqkv, iwo, inp, _, _,
         cg_ref, y_ref, pack_ref, gs, ys, xs, os, dqs, das, dqkv, dwo, dnp) = rest
    else:
        (wqkvI_ref, wo_ref, vec_ref, perm_ref, cg_ref, y_ref, dqkv, dwo, dnp, gs, ys, xs, os, dqs, das) = rest

    @pl.when(pl.program_id(0) == 0)
    def _():
        xs[...] = jnp.zeros_like(xs)
        for i, ref in enumerate((dqkv, dwo, dnp)):
            ref[...] = (iqkv, iwo, inp)[i][...] if SL else jnp.zeros_like(ref)

    col = lax.broadcasted_iota(jnp.int32, (16, 1, 1), 0)

    def turn(ref, out, j):
        block = ref[16 * j : min(16 * j + 16, FS)]
        if block.shape[0] < 16:
            block = jnp.concatenate([block, jnp.zeros((16 - block.shape[0],) + block.shape[1:], BF)], 0)
        if 16 * j + 16 > F:
            block = jnp.where(col < F - 16 * j, block, 0).astype(BF)
        out[:, 16 * j : 16 * j + 16, :] = turn_block(perm_ref, block, 16)

    for j in range(FP // 16):
        turn(g1t_ref, gs, j)
    back = []
    if SL:
        both = dsl_ref[0].astype(F32)
        for i in range(1, dsl_ref.shape[0]):
            both = both + dsl_ref[i].astype(F32)
        z0 = jnp.zeros((FP - FS, 2 * D), F32)
        for c in range(SL // 2):
            t = jnp.concatenate([both[c], z0], 0).T
            back += [t[0:D], t[D : 2 * D]]

    def pair(c):
        at = slice(2 * c * FP, (2 * c + 2) * FP)
        dabs, das32 = [], []
        for u in range(2):
            r = 2 * c + u
            xs[:, r * FP : r * FP + F] = x_ref[r]
            os[:, r * FP : (r + 1) * FP] = of_ref[r]
            g = gs[r].T[0:D].astype(F32)
            if r < SL:
                g = g + back[r]
            n = n_ref[r, 0:D, :].astype(F32)
            rc = n_ref[r, D : D + 16, :].astype(F32)[0:1]
            dnp[0] += g * n
            dnp[1] += g
            dabs.append(norm_back_t(g, n, rc, vec_ref[0]).astype(BF))
            yield
        dab = jnp.concatenate(dabs, 1)
        das[:, at] = dab
        do = mm(wo_ref[...], tall(dab))
        yield
        for u in range(2):
            r = 2 * c + u
            own = slice(u * FP, (u + 1) * FP)
            lanes_r = slice(r * FP, (r + 1) * FP)
            for j in range(H // 2):
                inv = l_ref[r, j : j + 1, :]
                parts, offs = [], []
                for t in range(2):
                    hs = slice(64 * j + 32 * t, 64 * j + 32 * t + 32)
                    d = do[hs, own] * inv[:, t * FP : (t + 1) * FP]
                    offs.append(jnp.sum(d * of_ref[r, hs, :].astype(F32), 0, keepdims=True))
                    parts.append(d.astype(BF))
                dom = two_heads(*parts)
                off = jnp.concatenate(offs, 1).astype(BF)
                dp = mm(qkv_ref[r, 2 * D + 64 * j : 2 * D + 64 * j + 64, :].T, dom)
                yield
                e = p_ref[r, :, 256 * j : 256 * j + 256]
                ds = e * (dp.astype(BF) - off)
                dv = mm_nt(dom, e)
                yield
                qm = two_heads(
                    qkv_ref[r, 64 * j : 64 * j + 32, :], qkv_ref[r, 64 * j + 32 : 64 * j + 64, :]
                )
                dk = mm_nt(qm, ds) * 0.6931471805599453
                dq = mm(qkv_ref[r, D + 64 * j : D + 64 * j + 64, :], ds)
                dq = jnp.concatenate([dq[0:32, 0:128], dq[32:64, 128:256]], 0) * SCALE
                yield
                for i, d in enumerate((dq, dk, dv)):
                    dqs[i * D + 64 * j : i * D + 64 * j + 64, lanes_r] = d.astype(BF)
        yield
        cg = mm(wqkvI_ref[...], jnp.concatenate([dqs[:, at], dab], 0))
        for u in range(2):
            cg_ref[2 * c + u] = cg[:, u * FP : u * FP + F]
        yield

    def outputs():
        for j in range(FP // 16):
            turn(yt_ref, ys, j)
            yield
        for r in range(R):
            y_ref[r] = ys[r].T[0:D, 0:F]
            yield

    def sums(part):
        at = slice(part * R * FP // 2, (part + 1) * R * FP // 2)
        for i in range(3):
            dqkv[i * D : (i + 1) * D] += mm_nt(dqs[i * D : (i + 1) * D, at], xs[:, at])
            yield
        dwo[...] += mm_nt(os[:, at], das[:, at])
        yield

    Q = R // 4
    for half in range(2):
        streams = [(pair(c), (c - half * Q) * OFF, 1) for c in range(half * Q, (half + 1) * Q)]
        streams.append((sums(0) if half else outputs(), 3, 1))
        weave(streams)
    for _ in sums(1):
        pass

    if SL:

        @pl.when(pl.program_id(0) == pl.num_programs(0) - 1)
        def _():
            zc = jnp.zeros((D, DP - D), F32)
            three = [jnp.concatenate([dqkv[i * D : (i + 1) * D], zc], 1).T for i in range(3)]
            pack_pair(pack_ref, 0, three[0], three[1])
            pack_pair(pack_ref, PAIR, three[2], dwo)
            pack_norms(pack_ref, 2 * PAIR, [dnp[0], dnp[1]])


def feature_backward(x, saved, g1t, yt, wqkvI, wo, vec, perm, row0, rows, R=16, OFF=6, slots=None, prev=None, packed=0):
    b0 = row0 // R
    nat = lambda a: pl.BlockSpec((R,) + a.shape[1:], lambda i: (i + b0, 0, 0))
    turned = pl.BlockSpec((FS, R, DP), lambda i: (0, i + b0, 0))
    real = pl.BlockSpec((R, D, F), lambda i: (i + b0, 0, 0))
    accs = [shape((3 * D, D), F32), shape((D, D), F32), shape((2, D, FP), F32)]
    ins = [x, *saved, g1t, yt]
    specs = [real] + [nat(a) for a in saved] + [turned] * 2
    out_shape = [shape((x.shape[0], D, F), F32), shape((x.shape[0], D, F))]
    out_specs = [real, real]
    M = R * FP
    scratch = [pltpu.VMEM(a, BF) for a in ((R, FP, DP), (R, FP, DP), (D, M), (D, M), (3 * D, M), (D, M))]
    SL = 0
    alias = {}
    shared = [wqkvI, wo, vec, perm]
    if slots is not None:
        SL = 2 * slots.shape[1]
        shared = [slots] + shared
    ins += shared
    specs += [whole(a) for a in shared]
    if prev is not None:
        cg, y, *acc = prev
        ins += list(acc) + [cg, y]
        specs += [whole(a) for a in acc] + [pl.BlockSpec(memory_space=pl.ANY)] * 2
        alias = {len(ins) - 2: 0, len(ins) - 1: 1}
        out_shape.append(shape((packed, 128)))
        out_specs.append(pl.BlockSpec((packed, 128), lambda i: (0, 0)))
        scratch += [pltpu.VMEM(a.shape, F32) for a in accs]
    else:
        out_shape += accs
        out_specs += [whole(a) for a in accs]
    return pl.pallas_call(
        functools.partial(backward_kernel, R, OFF, SL),
        grid=(rows // R,),
        in_specs=specs,
        out_specs=out_specs,
        out_shape=out_shape,
        input_output_aliases=alias,
        scratch_shapes=scratch,
        compiler_params=params(),
        cost_estimate=cost(60 * rows // R),
        name="feature_backward",
    )(*ins)


def sum_kernel(n, *refs):
    *ready_refs, parts_ref, out_ref = refs
    total = parts_ref[0].astype(F32)
    for i in range(1, n):
        total = total + parts_ref[i].astype(F32)
    total = total.astype(BF)
    if not ready_refs:
        out_ref[...] = total
        return
    rows = ready_refs[0].shape[0]
    for i in range(out_ref.shape[0]):
        out_ref[i, 0:rows] = ready_refs[0][...]
        out_ref[i, rows:] = total


def sum_parts(packed, n, ready=None):
    rows = packed.shape[0] // n
    parts = lax.all_to_all(packed.reshape(n, rows, 128), ("table", "rows"), 0, 0)
    ins = [parts] if ready is None else [ready, parts]
    out = (rows, 128) if ready is None else (lax.axis_size("rows"), ready.shape[0] + rows, 128)
    return pl.pallas_call(
        functools.partial(sum_kernel, n),
        out_shape=shape(out),
        compiler_params=params(),
        cost_estimate=cost(2),
        name="sum_parts",
    )(*ins)


def gather_all(copies):
    tables = lax.axis_size("table")
    ny = tables // 2
    own = lax.all_to_all(copies, "rows", 0, 0)
    pieces = [own]
    for s in range(1, ny):
        pieces.append(lax.ppermute(own, "table", [(t, (t // 2 + s) % ny * 2 + t % 2) for t in range(tables)]))
    other = [lax.ppermute(a, "table", [(t, t ^ 1) for t in range(tables)]) for a in pieces]
    return [a for pair in zip(pieces, other) for a in pair]


def to_row(c):
    return jnp.broadcast_to(c, (c.shape[0], 128)).T[0:1]


def to_col(r):
    return jnp.broadcast_to(r, (128, r.shape[1])).T[:, 0:1]


def clipped(update, weight, count):
    def total(v):
        return jnp.sum(jnp.sum(v, 0, keepdims=True), 1, keepdims=True)

    rms = jnp.sqrt(total(update * update) * (1.0 / count))
    weight_rms = jnp.sqrt(total(weight * weight) * (1.0 / count))
    return update * (RATE * jnp.maximum(0.001, weight_rms) / jnp.maximum(1.0, rms / CLIP))


def optimizer_kernel(
    tables, mid_rows, *refs):
    table_ref, *refs = refs
    piece_refs, refs = refs[:tables], refs[tables:]
    mid_ref, tail_ref = refs[-2:]
    table = table_ref[0]
    ny = tables // 2
    for i, ref in enumerate(piece_refs):
        place = lax.rem(table // 2 - i // 2 + ny, ny) * 2 + lax.rem(table + i % 2, 2)
        for out, at, end in ((mid_ref, 0, mid_rows), (tail_ref, mid_rows, ref.shape[1])):
            rows = ref.shape[0] * (end - at)
            start = pl.multiple_of(place * rows, 8)
            out[pl.ds(start, rows)] = ref[:, at:end, :].astype(F32).reshape(rows, 128)
    optimizer_steps(*refs)


def optimizer_steps(
    proj_ref, outw_ref, in_ref, hid_ref, norm_ref, sr_ref, sc_ref, mm_ref, mh_ref, ns_ref,
    proj_g, out_g, in_g, hid_g, norm_g, proj_n, out_n, in_n, hid_n, norm_n, sr_n, sc_n, mm_n, mh_n, ns_n, mid_ref, tail_ref,
):
    decay = 1.0 - STEP ** (-0.8)

    def stats(grad, col_old, row_old):
        square = grad * grad + 1e-30
        a, b = grad.shape
        over_sub = decay * row_old + (1.0 - decay) * (jnp.sum(square, 0, keepdims=True) * (1.0 / a))
        over_lane = decay * col_old + (1.0 - decay) * (jnp.sum(square, 1, keepdims=True) * (1.0 / b))
        return over_lane, over_sub

    def scaled(grad, col, row, mean):
        return grad * lax.rsqrt(col * (1.0 / mean)) * lax.rsqrt(row)

    def square_pair(ref, at):
        both = ref[at + 2 * D : at + 3 * D].astype(F32)
        a = jnp.concatenate([ref[at : at + D].astype(F32), both[:, 0:64]], 1)
        b = jnp.concatenate([ref[at + D : at + 2 * D].astype(F32), both[:, 64:128]], 1)
        return a, b

    wq, wk = square_pair(tail_ref, 0)
    wv, wo = square_pair(tail_ref, PAIR)
    wq2, wo2 = square_pair(mid_ref, 12 * D)
    wk2, wv2 = square_pair(mid_ref, 12 * D + PAIR)
    for i, grad in enumerate((wq, wk, wv, wq2, wk2, wv2, wo, wo2)):
        g_ref, n_ref, w_ref, j = (proj_g, proj_n, proj_ref, i) if i < 6 else (out_g, out_n, outw_ref, i - 6)
        g_ref[j] = grad
        col, row = stats(grad, to_col(sr_ref[i : i + 1, :]), sc_ref[i : i + 1, :])
        sr_n[i : i + 1, :] = to_row(col)
        sc_n[i : i + 1, :] = row
        mean = jnp.sum(col, 0, keepdims=True) * (1.0 / D)
        w = w_ref[j]
        n_ref[j] = w - clipped(scaled(grad, col, row, mean), w, D * D)

    def wide(at):
        return jnp.concatenate([mid_ref[at + D * j : at + D * j + D].astype(F32) for j in range(6)], 1)

    grad = wide(0)
    in_g[...] = grad
    col, row = stats(grad, to_col(mm_ref[0:1, :]), mh_ref[0:1, :])
    mm_n[0:1, :] = to_row(col)
    mh_n[0:1, :] = row
    mean = jnp.sum(col, 0, keepdims=True) * (1.0 / D)
    w = in_ref[...]
    in_n[...] = w - clipped(scaled(grad, col, row, mean), w, D * FF)
    grad = wide(6 * D)
    hid_g[...] = grad
    col, row = stats(grad, to_col(mm_ref[1:2, :]), mh_ref[1:2, :])
    mm_n[1:2, :] = to_row(col)
    mh_n[1:2, :] = row
    mean = jnp.sum(row, 1, keepdims=True) * (1.0 / FF)
    w = hid_ref[...]
    update = grad * lax.rsqrt(col) * lax.rsqrt(row * (1.0 / mean))
    hid_n[...] = w - clipped(update, w, D * FF)

    pieces = []
    for ref, at, count in ((tail_ref, 2 * PAIR, 2), (mid_ref, 12 * D + 2 * PAIR, 4)):
        v = ref[at : at + 16].astype(F32)
        for i in range(count):
            pieces.append(jnp.concatenate([v[2 * i : 2 * i + 1], v[2 * i + 1 : 2 * i + 2, 0:64]], 1))
    grad = jnp.concatenate(pieces, 0)
    norm_g[...] = grad
    second = decay * ns_ref[...] + (1.0 - decay) * (grad * grad + 1e-30)
    ns_n[...] = second
    update = grad * lax.rsqrt(second)
    rms = jnp.sqrt(jnp.sum(update * update, 1, keepdims=True) * (1.0 / D))
    w = norm_ref[...]
    w_rms = jnp.sqrt(jnp.sum(w * w, 1, keepdims=True) * (1.0 / D))
    norm_n[...] = w - update * (RATE * jnp.maximum(0.001, w_rms) / jnp.maximum(1.0, rms / CLIP))


def optimizer(pieces, mid_rows, *state):
    proj, outw, w_in, w_outT, norms, sr, sc, ms, hs, ns = state
    shards, rows, _ = pieces[0].shape
    table = lax.axis_index("table").astype(jnp.int32).reshape(1)
    order = [proj, outw, w_in, w_outT, norms, proj, outw, w_in, w_outT, norms, sr, sc, ms, hs, ns]
    outs = pl.pallas_call(
        functools.partial(optimizer_kernel, len(pieces), mid_rows),
        in_specs=[pl.BlockSpec(memory_space=pltpu.SMEM)] + [whole(a) for a in (*pieces, *state)],
        out_shape=[shape(a.shape, F32) for a in order],
        scratch_shapes=[
            pltpu.VMEM((len(pieces) * shards * mid_rows, 128), F32),
            pltpu.VMEM((len(pieces) * shards * (rows - mid_rows), 128), F32),
        ],
        compiler_params=params(),
        cost_estimate=cost(8), name="optimizer",
    )(table, *pieces, *state)
    outs = list(outs)
    for i in (3, 8):
        outs[i] = outs[i].T
    return outs


def on_device(n, cells, cotangent, train_count, key_mask, train_order, *state):
    state = list(state)
    state[3] = state[3].T
    proj, outw, w_in, w_outT, norms = state[:5]
    x = jnp.swapaxes(cells[0], 1, 2)
    cot = jnp.swapaxes(cotangent[0], 1, 2)
    rows_here = x.shape[0]
    unit = 8 * n
    tail_rows = -(-TAIL // unit) * unit
    mid_rows = -(-MID // unit) * unit
    perm = perm_matrix()
    (wqkvT, wqkvI, wo, woT, wkv2, wkv2T, wq2, wq2T, wo2I, wo2, w1T, w1, w2T, w2, vec) = prepare(
        proj, outw, w_in, w_outT, norms
    )
    R = 16
    shards = lax.axis_size("rows")
    own = slot_rows(shards, train_count, key_mask, train_order, x, wqkvT, woT, vec)
    slots = lax.all_to_all(own, "rows", 0, 0).reshape((-1,) + own.shape[2:])
    ht, ct, *saved = feature_forward(x, cot, (wqkvT, woT, vec, perm))
    ws = (wq2, wq2T, wo2I, wo2, w1T, w1, w2T, w2, wkv2, wkv2T)
    yt, g1t, back, mid = item_and_dense(ht, ct, slots, perm, ws, vec, mid_rows)
    back = lax.all_to_all(back.reshape(own.shape), "rows", 0, 0)
    args = (x, saved, g1t, yt, wqkvI, wo, vec, perm)
    prev = list(feature_backward(*args, row0=R, rows=rows_here - R, R=R))
    mid, back, prev[4] = lax.optimization_barrier((mid, back, prev[4]))
    mid = sum_parts(mid, n)
    cg, y, tail = feature_backward(*args, row0=0, rows=R, R=R, slots=back, prev=prev, packed=tail_rows)
    tail, mid = lax.optimization_barrier((tail, mid))
    pieces = gather_all(sum_parts(tail, n, mid))
    return (jnp.swapaxes(y, 1, 2)[None], jnp.swapaxes(cg, 1, 2)[None], *optimizer(pieces, mid.shape[0], *state))


def solution(mesh):
    n = int(mesh.shape["table"] * mesh.shape["rows"])
    cells = P("table", "rows", None, None)
    return jax.shard_map(
        functools.partial(on_device, n),
        mesh=mesh,
        in_specs=(cells, cells, P("table"), P("table", "rows"), P("table", "rows")) + (P(),) * 10,
        out_specs=(cells, cells) + (P(),) * 15,
        check_vma=False,
    )
```

profile of v0, /device:TPU:0, one launch (start us, length us, event | category | flops | bytes accessed | tf_op | source)
XLA Modules:
  0.0 240.7 jit_solution(15402507044799408419)
XLA Ops:
  1.3 3.8 %weights.1 = (bf16[576,256]{1,0:T(8,128)(2,1)}, bf16[192,768]{1,0:T(8,128)(2,1)}, bf16[192,256]{1,0:T(8,128)(2,1)}, bf16[192,256]{1,0:T(8,128)(2,1)}, bf16[256,5...) custom-call(f32[6,192,192]{2,1,0:T(8,128)} %refs_5_.1, ...), custom_call_target="tpu_custom_call" | custom-call | flops 4400000000 | bytes 4000000 | tf_op jit(solution)/shard_map/weights/pallas_call | solution.py:174
  5.1 4.6 %slot_rows.1 = bf16[8,2,120,384]{3,2,1,0:T(8,128)(2,1)} custom-call(s32[1]{0:T(128)S(6)} %copy.37.count_ref, s32[1,4]{1,0:T(1,128)} %mask_ref.1, s32[1,4]{1,0:T(1,128)} %order_ref.1, bf16[64,192,119]{2,1,0:T(8,128)(2,1)} %bitcast.24, bf16[576,256]{1,0:T(8,128)(2,1)} %get-tuple-element.71.wqkvT_ref, bf16[192,256]{1,0:T(8,128)(2,1)} %get-tuple-element.72.woT_ref, ...), custom_call_target="tpu_custom_call" | custom-call | flops 5500000256 | bytes 5000000 | tf_op jit(solution)/shard_map/slot_rows/pallas_call | solution.py:258
  9.8 7.3 %all-to-all-start = ((bf16[8,2,120,384]{3,2,1,0:T(8,128)(2,1)}), bf16[8,2,120,384]{3,2,1,0:T(8,128)(2,1)S(1)}, u32[]{:S(2)}, u32[]{:S(2)}) async-start(bf16[8,2,120,384]{3,2,1,0:T(8,128)(2,1)} %slot_rows.1), calls=%async_computation | async-start | bytes 2949120 | tf_op jit(solution)/shard_map/all_to_all | solution.py:968
  17.0 33.0 %feature_forward.1 = (bf16[128,64,256]{2,1,0:T(8,128)(2,1)}, bf16[128,64,256]{2,1,0:T(8,128)(2,1)}, bf16[64,208,128]{2,1,0:T(8,128)(2,1)}, bf16[64,576,128]{2,1,...) custom-call(bf16[64,192,119]{2,1,0:T(8,128)(2,1)} %bitcast.25, ...), custom_call_target="tpu_custom_call" | custom-call | flops 39600001024 | bytes 36000000 | tf_op jit(solution)/shard_map/feature_forward/pallas_call | solution.py:330
  50.1 1.9 all-to-all-done
  51.9 0.0 copy-start
  51.9 1.1 copy-done
  53.1 69.7 %item_and_dense.1 = (bf16[120,64,256]{2,1,0:T(8,128)(2,1)}, bf16[120,64,256]{2,1,0:T(8,128)(2,1)}, bf16[16,120,384]{2,1,0:T(8,128)(2,1)}, bf16[3584,128]{1,0:T(8,128)(2,1)}) custom-call(bf16[128,64,256]{2,1,0:T(8,128)(2,1)} %get-tuple-element.79.ht_ref, bf16[128,64,256]{2,1,0:T(8,128)(2,1)} %get-tuple-element.80.ct_ref, bf16[16,120,384]{2,1,0:T(8,128)(2,1)} %bitcast.20, ...), custom_call_target="tpu_custom_call" | custom-call | flops 72600002560 | bytes 66000000 | tf_op jit(solution)/shard_map/item_and_dense/pallas_call | solution.py:596
  122.8 4.5 %all-to-all-start.1 = ((bf16[8,2,120,384]{3,2,1,0:T(8,128)(2,1)}), bf16[8,2,120,384]{3,2,1,0:T(8,128)(2,1)}, u32[]{:S(2)}, u32[]{:S(2)}) async-start(bf16[8,2,120,384]{3,2,1,0:T(8,128)(2,1)} %bitcast.21), calls=%async_computation.1 | async-start | bytes 2949120 | tf_op jit(solution)/shard_map/all_to_all | solution.py:972
  127.3 30.0 %feature_backward.2 = (f32[64,192,119]{2,1,0:T(8,128)}, bf16[64,192,119]{2,1,0:T(8,128)(2,1)}, f32[576,192]{1,0:T(8,128)}, f32[192,192]{1,0:T(8,128)}, f32[2,192,128]{2,1,0:T(8,128)}) custom-call(bf16[64,192,119]{2,1,0:T(8,128)(2,1)} %bitcast.26, bf16[64,208,128]{2,1,0:T(8,128)(2,1)} %get-tuple-element.74.n_ref, ...), custom_call_target="tpu_custom_call" | custom-call | flops 198000001024 | bytes 180000000 | tf_op jit(solution)/shard_map/feature_backward/pallas_call | solution.py:769
  157.3 4.4 %all-to-all-done.1.rest_0_ = bf16[8,2,120,384]{3,2,1,0:T(8,128)(2,1)} async-done(((bf16[8,2,120,384]{3,2,1,0:T(8,128)(2,1)}), bf16[8,2,120,384]{3,2,1,0:T(8,128)(2,1)}, u32[]{:S(2)}, u32[]{:S(2)}) %all-to-all-start.1) | async-done | bytes 1474592 | tf_op jit(solution)/shard_map/all_to_all | solution.py:972
  161.7 3.8 %all-to-all-start.2 = ((bf16[32,112,128]{2,1,0:T(8,128)(2,1)}), bf16[32,112,128]{2,1,0:T(8,128)(2,1)S(1)}, u32[]{:S(2)}, u32[]{:S(2)}) async-start(bf16[32,112,128]{2,1,0:T(8,128)(2,1)} %bitcast.13), calls=%async_computation.2 | async-start | bytes 1835008 | tf_op jit(solution)/shard_map/all_to_all | solution.py:800
  165.5 14.0 %feature_backward.3 = (f32[64,192,119]{2,1,0:T(8,128)}, bf16[64,192,119]{2,1,0:T(8,128)(2,1)}, bf16[1280,128]{1,0:T(8,128)(2,1)}) custom-call(bf16[64,192,119]{2,1,0:T(8,128)(2,1)} %bitcast.27, bf16[64,208,128]{2,1,0:T(8,128)(2,1)} %get-tuple-element.74.n_ref, ...), custom_call_target="tpu_custom_call", output_to_operand_aliasing={{0}: (16, {}), {1}: (17, {})} | custom-call | flops 65999998976 | bytes 60000000 | tf_op jit(solution)/shard_map/feature_backward/pallas_call | solution.py:769
  179.6 0.0 copy-start.2
  179.6 10.5 %all-to-all-done.2.refs_0_ = bf16[32,112,128]{2,1,0:T(8,128)(2,1)S(1)} async-done(((bf16[32,112,128]{2,1,0:T(8,128)(2,1)}), bf16[32,112,128]{2,1,0:T(8,128)(2,1)S(1)}, u32[]{:S(2)}, u32[]{:S(2)}) %all-to-all-start.2) | async-done | bytes 917536 | tf_op jit(solution)/shard_map/all_to_all | solution.py:800
  190.1 0.0 copy-start.1
  190.1 0.9 copy-done.1
  191.0 1.9 sum_parts.2.refs_0_
  192.9 0.0 copy-done.2
  192.9 14.5 %all_to_all.25.refs_1_ = bf16[32,40,128]{2,1,0:T(8,128)(2,1)} all-to-all(bf16[32,40,128]{2,1,0:T(8,128)(2,1)S(1)} %bitcast.22), channel_id=1, replica_groups=mesh['table'=4,'rows'=8] {'table','rows'}, dimensions={0} | all-to-all | bytes 655360 | tf_op jit(solution)/shard_map/all_to_all | solution.py:800
  207.4 1.8 sum_parts.3
  209.2 13.8 %all_to_all.26.refs_1_ = bf16[8,152,128]{2,1,0:T(8,128)(2,1)S(1)} all-to-all(bf16[8,152,128]{2,1,0:T(8,128)(2,1)} %sum_parts.3), channel_id=1, replica_groups=mesh['table'=4,'rows'=8] {'rows'}, dimensions={0} | all-to-all | bytes 622592 | tf_op jit(solution)/shard_map/all_to_all | solution.py:815
  223.0 0.0 copy-start.3
  223.0 1.4 collective-permute-start.1
  224.5 0.0 collective-permute-start
  224.5 6.3 %collective-permute-done.1.refs_3_ = bf16[8,152,128]{2,1,0:T(8,128)(2,1)S(1)} collective-permute-done((bf16[8,152,128]{2,1,0:T(8,128)(2,1)S(1)}, bf16[8,152,128]{2,1,0:T(8,128)(2,1)S(1)}, u32[]{:S(2)}, u32[]{:S(2)}) %collective-permute-start.1) | collective-permute-done | bytes 311328 | tf_op jit(solution)/shard_map/ppermute | solution.py:818
  230.8 0.0 copy-start.4
  230.8 0.0 collective-permute-start.2
  230.8 0.0 collective-permute-done.refs_2_
  230.8 0.0 copy-start.5
  230.8 1.6 collective-permute-done.2.refs_4_
  232.4 0.0 copy-start.6
  232.4 0.0 copy-done.3
  232.4 0.0 copy-done.4
  232.4 0.0 copy-done.5
  232.4 0.7 copy-done.6
  233.2 7.3 %optimizer.1 = (f32[6,192,192]{2,1,0:T(8,128)}, f32[2,192,192]{2,1,0:T(8,128)}, f32[192,768]{1,0:T(8,128)}, f32[192,768]{1,0:T(8,128)}, f32[6,192]{1,0:T(8,128)}...) custom-call(s32[1]{0:T(128)} %bitcast.12.refs_0_, ...), custom_call_target="tpu_custom_call" | custom-call | flops 8800000000 | bytes 8000000 | tf_op jit(solution)/shard_map/optimizer/pallas_call | solution.py:934
Async XLA Ops:
  9.8 42.2 %all-to-all-start = ((bf16[8,2,120,384]{3,2,1,0:T(8,128)(2,1)}), bf16[8,2,120,384]{3,2,1,0:T(8,128)(2,1)S(1)}, u32[]{:S(2)}, u32[]{:S(2)}) async-start(bf16[8,2,120,384]{3,2,1,0:T(8,128)(2,1)} %slot_rows.1), calls=%async_computation | async-start | bytes 2949120 | tf_op jit(solution)/shard_map/all_to_all | solution.py:968
  51.9 1.1 copy-start
  122.8 39.0 %all-to-all-start.1 = ((bf16[8,2,120,384]{3,2,1,0:T(8,128)(2,1)}), bf16[8,2,120,384]{3,2,1,0:T(8,128)(2,1)}, u32[]{:S(2)}, u32[]{:S(2)}) async-start(bf16[8,2,120,384]{3,2,1,0:T(8,128)(2,1)} %bitcast.21), calls=%async_computation.1 | async-start | bytes 2949120 | tf_op jit(solution)/shard_map/all_to_all | solution.py:972
  161.7 28.3 %all-to-all-start.2 = ((bf16[32,112,128]{2,1,0:T(8,128)(2,1)}), bf16[32,112,128]{2,1,0:T(8,128)(2,1)S(1)}, u32[]{:S(2)}, u32[]{:S(2)}) async-start(bf16[32,112,128]{2,1,0:T(8,128)(2,1)} %bitcast.13), calls=%async_computation.2 | async-start | bytes 1835008 | tf_op jit(solution)/shard_map/all_to_all | solution.py:800
  179.6 13.3 %copy-start.2 = (bf16[1280,128]{1,0:T(8,128)(2,1)S(1)}, bf16[1280,128]{1,0:T(8,128)(2,1)}, u32[]{:S(2)}) copy-start(bf16[1280,128]{1,0:T(8,128)(2,1)} %get-tuple-element.109) | copy-start | bytes 983044
  190.1 0.9 copy-start.1
  223.0 9.4 %copy-start.3 = (bf16[8,152,128]{2,1,0:T(8,128)(2,1)}, bf16[8,152,128]{2,1,0:T(8,128)(2,1)S(1)}, u32[]{:S(2)}) copy-start(bf16[8,152,128]{2,1,0:T(8,128)(2,1)S(1)} %all_to_all.26.refs_1_) | copy-start | bytes 933892
  223.0 7.8 %collective-permute-start.1 = (bf16[8,152,128]{2,1,0:T(8,128)(2,1)S(1)}, bf16[8,152,128]{2,1,0:T(8,128)(2,1)S(1)}, u32[]{:S(2)}, u32[]{:S(2)}) collective-permute-start(bf16[8,152,128]{2,1,0:T(8,128)(2,1)S(1)} %all_to_all.26.refs_1_), channel_id=1, source_target_pairs={{0,16},{8,24},{16,0},{24,8},{1,17},{9,25},{17,1},{25,9},{2,18},{10... | collective-permute-start | bytes 933896 | tf_op jit(solution)/shard_map/ppermute | solution.py:818
  224.5 6.4 %collective-permute-start = (bf16[8,152,128]{2,1,0:T(8,128)(2,1)S(1)}, bf16[8,152,128]{2,1,0:T(8,128)(2,1)S(1)}, u32[]{:S(2)}, u32[]{:S(2)}) collective-permute-start(bf16[8,152,128]{2,1,0:T(8,128)(2,1)S(1)} %all_to_all.26.refs_1_), channel_id=1, source_target_pairs={{0,8},{8,0},{16,24},{24,16},{1,9},{9,1},{17,25},{25,17},{2,10},{10... | collective-permute-start | bytes 933896 | tf_op jit(solution)/shard_map/ppermute | solution.py:819
  230.8 1.6 copy-start.4
  230.8 1.6 collective-permute-start.2
  230.8 1.6 copy-start.5
  232.4 0.7 copy-start.6
where the time goes:
time: 241 us
  Pallas kernels  166 us (69%)
  blocking collectives  28.3 us (12%)
  waiting for transfers between devices  24.6 us (10%)
  starting transfers between devices  17.1 us (7%)
  local copies, waits for them, and re-layouts  2.78 us (1%)
    pallas_call x1, Pallas kernels, item_and_dense(): pl.pallas_call(functools.partial(item_kernel, RW, keys, OFF, WP, CC, WC),...  69.7 us
    pallas_call x2, Pallas kernels, feature_backward(): pl.pallas_call(functools.partial(backward_kernel, R, OFF, SL), grid=(rows...  44.1 us
    pallas_call x1, Pallas kernels, feature_forward(): pl.pallas_call(functools.partial(forward_kernel, R, OFF), grid=(rows // R...  33 us
    all_to_all x1, blocking collectives, sum_parts(): lax.all_to_all(packed.reshape(n, rows, 128), ('table', 'rows'), 0, 0)  14.5 us
    all_to_all x1, blocking collectives, gather_all(): own = lax.all_to_all(copies, 'rows', 0, 0)  13.8 us
    all_to_all x1, waiting for transfers between devices, sum_parts(): lax.all_to_all(packed.reshape(n, rows, 128), ('table', 'rows'), 0, 0)  10.5 us
    pallas_call x1, Pallas kernels, optimizer(): pl.pallas_call(functools.partial(optimizer_kernel, len(pieces), mid_rows)...  7.3 us
    all_to_all x1, starting transfers between devices, on_device(): slots = lax.all_to_all(own, 'rows', 0, 0).reshape((-1,) + own.shape[2:])  7.25 us
  transfers between devices with their start and end apart: 6, of which 5 were waited for; matrix products, arithmetic and copies ran while one was open for 0% of the time, Pallas kernels for 32%

commit v1 on v0

--- a/solution.py
+++ b/solution.py
@@ -122,35 +122,54 @@
     return jnp.asarray(place, BF)
 
 
-def prep_kernel(
-    proj, outw, w_in, w_outT, norms, wqkvT, wqkvI, wo, woT, wkv2, wkv2T, wq2, wq2T, wo2I, wo2, w1T, w1, w2T, w2, vec, nrow
-):
-    zc = jnp.zeros((D, DP - D), F32)
-    zr = jnp.zeros((DP - D, DP), BF)
+def padded_square(w):
+    a = jnp.concatenate([w, jnp.zeros((D, DP - D), F32)], 1).astype(BF)
+    a = jnp.concatenate([a, jnp.zeros((DP - D, DP), BF)], 0)
+    return a, a.T
+
+
+def first_weights_kernel(proj, outw, norms, wqkvT, woT, vec, nrow):
+    for i in range(3):
+        wqkvT[i * D : (i + 1) * D, :] = padded_square(proj[i])[1][0:D]
+    woT[...] = padded_square(outw[0])[1][0:D]
+    nrow[...] = jnp.zeros((8, DP), F32)
+    nrow[0:6, 0:D] = norms[...]
+    for i in range(6):
+        vec[i] = jnp.broadcast_to(nrow[i : i + 1, :], (128, DP)).T[0:D]
+
+
+def first_weights(proj, outw, norms):
+    return pl.pallas_call(
+        first_weights_kernel,
+        grid=(1,),
+        in_specs=[
+            pl.BlockSpec((3, D, D), lambda i: (0, 0, 0)),
+            pl.BlockSpec((1, D, D), lambda i: (0, 0, 0)),
+            whole(norms),
+        ],
+        out_specs=[whole(shape(a)) for a in ((3 * D, DP), (D, DP), (6, D, 128))],
+        out_shape=[shape((3 * D, DP)), shape((D, DP)), shape((6, D, 128), F32)],
+        scratch_shapes=[pltpu.VMEM((8, DP), F32)],
+        compiler_params=params(),
+        cost_estimate=cost(2),
+        name="first_weights",
+    )(proj, outw, norms)
+
+
+def weights_kernel(proj, outw, w_in, w_outT, wqkvI, wo, wkv2, wkv2T, wq2, wq2T, wo2I, wo2, w1T, w1, w2T, w2):
     row = lax.broadcasted_iota(jnp.int32, (D, DP), 0)
     eye = jnp.where(row == lax.broadcasted_iota(jnp.int32, (D, DP), 1), 1.0, 0.0).astype(BF)
-
-    def square(w):
-        a = jnp.concatenate([w, zc], 1)
-        a = jnp.concatenate([a.astype(BF), zr], 0)
-        return a, a.T
-
-    for i in range(3):
-        a, t = square(proj[i])
-        wqkvT[i * D : (i + 1) * D, :] = t[0:D]
     wqkvI[...] = jnp.concatenate([proj[0], proj[1], proj[2], eye[:, 0:D].astype(F32)], 1).astype(BF)
-    a, t = square(outw[0])
-    wo[...] = a[0:D]
-    woT[...] = t[0:D]
-    a, t = square(proj[3])
+    wo[...] = jnp.concatenate([outw[0], jnp.zeros((D, DP - D), F32)], 1).astype(BF)
+    a, t = padded_square(proj[3])
     wq2[...] = a
     wq2T[...] = t
-    a, t = square(outw[1])
+    a, t = padded_square(outw[1])
     wo2[...] = a[0:D]
     wo2I[:, 0:DP] = t[0:D]
     wo2I[:, DP : 2 * DP] = eye
     for i in range(2):
-        a, t = square(proj[4 + i])
+        a, t = padded_square(proj[4 + i])
         wkv2[:, i * DP : (i + 1) * DP] = a
         wkv2T[i * DP : (i + 1) * DP, :] = t
     zw = jnp.zeros((DP - D, FF), BF)
@@ -160,25 +179,19 @@
     a = w_outT[...].astype(BF)
     w2T[...] = a
     w2[...] = jnp.concatenate([a, zw], 0).T
-    nrow[...] = jnp.zeros((8, DP), F32)
-    nrow[0:6, 0:D] = norms[...]
-    for i in range(6):
-        vec[i] = jnp.broadcast_to(nrow[i : i + 1, :], (128, DP)).T[0:D]
-
-
-def prepare(proj, outw, w_in, w_outT, norms):
+
+
+def other_weights(proj, outw, w_in, w_outT):
     sq, half = shape((DP, DP)), shape((D, DP))
-    outs = [shape((3 * D, DP)), shape((D, 4 * D)), half, half, shape((DP, 2 * DP)), shape((2 * DP, DP)), sq, sq]
+    outs = [shape((D, 4 * D)), half, shape((DP, 2 * DP)), shape((2 * DP, DP)), sq, sq]
     outs += [shape((D, 2 * DP)), half, shape((FF, DP)), shape((D, FF)), shape((D, FF)), shape((FF, DP))]
-    outs += [shape((6, D, 128), F32)]
     return pl.pallas_call(
-        prep_kernel,
+        weights_kernel,
         out_shape=outs,
-        scratch_shapes=[pltpu.VMEM((8, DP), F32)],
         compiler_params=params(),
         cost_estimate=cost(4),
-        name="weights",
-    )(proj, outw, w_in, w_outT, norms)
+        name="other_weights",
+    )(proj, outw, w_in, w_outT)
 
 
 def two_heads(a, b):
@@ -321,7 +334,7 @@
         ht_ref[16 * j : 16 * j + 16] = turn_block(perm_ref, hs[:, 16 * j : 16 * j + 16, :], R)
 
 
-def feature_forward(cells, cot, ws, R=16, OFF=6):
+def feature_forward(cells, cot, ws, R=16, OFF=2):
     rows = cells.shape[0]
     nat = lambda a, b: pl.BlockSpec((R, a, b), lambda i: (i, 0, 0))
     turned = pl.BlockSpec((FP, R, DP), lambda i: (0, i, 0))
@@ -345,10 +358,23 @@
     )(cells, cot, *ws)
 
 
+def pair_up(table, i, ny, back=False):
+    shift = ny - i // 2 if back else i // 2
+    return lax.rem(table // 2 + shift, ny) * 2 + lax.rem(table + i % 2, 2)
+
+
+def hand_out(table_ref, pack, piece_refs):
+    tables = len(piece_refs)
+    rows = pack.shape[0] // tables
+    for i, ref in enumerate(piece_refs):
+        place = pair_up(table_ref[0], i, tables // 2)
+        ref[...] = pack[pl.ds(pl.multiple_of(place * rows, 8), rows)].astype(BF)
+
+
 def pack_pair(ref, at, a, b):
-    ref[at : at + D] = a[0:D, 0:128].astype(BF)
-    ref[at + D : at + 2 * D] = b[0:D, 0:128].astype(BF)
-    ref[at + 2 * D : at + 3 * D] = jnp.concatenate([a[0:D, 128:D], b[0:D, 128:D]], 1).astype(BF)
+    ref[at : at + D] = a[0:D, 0:128]
+    ref[at + D : at + 2 * D] = b[0:D, 0:128]
+    ref[at + 2 * D : at + 3 * D] = jnp.concatenate([a[0:D, 128:D], b[0:D, 128:D]], 1)
 
 
 def pack_norms(ref, at, sums):
@@ -359,14 +385,16 @@
         v = jnp.sum(s, 0, keepdims=True)
         rows += [v[:, 0:128], v[:, 128:256]]
     rows.append(jnp.zeros((ref.shape[0] - at - len(rows), 128), F32))
-    ref[at:] = jnp.concatenate(rows, 0).astype(BF)
+    ref[at:] = jnp.concatenate(rows, 0)
 
 
 def item_kernel(
-    RW, keys, OFF, WP, CC, WC, ht_ref, ct_ref, slot_ref, perm_ref, wq_ref, wqT_ref, woI_ref, wo_ref, w1T_ref, w1_ref, w2T_ref, w2_ref,
-    wkv_ref, wkvT_ref, vec_ref, y_ref, g1_ref, back_ref, pack_ref, dwq, dwo, dw1, dw2, dnp, dwkv, bias_ref, hk_ref, bk_ref,
-    dk_ref, dv_ref, hbTs, ois, hb2Ts, actss, dbTs, duss, dabTs, dqss, slp,
+    RW, keys, tables, OFF, WP, CC, WC, table_ref, ht_ref, ct_ref, slot_ref, perm_ref, wq_ref, wqT_ref, woI_ref, wo_ref, w1T_ref, w1_ref, w2T_ref, w2_ref,
+    wkv_ref, wkvT_ref, vec_ref, y_ref, g1_ref, back_ref, *rest
 ):
+    piece_refs, rest = rest[:tables], rest[tables:]
+    (dwq, dwo, dw1, dw2, dnp, dwkv, bias_ref, pack_ref, hk_ref, bk_ref,
+     dk_ref, dv_ref, hbTs, ois, hb2Ts, actss, dbTs, duss, dabTs, dqss, slp) = rest
     step = pl.program_id(0)
     blocks = [(s, b, min(16, FS - b)) for s in range(0, keys, 16) for b in range(0, FS, 16)]
 
@@ -577,26 +605,27 @@
         for ref in (dw1, dw2):
             t = ref[...].T
             for j in range(FF // 128):
-                pack_ref[at : at + D] = t[:, 128 * j : 128 * j + 128].astype(BF)
+                pack_ref[at : at + D] = t[:, 128 * j : 128 * j + 128]
                 at += D
         pack_pair(pack_ref, at, dwq, tall(dwo[...]).T)
         pack_pair(pack_ref, at + PAIR, dwkv[:, 0:DP], dwkv[:, DP:])
         pack_norms(pack_ref, at + 2 * PAIR, [dnp[i] for i in range(4)])
-
-
-def item_and_dense(ht, ct, slots, perm, ws, vec, packed, OFF=0, WP=20, CC=384, WC=384):
+        hand_out(table_ref, pack_ref, piece_refs)
+
+
+def item_and_dense(table, ht, ct, slots, perm, ws, vec, packed, tables, OFF=0, WP=20, CC=384, WC=384):
     RW = ht.shape[1]
     keys = 2 * slots.shape[0]
     M = FB * RW
     cells = pl.BlockSpec((FB, RW, DP), lambda i: (i, 0, 0))
-    accs = [(D, DP), (D, DP), (FF, D), (FF, D), (4, D, 128), (DP, 2 * DP), (keys, 128)]
+    accs = [(D, DP), (D, DP), (FF, D), (FF, D), (4, D, 128), (DP, 2 * DP), (keys, 128), (packed, 128)]
     kept = [(D, M), (M, DP), (D, M), (FF, M), (D, M), (FF, M), (D, M), (M, DP)]
     flat = [slots, perm, *ws, vec]
-    outs = [shape((FS, RW, DP))] * 2 + [shape(slots.shape), shape((packed, 128))]
+    outs = [shape((FS, RW, DP))] * 2 + [shape(slots.shape)] + [shape((packed // tables, 128))] * tables
     return pl.pallas_call(
-        functools.partial(item_kernel, RW, keys, OFF, WP, CC, WC),
+        functools.partial(item_kernel, RW, keys, tables, OFF, WP, CC, WC),
         grid=(FS // FB,),
-        in_specs=[cells, cells] + [whole(a) for a in flat],
+        in_specs=[pl.BlockSpec(memory_space=pltpu.SMEM), cells, cells] + [whole(a) for a in flat],
         out_specs=[cells, cells] + [whole(a) for a in outs[2:]],
         out_shape=outs,
         scratch_shapes=[pltpu.VMEM(a, F32) for a in accs]
@@ -607,54 +636,20 @@
         compiler_params=params(),
         cost_estimate=cost(66),
         name="item_and_dense",
-    )(ht, ct, *flat)
-
-
-def backward_kernel(R, OFF, SL, x_ref, n_ref, qkv_ref, p_ref, l_ref, of_ref, g1t_ref, yt_ref, *rest):
-    if SL:
-        (dsl_ref, wqkvI_ref, wo_ref, vec_ref, perm_ref, iqkv, iwo, inp, _, _,
-         cg_ref, y_ref, pack_ref, gs, ys, xs, os, dqs, das, dqkv, dwo, dnp) = rest
-    else:
-        (wqkvI_ref, wo_ref, vec_ref, perm_ref, cg_ref, y_ref, dqkv, dwo, dnp, gs, ys, xs, os, dqs, das) = rest
-
-    @pl.when(pl.program_id(0) == 0)
-    def _():
-        xs[...] = jnp.zeros_like(xs)
-        for i, ref in enumerate((dqkv, dwo, dnp)):
-            ref[...] = (iqkv, iwo, inp)[i][...] if SL else jnp.zeros_like(ref)
-
-    col = lax.broadcasted_iota(jnp.int32, (16, 1, 1), 0)
-
-    def turn(ref, out, j):
-        block = ref[16 * j : min(16 * j + 16, FS)]
-        if block.shape[0] < 16:
-            block = jnp.concatenate([block, jnp.zeros((16 - block.shape[0],) + block.shape[1:], BF)], 0)
-        if 16 * j + 16 > F:
-            block = jnp.where(col < F - 16 * j, block, 0).astype(BF)
-        out[:, 16 * j : 16 * j + 16, :] = turn_block(perm_ref, block, 16)
-
-    for j in range(FP // 16):
-        turn(g1t_ref, gs, j)
-    back = []
-    if SL:
-        both = dsl_ref[0].astype(F32)
-        for i in range(1, dsl_ref.shape[0]):
-            both = both + dsl_ref[i].astype(F32)
-        z0 = jnp.zeros((FP - FS, 2 * D), F32)
-        for c in range(SL // 2):
-            t = jnp.concatenate([both[c], z0], 0).T
-            back += [t[0:D], t[D : 2 * D]]
-
+    )(table, ht, ct, *flat)
+
+
+def backward_rows(
+    x_ref, n_ref, qkv_ref, p_ref, l_ref, of_ref, wqkvI_ref, wo_ref, vec_ref, cg_ref, xs, os, dqs, das, dqkv, dwo, dnp, grad_of, base_ref=None
+):
     def pair(c):
         at = slice(2 * c * FP, (2 * c + 2) * FP)
-        dabs, das32 = [], []
+        dabs = []
         for u in range(2):
             r = 2 * c + u
             xs[:, r * FP : r * FP + F] = x_ref[r]
             os[:, r * FP : (r + 1) * FP] = of_ref[r]
-            g = gs[r].T[0:D].astype(F32)
-            if r < SL:
-                g = g + back[r]
+            g = grad_of(r)
             n = n_ref[r, 0:D, :].astype(F32)
             rc = n_ref[r, D : D + 16, :].astype(F32)[0:1]
             dnp[0] += g * n
@@ -697,8 +692,40 @@
         yield
         cg = mm(wqkvI_ref[...], jnp.concatenate([dqs[:, at], dab], 0))
         for u in range(2):
-            cg_ref[2 * c + u] = cg[:, u * FP : u * FP + F]
-        yield
+            own = cg[:, u * FP : u * FP + F]
+            cg_ref[2 * c + u] = own if base_ref is None else own + base_ref[2 * c + u]
+        yield
+
+    def sums(at):
+        dqkv[...] += mm_nt(dqs[:, at], xs[:, at])
+        yield
+        dwo[...] += mm_nt(os[:, at], das[:, at])
+        yield
+
+    return pair, sums
+
+
+def backward_kernel(
+    R, OFF, x_ref, n_ref, qkv_ref, p_ref, l_ref, of_ref, g1t_ref, yt_ref, wqkvI_ref, wo_ref, vec_ref, perm_ref,
+    cg_ref, y_ref, dqkv, dwo, dnp, gs, ys, xs, os, dqs, das,
+):
+    @pl.when(pl.program_id(0) == 0)
+    def _():
+        for ref in (xs, dqkv, dwo, dnp):
+            ref[...] = jnp.zeros_like(ref)
+
+    col = lax.broadcasted_iota(jnp.int32, (16, 1, 1), 0)
+
+    def turn(ref, out, j):
+        block = ref[16 * j : min(16 * j + 16, FS)]
+        if block.shape[0] < 16:
+            block = jnp.concatenate([block, jnp.zeros((16 - block.shape[0],) + block.shape[1:], BF)], 0)
+        if 16 * j + 16 > F:
+            block = jnp.where(col < F - 16 * j, block, 0).astype(BF)
+        out[:, 16 * j : 16 * j + 16, :] = turn_block(perm_ref, block, 16)
+
+    for j in range(FP // 16):
+        turn(g1t_ref, gs, j)
 
     def outputs():
         for j in range(FP // 16):
@@ -708,105 +735,150 @@
             y_ref[r] = ys[r].T[0:D, 0:F]
             yield
 
-    def sums(part):
-        at = slice(part * R * FP // 2, (part + 1) * R * FP // 2)
-        for i in range(3):
-            dqkv[i * D : (i + 1) * D] += mm_nt(dqs[i * D : (i + 1) * D, at], xs[:, at])
-            yield
-        dwo[...] += mm_nt(os[:, at], das[:, at])
-        yield
-
+    pair, sums = backward_rows(
+        x_ref, n_ref, qkv_ref, p_ref, l_ref, of_ref, wqkvI_ref, wo_ref, vec_ref, cg_ref, xs, os, dqs, das, dqkv, dwo, dnp,
+        lambda r: gs[r].T[0:D].astype(F32),
+    )
     Q = R // 4
+    M = R * FP // 2
     for half in range(2):
         streams = [(pair(c), (c - half * Q) * OFF, 1) for c in range(half * Q, (half + 1) * Q)]
-        streams.append((sums(0) if half else outputs(), 3, 1))
+        streams.append((sums(slice(0, M)) if half else outputs(), 3, 1))
         weave(streams)
-    for _ in sums(1):
+    for _ in sums(slice(M, 2 * M)):
         pass
 
-    if SL:
-
-        @pl.when(pl.program_id(0) == pl.num_programs(0) - 1)
-        def _():
-            zc = jnp.zeros((D, DP - D), F32)
-            three = [jnp.concatenate([dqkv[i * D : (i + 1) * D], zc], 1).T for i in range(3)]
-            pack_pair(pack_ref, 0, three[0], three[1])
-            pack_pair(pack_ref, PAIR, three[2], dwo)
-            pack_norms(pack_ref, 2 * PAIR, [dnp[0], dnp[1]])
-
-
-def feature_backward(x, saved, g1t, yt, wqkvI, wo, vec, perm, row0, rows, R=16, OFF=6, slots=None, prev=None, packed=0):
-    b0 = row0 // R
-    nat = lambda a: pl.BlockSpec((R,) + a.shape[1:], lambda i: (i + b0, 0, 0))
-    turned = pl.BlockSpec((FS, R, DP), lambda i: (0, i + b0, 0))
-    real = pl.BlockSpec((R, D, F), lambda i: (i + b0, 0, 0))
+
+def feature_backward(x, saved, g1t, yt, wqkvI, wo, vec, perm, R=16, OFF=1):
+    rows = x.shape[0]
+    nat = lambda a: pl.BlockSpec((R,) + a.shape[1:], lambda i: (i, 0, 0))
+    turned = pl.BlockSpec((FS, R, DP), lambda i: (0, i, 0))
     accs = [shape((3 * D, D), F32), shape((D, D), F32), shape((2, D, FP), F32)]
-    ins = [x, *saved, g1t, yt]
-    specs = [real] + [nat(a) for a in saved] + [turned] * 2
-    out_shape = [shape((x.shape[0], D, F), F32), shape((x.shape[0], D, F))]
-    out_specs = [real, real]
+    shared = [wqkvI, wo, vec, perm]
     M = R * FP
-    scratch = [pltpu.VMEM(a, BF) for a in ((R, FP, DP), (R, FP, DP), (D, M), (D, M), (3 * D, M), (D, M))]
-    SL = 0
-    alias = {}
-    shared = [wqkvI, wo, vec, perm]
-    if slots is not None:
-        SL = 2 * slots.shape[1]
-        shared = [slots] + shared
-    ins += shared
-    specs += [whole(a) for a in shared]
-    if prev is not None:
-        cg, y, *acc = prev
-        ins += list(acc) + [cg, y]
-        specs += [whole(a) for a in acc] + [pl.BlockSpec(memory_space=pl.ANY)] * 2
-        alias = {len(ins) - 2: 0, len(ins) - 1: 1}
-        out_shape.append(shape((packed, 128)))
-        out_specs.append(pl.BlockSpec((packed, 128), lambda i: (0, 0)))
-        scratch += [pltpu.VMEM(a.shape, F32) for a in accs]
-    else:
-        out_shape += accs
-        out_specs += [whole(a) for a in accs]
     return pl.pallas_call(
-        functools.partial(backward_kernel, R, OFF, SL),
+        functools.partial(backward_kernel, R, OFF),
         grid=(rows // R,),
-        in_specs=specs,
-        out_specs=out_specs,
-        out_shape=out_shape,
-        input_output_aliases=alias,
-        scratch_shapes=scratch,
+        in_specs=[nat(x)] + [nat(a) for a in saved] + [turned] * 2 + [whole(a) for a in shared],
+        out_specs=[nat(x), nat(x)] + [whole(a) for a in accs],
+        out_shape=[shape(x.shape, F32), shape(x.shape)] + accs,
+        scratch_shapes=[pltpu.VMEM(a, BF) for a in ((R, FP, DP), (R, FP, DP), (D, M), (D, M), (3 * D, M), (D, M))],
         compiler_params=params(),
         cost_estimate=cost(60 * rows // R),
         name="feature_backward",
+    )(x, *saved, g1t, yt, *shared)
+
+
+def slots_back_kernel(
+    SL, tables, table_ref, x_ref, n_ref, qkv_ref, p_ref, l_ref, of_ref, slot_ref, base_ref, iqkv, iwo, inp, wqkvI_ref, wo_ref, vec_ref,
+    cg_ref, *rest,
+):
+    piece_refs, rest = rest[:tables], rest[tables:]
+    pack_ref, xs, os, dqs, das, dqkv, dwo, dnp = rest
+    xs[...] = jnp.zeros_like(xs)
+    for ref, init in ((dqkv, iqkv), (dwo, iwo), (dnp, inp)):
+        ref[...] = init[...]
+    both = slot_ref[0].astype(F32)
+    for i in range(1, slot_ref.shape[0]):
+        both = both + slot_ref[i].astype(F32)
+    z0 = jnp.zeros((FP - FS, 2 * D), F32)
+    live = lax.broadcasted_iota(jnp.int32, (1, FP), 1) < F
+    back = []
+    for c in range(SL // 2):
+        t = jnp.where(live, jnp.concatenate([both[c], z0], 0).T, 0.0)
+        back += [t[0:D], t[D : 2 * D]]
+    pair, sums = backward_rows(
+        x_ref, n_ref, qkv_ref, p_ref, l_ref, of_ref, wqkvI_ref, wo_ref, vec_ref, cg_ref, xs, os, dqs, das, dqkv, dwo, dnp,
+        lambda r: back[r], base_ref,
+    )
+    weave([(pair(c), 0, 1) for c in range(SL // 2)])
+    for _ in sums(slice(0, SL * FP)):
+        pass
+    zc = jnp.zeros((D, DP - D), F32)
+    three = [jnp.concatenate([dqkv[i * D : (i + 1) * D], zc], 1).T for i in range(3)]
+    pack_pair(pack_ref, 0, three[0], three[1])
+    pack_pair(pack_ref, PAIR, three[2], dwo)
+    pack_norms(pack_ref, 2 * PAIR, [dnp[0], dnp[1]])
+    hand_out(table_ref, pack_ref, piece_refs)
+
+
+def slots_backward(table, x, saved, slots, prev, wqkvI, wo, vec, packed, tables):
+    SL = 2 * slots.shape[1]
+    nat = lambda a: pl.BlockSpec((SL,) + a.shape[1:], lambda i: (i, 0, 0))
+    cg, *accs = prev
+    flat = list(accs) + [wqkvI, wo, vec]
+    pieces = [shape((packed // tables, 128))] * tables
+    M = SL * FP
+    ins = [table, x, *saved, slots, cg, *flat]
+    return pl.pallas_call(
+        functools.partial(slots_back_kernel, SL, tables),
+        grid=(1,),
+        in_specs=[pl.BlockSpec(memory_space=pltpu.SMEM), nat(x)]
+        + [nat(a) for a in saved]
+        + [whole(slots), nat(cg)]
+        + [whole(a) for a in flat],
+        out_specs=[nat(cg)] + [whole(a) for a in pieces],
+        out_shape=[shape(cg.shape, F32)] + pieces,
+        input_output_aliases={len(saved) + 3: 0},
+        scratch_shapes=[pltpu.VMEM((packed, 128), F32)]
+        + [pltpu.VMEM(a, BF) for a in ((D, M), (D, M), (3 * D, M), (D, M))]
+        + [pltpu.VMEM(a.shape, F32) for a in accs],
+        compiler_params=params(),
+        cost_estimate=cost(8),
+        name="slots_backward",
     )(*ins)
 
 
-def sum_kernel(n, *refs):
-    *ready_refs, parts_ref, out_ref = refs
+def table_sums(tables, pieces):
+    sent = []
+    for i, a in enumerate(pieces):
+        to = [(t, (t // 2 + i // 2) % (tables // 2) * 2 + (t + i) % 2) for t in range(tables)]
+        sent.append(lax.ppermute(a, "table", to) if i else a)
+    return sent
+
+
+def join_kernel(tables, *refs):
+    out_ref = refs[-1]
+    at = 0
+    for group in (refs[:tables], refs[tables : 2 * tables]):
+        total = group[0][...].astype(F32)
+        for ref in group[1:]:
+            total = total + ref[...].astype(F32)
+        rows = total.shape[0] // out_ref.shape[0]
+        for i in range(out_ref.shape[0]):
+            out_ref[i, at : at + rows] = total[i * rows : (i + 1) * rows].astype(BF)
+        at += rows
+
+
+def join_tables(shards, mids, tails):
+    rows = (mids[0].shape[0] + tails[0].shape[0]) // shards
+    return pl.pallas_call(
+        functools.partial(join_kernel, len(mids)),
+        out_shape=shape((shards, rows, 128)),
+        compiler_params=params(),
+        cost_estimate=cost(2),
+        name="join_tables",
+    )(*mids, *tails)
+
+
+def sum_kernel(parts_ref, out_ref):
     total = parts_ref[0].astype(F32)
-    for i in range(1, n):
+    for i in range(1, parts_ref.shape[0]):
         total = total + parts_ref[i].astype(F32)
     total = total.astype(BF)
-    if not ready_refs:
-        out_ref[...] = total
-        return
-    rows = ready_refs[0].shape[0]
     for i in range(out_ref.shape[0]):
-        out_ref[i, 0:rows] = ready_refs[0][...]
-        out_ref[i, rows:] = total
-
-
-def sum_parts(packed, n, ready=None):
-    rows = packed.shape[0] // n
-    parts = lax.all_to_all(packed.reshape(n, rows, 128), ("table", "rows"), 0, 0)
-    ins = [parts] if ready is None else [ready, parts]
-    out = (rows, 128) if ready is None else (lax.axis_size("rows"), ready.shape[0] + rows, 128)
+        out_ref[i] = total
+
+
+def sum_rows(parts):
+    parts = lax.all_to_all(parts, "rows", 0, 0)
     return pl.pallas_call(
-        functools.partial(sum_kernel, n),
-        out_shape=shape(out),
+        sum_kernel,
+        out_shape=shape(parts.shape),
         compiler_params=params(),
         cost_estimate=cost(2),
-        name="sum_parts",
-    )(*ins)
+        name="sum_rows",
+    )(parts)
 
 
 def gather_all(copies):
@@ -845,7 +917,7 @@
     table = table_ref[0]
     ny = tables // 2
     for i, ref in enumerate(piece_refs):
-        place = lax.rem(table // 2 - i // 2 + ny, ny) * 2 + lax.rem(table + i % 2, 2)
+        place = pair_up(table, i, ny, True)
         for out, at, end in ((mid_ref, 0, mid_rows), (tail_ref, mid_rows, ref.shape[1])):
             rows = ref.shape[0] * (end - at)
             start = pl.multiple_of(place * rows, 8)
@@ -926,10 +998,9 @@
     norm_n[...] = w - update * (RATE * jnp.maximum(0.001, w_rms) / jnp.maximum(1.0, rms / CLIP))
 
 
-def optimizer(pieces, mid_rows, *state):
+def optimizer(table, pieces, mid_rows, *state):
     proj, outw, w_in, w_outT, norms, sr, sc, ms, hs, ns = state
     shards, rows, _ = pieces[0].shape
-    table = lax.axis_index("table").astype(jnp.int32).reshape(1)
     order = [proj, outw, w_in, w_outT, norms, proj, outw, w_in, w_outT, norms, sr, sc, ms, hs, ns]
     outs = pl.pallas_call(
         functools.partial(optimizer_kernel, len(pieces), mid_rows),
@@ -959,25 +1030,24 @@
     tail_rows = -(-TAIL // unit) * unit
     mid_rows = -(-MID // unit) * unit
     perm = perm_matrix()
-    (wqkvT, wqkvI, wo, woT, wkv2, wkv2T, wq2, wq2T, wo2I, wo2, w1T, w1, w2T, w2, vec) = prepare(
-        proj, outw, w_in, w_outT, norms
-    )
-    R = 16
-    shards = lax.axis_size("rows")
+    shards, tables = lax.axis_size("rows"), lax.axis_size("table")
+    table = lax.axis_index("table").astype(jnp.int32).reshape(1)
+    wqkvT, woT, vec = first_weights(proj, outw, norms)
     own = slot_rows(shards, train_count, key_mask, train_order, x, wqkvT, woT, vec)
     slots = lax.all_to_all(own, "rows", 0, 0).reshape((-1,) + own.shape[2:])
+    w_in, _ = lax.optimization_barrier((w_in, own))
+    wqkvI, wo, *ws = other_weights(proj, outw, w_in, w_outT)
     ht, ct, *saved = feature_forward(x, cot, (wqkvT, woT, vec, perm))
-    ws = (wq2, wq2T, wo2I, wo2, w1T, w1, w2T, w2, wkv2, wkv2T)
-    yt, g1t, back, mid = item_and_dense(ht, ct, slots, perm, ws, vec, mid_rows)
+    wkv2, wkv2T, *ws = ws
+    yt, g1t, back, *mids = item_and_dense(table, ht, ct, slots, perm, (*ws, wkv2, wkv2T), vec, mid_rows, tables)
     back = lax.all_to_all(back.reshape(own.shape), "rows", 0, 0)
-    args = (x, saved, g1t, yt, wqkvI, wo, vec, perm)
-    prev = list(feature_backward(*args, row0=R, rows=rows_here - R, R=R))
-    mid, back, prev[4] = lax.optimization_barrier((mid, back, prev[4]))
-    mid = sum_parts(mid, n)
-    cg, y, tail = feature_backward(*args, row0=0, rows=R, R=R, slots=back, prev=prev, packed=tail_rows)
-    tail, mid = lax.optimization_barrier((tail, mid))
-    pieces = gather_all(sum_parts(tail, n, mid))
-    return (jnp.swapaxes(y, 1, 2)[None], jnp.swapaxes(cg, 1, 2)[None], *optimizer(pieces, mid.shape[0], *state))
+    mids = table_sums(tables, mids)
+    cg, y, *accs = feature_backward(x, saved, g1t, yt, wqkvI, wo, vec, perm)
+    mids, accs = lax.optimization_barrier((mids, accs))
+    cg, *tails = slots_backward(table, x, saved, back, (cg, *accs), wqkvI, wo, vec, tail_rows, tables)
+    tails = table_sums(tables, tails)
+    pieces = gather_all(sum_rows(join_tables(shards, mids, tails)))
+    return (jnp.swapaxes(y, 1, 2)[None], jnp.swapaxes(cg, 1, 2)[None], *optimizer(table, pieces, mid_rows // n, *state))
 
 
 def solution(mesh):

time: 241 us -> 226 us (0.938)
  Pallas kernels: 166 us -> 156 us
  waiting for transfers between devices: 24.6 us -> 18.4 us
    all_to_all x1 -> x0, waiting for transfers between devices: 10.5 us -> none  [sum_parts(): lax.all_to_all(packed.reshape(n, rows, 128), ('table', 'rows'), 0, 0)]
    pallas_call x1, Pallas kernels: 33 us -> 25.2 us  [feature_forward(): pl.pallas_call(functools.partial(forward_kernel, R, OFF), grid=(rows // R...]
    ppermute x0 -> x6, waiting for transfers between devices: none -> 4.91 us  [table_sums(): sent.append(lax.ppermute(a, 'table', to) if i else a)]
    all_to_all x1, waiting for transfers between devices: 1.85 us -> 6.28 us  [on_device(): slots = lax.all_to_all(own, 'rows', 0, 0).reshape((-1,) + own.shape[2:])]
    all_to_all x1, waiting for transfers between devices: 4.36 us -> 0.01 us  [on_device(): back = lax.all_to_all(back.reshape(own.shape), 'rows', 0, 0)]
    ppermute x0 -> x6, starting transfers between devices: none -> 3.83 us  [table_sums(): sent.append(lax.ppermute(a, 'table', to) if i else a)]
    all_to_all x1 -> x0, starting transfers between devices: 3.81 us -> none  [sum_parts(): lax.all_to_all(packed.reshape(n, rows, 128), ('table', 'rows'), 0, 0)]
    pallas_call x6 -> x7, Pallas kernels: 121 us -> 119 us  [the longest x1 70 us: item_and_dense(): pl.pallas_call(functools.partial(item_kernel, RW, keys, tables, OFF, WP,...]
  transfers between devices with their start and end apart: 6 -> 11, of which waited for: 5 -> 5; matrix products, arithmetic and copies ran while one was open for 0% -> 0% of each run, Pallas kernels for 32% -> 27%
where the time goes in v1:
time: 226 us; the launch traced here: 225 us
  Pallas kernels  156 us (69%)
  blocking collectives  30.1 us (13%)
  waiting for transfers between devices  18.4 us (8%)
  starting transfers between devices  16.9 us (7%)
  local copies, waits for them, and re-layouts  2.47 us (1%)
    pallas_call x1, Pallas kernels, item_and_dense(): pl.pallas_call(functools.partial(item_kernel, RW, keys, tables, OFF, WP,...  70 us
    pallas_call x1, Pallas kernels, feature_backward(): pl.pallas_call(functools.partial(backward_kernel, R, OFF), grid=(rows //...  33 us
    pallas_call x1, Pallas kernels, feature_forward(): pl.pallas_call(functools.partial(forward_kernel, R, OFF), grid=(rows // R...  25.2 us
    all_to_all x1, blocking collectives, sum_rows(): parts = lax.all_to_all(parts, 'rows', 0, 0)  16.6 us
    all_to_all x1, blocking collectives, gather_all(): own = lax.all_to_all(copies, 'rows', 0, 0)  13.5 us
    pallas_call x1, Pallas kernels, optimizer(): pl.pallas_call(functools.partial(optimizer_kernel, len(pieces), mid_rows)...  7.3 us
    all_to_all x1, starting transfers between devices, on_device(): slots = lax.all_to_all(own, 'rows', 0, 0).reshape((-1,) + own.shape[2:])  7.25 us
    all_to_all x1, waiting for transfers between devices, on_device(): slots = lax.all_to_all(own, 'rows', 0, 0).reshape((-1,) + own.shape[2:])  6.28 us
  transfers between devices with their start and end apart: 11, of which 5 were waited for; matrix products, arithmetic and copies ran while one was open for 0% of the time, Pallas kernels for 27%

profile of v1, /device:TPU:0, one launch (start us, length us, event | category | flops | bytes accessed | tf_op | source)
XLA Modules:
  0.0 225.4 jit_solution(17605866991216341643)
XLA Ops:
  1.3 2.4 %first_weights.1 = (bf16[576,256]{1,0:T(8,128)(2,1)}, bf16[192,256]{1,0:T(8,128)(2,1)}, f32[6,192,128]{2,1,0:T(8,128)}) custom-call(f32[6,192,192]{2,1,0:T(8,128)} %refs_5_.1, f32[2,192,192]{2,1,0:T(8,128)} %refs_6_.1, f32[6,192]{1,0:T(8,128)} %refs_9_.1), custom_call_target="tpu_custom_call" | custom-call | flops 2200000000 | bytes 2000000 | tf_op jit(solution)/shard_map/first_weights/pallas_call | solution.py:142
  3.7 4.7 %slot_rows.1 = bf16[8,2,120,384]{3,2,1,0:T(8,128)(2,1)} custom-call(s32[1]{0:T(128)S(6)} %copy.35.count_ref, s32[1,4]{1,0:T(1,128)} %mask_ref.1, s32[1,4]{1,0:T(1,128)} %order_ref.1, bf16[64,192,119]{2,1,0:T(8,128)(2,1)} %bitcast.19, bf16[576,256]{1,0:T(8,128)(2,1)} %get-tuple-element.79.wqkvT_ref, bf16[192,256]{1,0:T(8,128)(2,1)} %get-tuple-element.80.woT_ref, ...), custom_call_target="tpu_custom_call" | custom-call | flops 5500000256 | bytes 5000000 | tf_op jit(solution)/shard_map/slot_rows/pallas_call | solution.py:271
  8.3 7.2 %all-to-all-start = ((bf16[8,2,120,384]{3,2,1,0:T(8,128)(2,1)}), bf16[8,2,120,384]{3,2,1,0:T(8,128)(2,1)S(1)}, u32[]{:S(2)}, u32[]{:S(2)}) async-start(bf16[8,2,120,384]{3,2,1,0:T(8,128)(2,1)} %slot_rows.1), calls=%async_computation | async-start | bytes 2949120 | tf_op jit(solution)/shard_map/all_to_all | solution.py:1037
  15.6 3.4 %other_weights.1 = (bf16[192,768]{1,0:T(8,128)(2,1)}, bf16[192,256]{1,0:T(8,128)(2,1)}, bf16[256,512]{1,0:T(8,128)(2,1)}, bf16[512,256]{1,0:T(8,128)(2,1)}, bf16...) custom-call(f32[6,192,192]{2,1,0:T(8,128)} %refs_5_.1, ...), custom_call_target="tpu_custom_call" | custom-call | flops 4400000000 | bytes 4000000 | tf_op jit(solution)/shard_map/other_weights/pallas_call | solution.py:188
  19.0 25.2 %feature_forward.1 = (bf16[128,64,256]{2,1,0:T(8,128)(2,1)}, bf16[128,64,256]{2,1,0:T(8,128)(2,1)}, bf16[64,208,128]{2,1,0:T(8,128)(2,1)}, bf16[64,576,128]{2,1,...) custom-call(bf16[64,192,119]{2,1,0:T(8,128)(2,1)} %bitcast.20, ...), custom_call_target="tpu_custom_call" | custom-call | flops 39600001024 | bytes 36000000 | tf_op jit(solution)/shard_map/feature_forward/pallas_call | solution.py:343
  44.2 6.3 %all-to-all-done = bf16[8,2,120,384]{3,2,1,0:T(8,128)(2,1)S(1)} async-done(((bf16[8,2,120,384]{3,2,1,0:T(8,128)(2,1)}), bf16[8,2,120,384]{3,2,1,0:T(8,128)(2,1)S(1)}, u32[]{:S(2)}, u32[]{:S(2)}) %all-to-all-start) | async-done | bytes 1474592 | tf_op jit(solution)/shard_map/all_to_all | solution.py:1037
  50.5 0.0 copy-start
  50.5 1.1 copy-done
  51.6 70.0 %item_and_dense.1 = (bf16[120,64,256]{2,1,0:T(8,128)(2,1)}, bf16[120,64,256]{2,1,0:T(8,128)(2,1)}, bf16[16,120,384]{2,1,0:T(8,128)(2,1)}, bf16[896,128]{1,0:T(8,...) custom-call(s32[1]{0:T(128)} %bitcast.5.table_ref.refs_0_, ...), custom_call_target="tpu_custom_call" | custom-call | flops 72600002560 | bytes 66000000 | tf_op jit(solution)/shard_map/item_and_dense/pallas_call | solution.py:625
  121.6 4.5 %all-to-all-start.1 = ((bf16[8,2,120,384]{3,2,1,0:T(8,128)(2,1)}), bf16[8,2,120,384]{3,2,1,0:T(8,128)(2,1)}, u32[]{:S(2)}, u32[]{:S(2)}) async-start(bf16[8,2,120,384]{3,2,1,0:T(8,128)(2,1)} %bitcast.23), calls=%async_computation.1 | async-start | bytes 2949120 | tf_op jit(solution)/shard_map/all_to_all | solution.py:1043
  126.1 0.1 collective-permute-start
  126.2 1.6 collective-permute-start.1
  127.8 0.3 collective-permute-start.2
  128.1 33.0 %feature_backward.1 = (f32[64,192,119]{2,1,0:T(8,128)}, bf16[64,192,119]{2,1,0:T(8,128)(2,1)}, f32[576,192]{1,0:T(8,128)}, f32[192,192]{1,0:T(8,128)}, f32[2,192,128]{2,1,0:T(8,128)}) custom-call(bf16[64,192,119]{2,1,0:T(8,128)(2,1)} %bitcast.21, bf16[64,208,128]{2,1,0:T(8,128)(2,1)} %get-tuple-element.82.n_ref, ...), custom_call_target="tpu_custom_call" | custom-call | flops 263999995904 | bytes 240000000 | tf_op jit(solution)/shard_map/feature_backward/pallas_call | solution.py:759
  161.0 0.0 collective-permute-done.refs_1_
  161.1 0.0 collective-permute-done.1.refs_2_
  161.1 0.0 collective-permute-done.2.refs_3_
  161.1 0.0 all-to-all-done.1.slot_ref
  161.1 6.1 %slots_backward.1 = (f32[64,192,119]{2,1,0:T(8,128)}, bf16[320,128]{1,0:T(8,128)(2,1)}, bf16[320,128]{1,0:T(8,128)(2,1)}, bf16[320,128]{1,0:T(8,128)(2,1)}, bf16[320,128]{1,0:T(8,128)(2,1)}) custom-call(s32[1]{0:T(128)} %bitcast.5.table_ref.refs_0_, bf16[64,192,119]{2,1,0:T(8,128)(2,1)} %bitcast.22, ...), custom_call_target="tpu_custom_call", output_to_operand_aliasing={{0}: (8, {})} | custom-call | flops 8800000000 | bytes 8000000 | tf_op jit(solution)/shard_map/slots_backward/pallas_call | solution.py:813
  167.1 0.3 collective-permute-start.3
  167.5 1.6 collective-permute-start.4
  169.0 0.0 collective-permute-start.5
  169.0 0.0 collective-permute-done.3.refs_5_
  169.0 0.0 copy-start.5
  169.1 3.2 %collective-permute-done.4.refs_6_ = bf16[320,128]{1,0:T(8,128)(2,1)S(1)} collective-permute-done((bf16[320,128]{1,0:T(8,128)(2,1)}, bf16[320,128]{1,0:T(8,128)(2,1)S(1)}, u32[]{:S(2)}, u32[]{:S(2)}) %collective-permute-start.4) | collective-permute-done | bytes 81952 | tf_op jit(solution)/shard_map/ppermute | solution.py:836
  172.2 0.0 copy-start.6
  172.2 1.7 collective-permute-done.5.refs_7_
  174.0 0.0 copy-start.7
  174.0 0.0 copy-done.5
  174.0 0.0 copy-done.6
  174.0 0.6 copy-done.7
  174.6 2.2 join_tables.1
  176.8 16.6 %all_to_all.20.parts_ref = bf16[8,152,128]{2,1,0:T(8,128)(2,1)} all-to-all(bf16[8,152,128]{2,1,0:T(8,128)(2,1)} %join_tables.1), channel_id=1, replica_groups=mesh['table'=4,'rows'=8] {'rows'}, dimensions={0} | all-to-all | bytes 622592 | tf_op jit(solution)/shard_map/all_to_all | solution.py:874
  193.4 1.7 sum_rows.1
  195.1 13.5 %all_to_all.21.refs_1_ = bf16[8,152,128]{2,1,0:T(8,128)(2,1)S(1)} all-to-all(bf16[8,152,128]{2,1,0:T(8,128)(2,1)} %sum_rows.1), channel_id=1, replica_groups=mesh['table'=4,'rows'=8] {'rows'}, dimensions={0} | all-to-all | bytes 622592 | tf_op jit(solution)/shard_map/all_to_all | solution.py:887
  208.6 0.0 copy-start.1
  208.7 1.3 collective-permute-start.7
  210.0 0.0 collective-permute-start.6
  210.0 5.6 %collective-permute-done.7.refs_3_ = bf16[8,152,128]{2,1,0:T(8,128)(2,1)S(1)} collective-permute-done((bf16[8,152,128]{2,1,0:T(8,128)(2,1)S(1)}, bf16[8,152,128]{2,1,0:T(8,128)(2,1)S(1)}, u32[]{:S(2)}, u32[]{:S(2)}) %collective-permute-start.7) | collective-permute-done | bytes 311328 | tf_op jit(solution)/shard_map/ppermute | solution.py:890
  215.6 0.0 copy-start.2
  215.6 0.0 collective-permute-start.8
  215.6 0.0 collective-permute-done.6.refs_2_
  215.6 0.0 copy-start.3
  215.6 1.6 collective-permute-done.8.refs_4_
  217.2 0.0 copy-done.1
  217.2 0.0 copy-done.2
  217.2 0.0 copy-done.3
  217.2 0.0 copy-start.4
  217.2 0.7 copy-done.4
  217.9 7.3 %optimizer.1 = (f32[6,192,192]{2,1,0:T(8,128)}, f32[2,192,192]{2,1,0:T(8,128)}, f32[192,768]{1,0:T(8,128)}, f32[192,768]{1,0:T(8,128)}, f32[6,192]{1,0:T(8,128)}...) custom-call(s32[1]{0:T(128)} %bitcast.5.table_ref.refs_0_, ...), custom_call_target="tpu_custom_call" | custom-call | flops 8800000000 | bytes 8000000 | tf_op jit(solution)/shard_map/optimizer/pallas_call | solution.py:1005
Async XLA Ops:
  8.3 42.1 %all-to-all-start = ((bf16[8,2,120,384]{3,2,1,0:T(8,128)(2,1)}), bf16[8,2,120,384]{3,2,1,0:T(8,128)(2,1)S(1)}, u32[]{:S(2)}, u32[]{:S(2)}) async-start(bf16[8,2,120,384]{3,2,1,0:T(8,128)(2,1)} %slot_rows.1), calls=%async_computation | async-start | bytes 2949120 | tf_op jit(solution)/shard_map/all_to_all | solution.py:1037
  50.5 1.1 copy-start
  121.6 39.5 %all-to-all-start.1 = ((bf16[8,2,120,384]{3,2,1,0:T(8,128)(2,1)}), bf16[8,2,120,384]{3,2,1,0:T(8,128)(2,1)}, u32[]{:S(2)}, u32[]{:S(2)}) async-start(bf16[8,2,120,384]{3,2,1,0:T(8,128)(2,1)} %bitcast.23), calls=%async_computation.1 | async-start | bytes 2949120 | tf_op jit(solution)/shard_map/all_to_all | solution.py:1043
  126.1 34.9 %collective-permute-start = (bf16[896,128]{1,0:T(8,128)(2,1)}, bf16[896,128]{1,0:T(8,128)(2,1)}, u32[]{:S(2)}, u32[]{:S(2)}) collective-permute-start(bf16[896,128]{1,0:T(8,128)(2,1)} %get-tuple-element.108), channel_id=1, source_target_pairs={{0,8},{8,0},{16,24},{24,16},{1,9},{9,1},{17,25},{25,17},{2,10},{10... | collective-permute-start | bytes 688136 | tf_op jit(solution)/shard_map/ppermute | solution.py:836
  126.2 34.9 %collective-permute-start.1 = (bf16[896,128]{1,0:T(8,128)(2,1)}, bf16[896,128]{1,0:T(8,128)(2,1)}, u32[]{:S(2)}, u32[]{:S(2)}) collective-permute-start(bf16[896,128]{1,0:T(8,128)(2,1)} %get-tuple-element.109), channel_id=1, source_target_pairs={{0,16},{8,24},{16,0},{24,8},{1,17},{9,25},{17,1},{25,9},{2,18},{10... | collective-permute-start | bytes 688136 | tf_op jit(solution)/shard_map/ppermute | solution.py:836
  127.8 33.3 %collective-permute-start.2 = (bf16[896,128]{1,0:T(8,128)(2,1)}, bf16[896,128]{1,0:T(8,128)(2,1)}, u32[]{:S(2)}, u32[]{:S(2)}) collective-permute-start(bf16[896,128]{1,0:T(8,128)(2,1)} %get-tuple-element.110), channel_id=1, source_target_pairs={{0,24},{8,16},{16,8},{24,0},{1,25},{9,17},{17,9},{25,1},{2,26},{10... | collective-permute-start | bytes 688136 | tf_op jit(solution)/shard_map/ppermute | solution.py:836
  167.1 1.9 collective-permute-start.3
  167.5 4.7 %collective-permute-start.4 = (bf16[320,128]{1,0:T(8,128)(2,1)}, bf16[320,128]{1,0:T(8,128)(2,1)S(1)}, u32[]{:S(2)}, u32[]{:S(2)}) collective-permute-start(bf16[320,128]{1,0:T(8,128)(2,1)} %get-tuple-element.124), channel_id=1, source_target_pairs={{0,16},{8,24},{16,0},{24,8},{1,17},{9,25},{17,1},{25,9},{2,18},{10... | collective-permute-start | bytes 245768 | tf_op jit(solution)/shard_map/ppermute | solution.py:836
  169.0 4.9 %collective-permute-start.5 = (bf16[320,128]{1,0:T(8,128)(2,1)}, bf16[320,128]{1,0:T(8,128)(2,1)S(1)}, u32[]{:S(2)}, u32[]{:S(2)}) collective-permute-start(bf16[320,128]{1,0:T(8,128)(2,1)} %get-tuple-element.125), channel_id=1, source_target_pairs={{0,24},{8,16},{16,8},{24,0},{1,25},{9,17},{17,9},{25,1},{2,26},{10... | collective-permute-start | bytes 245768 | tf_op jit(solution)/shard_map/ppermute | solution.py:836
  169.0 4.9 %copy-start.5 = (bf16[320,128]{1,0:T(8,128)(2,1)}, bf16[320,128]{1,0:T(8,128)(2,1)S(1)}, u32[]{:S(2)}) copy-start(bf16[320,128]{1,0:T(8,128)(2,1)S(1)} %collective-permute-done.3.refs_5_) | copy-start | bytes 245764
  172.2 1.7 copy-start.6
  174.0 0.6 copy-start.7
  208.6 8.5 %copy-start.1 = (bf16[8,152,128]{2,1,0:T(8,128)(2,1)}, bf16[8,152,128]{2,1,0:T(8,128)(2,1)S(1)}, u32[]{:S(2)}) copy-start(bf16[8,152,128]{2,1,0:T(8,128)(2,1)S(1)} %all_to_all.21.refs_1_) | copy-start | bytes 933892
  208.7 6.9 %collective-permute-start.7 = (bf16[8,152,128]{2,1,0:T(8,128)(2,1)S(1)}, bf16[8,152,128]{2,1,0:T(8,128)(2,1)S(1)}, u32[]{:S(2)}, u32[]{:S(2)}) collective-permute-start(bf16[8,152,128]{2,1,0:T(8,128)(2,1)S(1)} %all_to_all.21.refs_1_), channel_id=1, source_target_pairs={{0,16},{8,24},{16,0},{24,8},{1,17},{9,25},{17,1},{25,9},{2,18},{10... | collective-permute-start | bytes 933896 | tf_op jit(solution)/shard_map/ppermute | solution.py:890
  210.0 5.6 %collective-permute-start.6 = (bf16[8,152,128]{2,1,0:T(8,128)(2,1)S(1)}, bf16[8,152,128]{2,1,0:T(8,128)(2,1)S(1)}, u32[]{:S(2)}, u32[]{:S(2)}) collective-permute-start(bf16[8,152,128]{2,1,0:T(8,128)(2,1)S(1)} %all_to_all.21.refs_1_), channel_id=1, source_target_pairs={{0,8},{8,0},{16,24},{24,16},{1,9},{9,1},{17,25},{25,17},{2,10},{10... | collective-permute-start | bytes 933896 | tf_op jit(solution)/shard_map/ppermute | solution.py:891
  215.6 1.6 copy-start.2
  215.6 1.6 collective-permute-start.8
  215.6 1.6 copy-start.3
  217.2 0.7 copy-start.4

commit v2 on v1

--- a/solution.py
+++ b/solution.py
@@ -128,7 +128,7 @@
     return a, a.T
 
 
-def first_weights_kernel(proj, outw, norms, wqkvT, woT, vec, nrow):
+def first_weights(proj, outw, norms, wqkvT, woT, vec, nrow):
     for i in range(3):
         wqkvT[i * D : (i + 1) * D, :] = padded_square(proj[i])[1][0:D]
     woT[...] = padded_square(outw[0])[1][0:D]
@@ -136,24 +136,6 @@
     nrow[0:6, 0:D] = norms[...]
     for i in range(6):
         vec[i] = jnp.broadcast_to(nrow[i : i + 1, :], (128, DP)).T[0:D]
-
-
-def first_weights(proj, outw, norms):
-    return pl.pallas_call(
-        first_weights_kernel,
-        grid=(1,),
-        in_specs=[
-            pl.BlockSpec((3, D, D), lambda i: (0, 0, 0)),
-            pl.BlockSpec((1, D, D), lambda i: (0, 0, 0)),
-            whole(norms),
-        ],
-        out_specs=[whole(shape(a)) for a in ((3 * D, DP), (D, DP), (6, D, 128))],
-        out_shape=[shape((3 * D, DP)), shape((D, DP)), shape((6, D, 128), F32)],
-        scratch_shapes=[pltpu.VMEM((8, DP), F32)],
-        compiler_params=params(),
-        cost_estimate=cost(2),
-        name="first_weights",
-    )(proj, outw, norms)
 
 
 def weights_kernel(proj, outw, w_in, w_outT, wqkvI, wo, wkv2, wkv2T, wq2, wq2T, wo2I, wo2, w1T, w1, w2T, w2):
@@ -239,8 +221,11 @@
         yield
 
 
-def slots_kernel(SL, count_ref, mask_ref, order_ref, x_ref, wqkvT_ref, woT_ref, vec_ref, out_ref, xs):
+def slots_kernel(
+    SL, count_ref, mask_ref, order_ref, x_ref, proj_ref, outw_ref, norm_ref, out_ref, wqkvT_ref, woT_ref, vec_ref, xs, nrow
+):
     xs[...] = jnp.zeros_like(xs)
+    first_weights(proj_ref, outw_ref, norm_ref, wqkvT_ref, woT_ref, vec_ref, nrow)
     row = lax.broadcasted_iota(jnp.int32, (FS, 1), 0)
     lane = lax.broadcasted_iota(jnp.int32, (1, 2 * D), 1)
 
@@ -264,22 +249,22 @@
     weave([(pair(c), 0, 1) for c in range(SL // 2)])
 
 
-def slot_rows(shards, count, mask, order, cells, wqkvT, woT, vec):
+def slot_rows(shards, count, mask, order, cells, proj, outw, norms):
     SL = mask.shape[1]
     smem = pl.BlockSpec(memory_space=pltpu.SMEM)
-    sent = shape((shards, SL // 2, FS, 2 * D))
+    part = lambda a, k: pl.BlockSpec((k,) + a.shape[1:], lambda i: (0, 0, 0))
+    outs = [shape((shards, SL // 2, FS, 2 * D)), shape((3 * D, DP)), shape((D, DP)), shape((6, D, 128), F32)]
     return pl.pallas_call(
         functools.partial(slots_kernel, SL),
         grid=(1,),
-        in_specs=[smem, smem, smem, pl.BlockSpec((SL, D, F), lambda i: (0, 0, 0))]
-        + [whole(a) for a in (wqkvT, woT, vec)],
-        out_specs=whole(sent),
-        out_shape=sent,
-        scratch_shapes=[pltpu.VMEM((SL // 2, DP, 2 * FP), BF)],
+        in_specs=[smem, smem, smem, part(cells, SL), part(proj, 3), part(outw, 1), whole(norms)],
+        out_specs=[whole(a) for a in outs],
+        out_shape=outs,
+        scratch_shapes=[pltpu.VMEM((SL // 2, DP, 2 * FP), BF), pltpu.VMEM((8, DP), F32)],
         compiler_params=params(),
-        cost_estimate=cost(5),
+        cost_estimate=cost(6),
         name="slot_rows",
-    )(count, mask, order, cells, wqkvT, woT, vec)
+    )(count, mask, order, cells, proj, outw, norms)
 
 
 def turn_block(perm_ref, block, R):
@@ -287,7 +272,7 @@
 
 
 def forward_kernel(
-    R, OFF, x_ref, c_ref, wqkvT_ref, woT_ref, vec_ref, perm_ref, ht_ref, ct_ref, n_ref, qkv_ref, p_ref, l_ref, of_ref, xs, hs, cp, cs
+    R, OFF, x_ref, c_ref, wqkvT_ref, woT_ref, vec_ref, perm_ref, wq_ref, ht_ref, ct_ref, qt_ref, n_ref, qkv_ref, p_ref, l_ref, of_ref, xs, hs, cp, cs
 ):
     @pl.when(pl.program_id(0) == 0)
     def _():
@@ -331,7 +316,10 @@
 
     weave([(pair(c), c * OFF, 1) for c in range(R // 2)] + [(cotangents(), 4, 1)])
     for j in range(FP // 16):
-        ht_ref[16 * j : 16 * j + 16] = turn_block(perm_ref, hs[:, 16 * j : 16 * j + 16, :], R)
+        block = turn_block(perm_ref, hs[:, 16 * j : 16 * j + 16, :], R)
+        ht_ref[16 * j : 16 * j + 16] = block
+        q = (mm(block.reshape(16 * R, DP), wq_ref[...]) * SCALE2).astype(BF)
+        qt_ref[16 * j : 16 * j + 16] = q.reshape(16, R, DP)
 
 
 def feature_forward(cells, cot, ws, R=16, OFF=2):
@@ -344,8 +332,8 @@
         functools.partial(forward_kernel, R, OFF),
         grid=(rows // R,),
         in_specs=[nat(D, F), nat(D, F)] + [whole(a) for a in ws],
-        out_specs=[turned, turned] + [nat(*a) for a in sizes],
-        out_shape=[shape((FP, rows, DP))] * 2 + [shape((rows,) + a, t) for a, t in zip(sizes, kinds)],
+        out_specs=[turned] * 3 + [nat(*a) for a in sizes],
+        out_shape=[shape((FP, rows, DP))] * 3 + [shape((rows,) + a, t) for a, t in zip(sizes, kinds)],
         scratch_shapes=[
             pltpu.VMEM((R // 2, DP, 2 * FP), BF),
             pltpu.VMEM((R, FP, DP), BF),
@@ -389,12 +377,12 @@
 
 
 def item_kernel(
-    RW, keys, tables, OFF, WP, CC, WC, table_ref, ht_ref, ct_ref, slot_ref, perm_ref, wq_ref, wqT_ref, woI_ref, wo_ref, w1T_ref, w1_ref, w2T_ref, w2_ref,
+    RW, keys, tables, OFF, AO, AS, WP, CC, WC, table_ref, ht_ref, next_ref, q_ref, qnext_ref, ct_ref, slot_ref, perm_ref, wqT_ref, woI_ref, wo_ref, w1T_ref, w1_ref, w2T_ref, w2_ref,
     wkv_ref, wkvT_ref, vec_ref, y_ref, g1_ref, back_ref, *rest
 ):
     piece_refs, rest = rest[:tables], rest[tables:]
     (dwq, dwo, dw1, dw2, dnp, dwkv, bias_ref, pack_ref, hk_ref, bk_ref,
-     dk_ref, dv_ref, hbTs, ois, hb2Ts, actss, dbTs, duss, dabTs, dqss, slp) = rest
+     dks, dvs, hbTs, ois, hb2Ts, actss, dbTs, duss, dabTs, dqss, pbss, kvss, slp) = rest
     step = pl.program_id(0)
     blocks = [(s, b, min(16, FS - b)) for s in range(0, keys, 16) for b in range(0, FS, 16)]
 
@@ -402,8 +390,10 @@
     def _():
         for ref in (dwq, dwo, dw1, dw2, dnp, dwkv):
             ref[...] = jnp.zeros_like(ref)
-        for ref in (hbTs, ois, hb2Ts, actss, dbTs, duss, dabTs, dqss):
+        for ref in (hb2Ts, actss, dbTs, duss, dabTs, dqss, dks, dvs):
             ref[1] = jnp.zeros_like(ref[1])
+        for ref in (hbTs, ois):
+            ref[2] = jnp.zeros_like(ref[2])
         hk_ref[:, :, D:DP] = jnp.zeros((FS, keys, DP - D), BF)
         for s, b, n in blocks:
             own = slot_ref[s // 2 : s // 2 + 8, b : b + n, :]
@@ -416,43 +406,60 @@
             for i, at in enumerate((0, DP)):
                 bias_ref[s + 8 * i : s + 8 * i + 8] = jnp.where(flag[:, at : at + 128] > 0.5, 0.0, -1e30)
 
-    cur = step % 2
     masks = half_masks()
     LW = 2 * RW
     left = lax.broadcasted_iota(jnp.int32, (1, LW), 1) < RW
     HK = H * keys
-    hbT, oi, hb2T, acts, dbT, dus, dabT, dqs = [r.at[cur] for r in (hbTs, ois, hb2Ts, actss, dbTs, duss, dabTs, dqss)]
-    hk = hk_ref[pl.ds(pl.multiple_of(step * FB, FB), FB)].reshape(FB * keys, DP)
-    kvs = [mm(hk, wkv_ref[...]).astype(BF)]
-
-    def attend(j, out):
-        h = ht_ref[2 * j:2 * j + 2].reshape(LW, DP)
-        q = (mm(h, wq_ref[...]) * SCALE2).astype(BF)
-        yield
-        ks = [spread_halves(kvs[0][(2 * j + c) * keys : (2 * j + c + 1) * keys, 0:DP], masks) for c in range(2)]
-        hbT[:, j * LW:(j + 1) * LW] = h.T[0:D]
+    cur, prev = lax.rem(step, 2), lax.rem(step + 1, 2)
+    cur3, next3, prev3 = [lax.rem(step + i, 3) for i in range(3)]
+    hb2T, acts, dbT, dus, dabT, dqs = [r.at[cur] for r in (hb2Ts, actss, dbTs, duss, dabTs, dqss)]
+
+    def step_rows(at):
+        return hk_ref[pl.ds(pl.multiple_of(at * FB, FB), FB)].reshape(FB * keys, DP)
+
+    def keys_values(at, to):
+        kvss[to] = mm(step_rows(at), wkv_ref[...]).astype(BF)
+
+    def spreads(to, j, first):
+        return [
+            spread_halves(kvss[to, (2 * j + c) * keys : (2 * j + c + 1) * keys, first : first + DP], masks)
+            for c in range(2)
+        ]
+
+    def attend(j, ref, qref, to, to3):
+        h = ref[2 * j : 2 * j + 2].reshape(LW, DP)
+        q = qref[2 * j : 2 * j + 2].reshape(LW, DP)
+        ks = spreads(to, j, 0)
+        hbTs[to3, :, j * LW : (j + 1) * LW] = h.T[0:D]
         yield
         st = jnp.where(left, mm_nt(ks[0], q), mm_nt(ks[1], q))
         yield
-        vs = [spread_halves(kvs[0][(2 * j + c) * keys : (2 * j + c + 1) * keys, DP:], masks) for c in range(2)]
+        vs = spreads(to, j, DP)
         pbs = []
         for hh in range(H):
-            s = st[hh * keys:(hh + 1) * keys] + bias_ref[...]
+            s = st[hh * keys : (hh + 1) * keys] + bias_ref[...]
             e = jnp.exp2(s - jnp.max(s, 0, keepdims=True))
             pbs.append((e * (1.0 / jnp.sum(e, 0, keepdims=True))).astype(BF))
-            if hh % 2: yield
+            if hh % 2:
+                yield
         pb = jnp.concatenate(pbs, 0)
+        pbss[to, j] = pb
         pt = pb.T
         yield
         o = jnp.concatenate([mm(pt[:RW], vs[0]), mm(pt[RW:], vs[1])], 0).astype(BF)
-        oi[j * LW:(j + 1) * LW] = o
-        out.extend([q, pb, ks, vs, o])
-        yield
-    def dense(i, os, out):
+        ois[to3, j * LW : (j + 1) * LW] = o
+        yield
+
+    @pl.when(step == 0)
+    def _():
+        keys_values(0, 0)
+        weave([(attend(j, ht_ref, q_ref, 0, 0), 0, 1) for j in range(FB // 2)])
+
+    def dense(i, out):
         c0 = i * 2 * LW
         g1v, b1v, g2v, b2v = [vec_ref[i] for i in range(2, 6)]
         h = ht_ref[4 * i:4 * i + 4].reshape(2 * LW, DP)
-        o = jnp.concatenate(os, 0)
+        o = ois[cur3, c0 : c0 + 2 * LW]
         aT = mm_nt(woI_ref[...], jnp.concatenate([o, h], 1))
         yield
         n2, rc2, h2, hb2 = [], [], [], []
@@ -515,13 +522,14 @@
         doT = mm(wo_ref[...], tall(dab)).astype(BF)
         out.extend([dab, doT])
         yield
-    def back(j, at, doT, out):
-        q, pb, ks, vs, _ = at
+    def back(j, doT, out):
+        q, pb = q_ref[2 * j : 2 * j + 2].reshape(LW, DP), pbss[cur, j]
+        ks, vs = spreads(cur, j, 0), spreads(cur, j, DP)
         do = tall(doT)
         don = do.T
         dp = jnp.where(left, mm(vs[0], do), mm(vs[1], do))
         yield
-        slot_sums(dv_ref, j, pb, don, None)
+        slot_sums(dvs, j, pb, don, None)
         yield
         dss = []
         for hh in range(H):
@@ -532,7 +540,7 @@
         ds = jnp.concatenate(dss, 0)
         dst = ds.T
         yield
-        slot_sums(dk_ref, j, ds, q, 0.6931471805599453)
+        slot_sums(dks, j, ds, q, 0.6931471805599453)
         yield
         dq = jnp.concatenate([mm(dst[:RW], ks[0]), mm(dst[RW:], ks[1])], 0) * SCALE
         dq = dq.astype(BF)
@@ -555,45 +563,52 @@
                 out[c].append(v)
         for c in range(2):
             v = jnp.concatenate(out[c], 1)
-            ref[2 * j + c] = (v if scale is None else v * scale).astype(BF)
+            ref[cur, 2 * j + c] = (v if scale is None else v * scale).astype(BF)
     def finish(i, dqv, dab):
         dq = jnp.concatenate(dqv, 0)
         g1 = mm(dq, wqT_ref[...]) + tall(dab).T.astype(F32)
         g1_ref[4 * i:4 * i + 4] = g1.astype(BF).reshape(4, RW, DP)
         yield
     def chunk(i):
-        at = [[], []]
-        ga, gb = attend(2 * i, at[0]), attend(2 * i + 1, at[1])
-        for _ in zip(ga, gb): yield
-        for _ in ga: yield
-        for _ in gb: yield
         out = []
-        yield from dense(i, [at[0][4], at[1][4]], out)
+        yield from dense(i, out)
         dab, doT = out
         dq = []
         for t in range(2):
-            yield from back(2 * i + t, at[t], doT[:, t * LW:(t + 1) * LW], dq)
+            yield from back(2 * i + t, doT[:, t * LW : (t + 1) * LW], dq)
         yield from finish(i, dq, dab)
-    def wgrad(b):
-        dwq[...] += mm(hbTs[b], dqss[b])
-        yield
-        dwo[...] += mm(dabTs[b], ois[b])
+
+    def wgrad(at, b, b3):
+        dwq[...] += mm(hbTs[b3], dqss[b])
+        yield
+        dwo[...] += mm(dabTs[b], ois[b3])
         yield
         for c in range(0, FF, WC):
-            dw1[c:c + WC] += mm_nt(duss[b, c:c + WC], hb2Ts[b])
+            dw1[c : c + WC] += mm_nt(duss[b, c : c + WC], hb2Ts[b])
             yield
         for c in range(0, FF, WC):
-            dw2[c:c + WC] += mm_nt(actss[b, c:c + WC], dbTs[b])
-            yield
+            dw2[c : c + WC] += mm_nt(actss[b, c : c + WC], dbTs[b])
+            yield
+        dkv = jnp.concatenate([r[b].reshape(FB * keys, DP) for r in (dks, dvs)], 1)
+        dwkv[...] += mm_tn(step_rows(at), dkv)
+        yield
+        back_rows = mm(dkv, wkvT_ref[...]).astype(BF).reshape(FB, keys, DP)
+        bk_ref[pl.ds(pl.multiple_of(at * FB, FB), FB)] = back_rows
+        yield
+
+    def ahead():
+        keys_values(jnp.minimum(step + 1, pl.num_programs(0) - 1), prev)
+        yield
+
     NC = FB // 4
-    weave([(chunk(i), i * OFF, 1) for i in range(NC)] + [(wgrad(1 - cur), WP, 1)])
-    dkv = jnp.concatenate([r[...].reshape(FB * keys, DP) for r in (dk_ref, dv_ref)], 1)
-    dwkv[...] += mm_tn(hk, dkv)
-    bk_ref[pl.ds(pl.multiple_of(step * FB, FB), FB)] = mm(dkv, wkvT_ref[...]).astype(BF).reshape(FB, keys, DP)
+    streams = [(ahead(), 0, 1)] + [(chunk(i), i * OFF, 1) for i in range(NC)]
+    streams += [(attend(j, next_ref, qnext_ref, prev, next3), AO + j * AS, 1) for j in range(FB // 2)]
+    streams += [(wgrad(jnp.maximum(step - 1, 0), prev, prev3), WP, 1)]
+    weave(streams)
 
     @pl.when(step == pl.num_programs(0) - 1)
     def _():
-        for _ in wgrad(cur):
+        for _ in wgrad(step, cur, cur3):
             pass
         for s, b, n in blocks:
             own = bk_ref[b : b + n, s : s + 16, :]
@@ -603,7 +618,7 @@
             back_ref[s // 2 : s // 2 + 8, b : b + n, :] = jnp.concatenate([own[0:8], own[8:16]], 2)
         at = 0
         for ref in (dw1, dw2):
-            t = ref[...].T
+            t = ref[...].astype(BF).T.astype(F32)
             for j in range(FF // 128):
                 pack_ref[at : at + D] = t[:, 128 * j : 128 * j + 128]
                 at += D
@@ -613,30 +628,31 @@
         hand_out(table_ref, pack_ref, piece_refs)
 
 
-def item_and_dense(table, ht, ct, slots, perm, ws, vec, packed, tables, OFF=0, WP=20, CC=384, WC=384):
+def item_and_dense(table, ht, qt, ct, slots, perm, ws, vec, packed, tables, OFF=0, AO=2, AS=6, WP=4, CC=384, WC=192):
     RW = ht.shape[1]
     keys = 2 * slots.shape[0]
     M = FB * RW
     cells = pl.BlockSpec((FB, RW, DP), lambda i: (i, 0, 0))
     accs = [(D, DP), (D, DP), (FF, D), (FF, D), (4, D, 128), (DP, 2 * DP), (keys, 128), (packed, 128)]
-    kept = [(D, M), (M, DP), (D, M), (FF, M), (D, M), (FF, M), (D, M), (M, DP)]
+    kept = [(3, D, M), (3, M, DP)] + [(2,) + a for a in ((D, M), (FF, M), (D, M), (FF, M), (D, M), (M, DP))]
+    kept += [(2, FB // 2, H * keys, 2 * RW), (2, FB * keys, 2 * DP), (FF, M)]
+    ahead = pl.BlockSpec((FB, RW, DP), lambda i: (jnp.minimum(i + 1, FS // FB - 1), 0, 0))
     flat = [slots, perm, *ws, vec]
     outs = [shape((FS, RW, DP))] * 2 + [shape(slots.shape)] + [shape((packed // tables, 128))] * tables
     return pl.pallas_call(
-        functools.partial(item_kernel, RW, keys, tables, OFF, WP, CC, WC),
+        functools.partial(item_kernel, RW, keys, tables, OFF, AO, AS, WP, CC, WC),
         grid=(FS // FB,),
-        in_specs=[pl.BlockSpec(memory_space=pltpu.SMEM), cells, cells] + [whole(a) for a in flat],
+        in_specs=[pl.BlockSpec(memory_space=pltpu.SMEM), cells, ahead, cells, ahead, cells] + [whole(a) for a in flat],
         out_specs=[cells, cells] + [whole(a) for a in outs[2:]],
         out_shape=outs,
         scratch_shapes=[pltpu.VMEM(a, F32) for a in accs]
         + [pltpu.VMEM((FS, keys, DP), BF)] * 2
-        + [pltpu.VMEM((FB, keys, DP), BF)] * 2
-        + [pltpu.VMEM((2,) + a, BF) for a in kept]
-        + [pltpu.VMEM((FF, M), BF)],
+        + [pltpu.VMEM((2, FB, keys, DP), BF)] * 2
+        + [pltpu.VMEM(a, BF) for a in kept],
         compiler_params=params(),
         cost_estimate=cost(66),
         name="item_and_dense",
-    )(table, ht, ct, *flat)
+    )(table, ht, ht, qt, qt, ct, *flat)
 
 
 def backward_rows(
@@ -706,7 +722,7 @@
 
 
 def backward_kernel(
-    R, OFF, x_ref, n_ref, qkv_ref, p_ref, l_ref, of_ref, g1t_ref, yt_ref, wqkvI_ref, wo_ref, vec_ref, perm_ref,
+    R, OFF, YO, x_ref, n_ref, qkv_ref, p_ref, l_ref, of_ref, g1t_ref, yt_ref, wqkvI_ref, wo_ref, vec_ref, perm_ref,
     cg_ref, y_ref, dqkv, dwo, dnp, gs, ys, xs, os, dqs, das,
 ):
     @pl.when(pl.program_id(0) == 0)
@@ -739,17 +755,14 @@
         x_ref, n_ref, qkv_ref, p_ref, l_ref, of_ref, wqkvI_ref, wo_ref, vec_ref, cg_ref, xs, os, dqs, das, dqkv, dwo, dnp,
         lambda r: gs[r].T[0:D].astype(F32),
     )
-    Q = R // 4
-    M = R * FP // 2
-    for half in range(2):
-        streams = [(pair(c), (c - half * Q) * OFF, 1) for c in range(half * Q, (half + 1) * Q)]
-        streams.append((sums(slice(0, M)) if half else outputs(), 3, 1))
-        weave(streams)
-    for _ in sums(slice(M, 2 * M)):
+    streams = [(pair(c), c * OFF, 1) for c in range(R // 2)]
+    streams.append((outputs(), YO, 1))
+    weave(streams)
+    for _ in sums(slice(0, R * FP)):
         pass
 
 
-def feature_backward(x, saved, g1t, yt, wqkvI, wo, vec, perm, R=16, OFF=1):
+def feature_backward(x, saved, g1t, yt, wqkvI, wo, vec, perm, R=16, OFF=2, YO=3):
     rows = x.shape[0]
     nat = lambda a: pl.BlockSpec((R,) + a.shape[1:], lambda i: (i, 0, 0))
     turned = pl.BlockSpec((FS, R, DP), lambda i: (0, i, 0))
@@ -757,7 +770,7 @@
     shared = [wqkvI, wo, vec, perm]
     M = R * FP
     return pl.pallas_call(
-        functools.partial(backward_kernel, R, OFF),
+        functools.partial(backward_kernel, R, OFF, YO),
         grid=(rows // R,),
         in_specs=[nat(x)] + [nat(a) for a in saved] + [turned] * 2 + [whole(a) for a in shared],
         out_specs=[nat(x), nat(x)] + [whole(a) for a in accs],
@@ -927,8 +940,15 @@
 
 def optimizer_steps(
     proj_ref, outw_ref, in_ref, hid_ref, norm_ref, sr_ref, sc_ref, mm_ref, mh_ref, ns_ref,
-    proj_g, out_g, in_g, hid_g, norm_g, proj_n, out_n, in_n, hid_n, norm_n, sr_n, sc_n, mm_n, mh_n, ns_n, mid_ref, tail_ref,
+    proj_gx, out_gx, in_gx, hid_gx, norm_g, proj_nx, out_nx, in_nx, hid_nx, norm_n, sr_n, sc_n, mm_n, mh_n, ns_n,
+    proj_g, out_g, in_g, hid_g, proj_n, out_n, in_n, hid_n, sems, mid_ref, tail_ref,
 ):
+    copies = []
+
+    def send(a, b):
+        copies.append(pltpu.make_async_copy(a, b, sems.at[len(copies)]))
+        copies[-1].start()
+
     decay = 1.0 - STEP ** (-0.8)
 
     def stats(grad, col_old, row_old):
@@ -953,27 +973,33 @@
     wk2, wv2 = square_pair(mid_ref, 12 * D + PAIR)
     for i, grad in enumerate((wq, wk, wv, wq2, wk2, wv2, wo, wo2)):
         g_ref, n_ref, w_ref, j = (proj_g, proj_n, proj_ref, i) if i < 6 else (out_g, out_n, outw_ref, i - 6)
+        gx, nx = (proj_gx, proj_nx) if i < 6 else (out_gx, out_nx)
         g_ref[j] = grad
+        send(g_ref.at[j], gx.at[j])
         col, row = stats(grad, to_col(sr_ref[i : i + 1, :]), sc_ref[i : i + 1, :])
         sr_n[i : i + 1, :] = to_row(col)
         sc_n[i : i + 1, :] = row
         mean = jnp.sum(col, 0, keepdims=True) * (1.0 / D)
         w = w_ref[j]
         n_ref[j] = w - clipped(scaled(grad, col, row, mean), w, D * D)
+        send(n_ref.at[j], nx.at[j])
 
     def wide(at):
         return jnp.concatenate([mid_ref[at + D * j : at + D * j + D].astype(F32) for j in range(6)], 1)
 
     grad = wide(0)
     in_g[...] = grad
+    send(in_g, in_gx)
     col, row = stats(grad, to_col(mm_ref[0:1, :]), mh_ref[0:1, :])
     mm_n[0:1, :] = to_row(col)
     mh_n[0:1, :] = row
     mean = jnp.sum(col, 0, keepdims=True) * (1.0 / D)
     w = in_ref[...]
     in_n[...] = w - clipped(scaled(grad, col, row, mean), w, D * FF)
+    send(in_n, in_nx)
     grad = wide(6 * D)
     hid_g[...] = grad
+    send(hid_g, hid_gx)
     col, row = stats(grad, to_col(mm_ref[1:2, :]), mh_ref[1:2, :])
     mm_n[1:2, :] = to_row(col)
     mh_n[1:2, :] = row
@@ -981,6 +1007,7 @@
     w = hid_ref[...]
     update = grad * lax.rsqrt(col) * lax.rsqrt(row * (1.0 / mean))
     hid_n[...] = w - clipped(update, w, D * FF)
+    send(hid_n, hid_nx)
 
     pieces = []
     for ref, at, count in ((tail_ref, 2 * PAIR, 2), (mid_ref, 12 * D + 2 * PAIR, 4)):
@@ -996,22 +1023,29 @@
     w = norm_ref[...]
     w_rms = jnp.sqrt(jnp.sum(w * w, 1, keepdims=True) * (1.0 / D))
     norm_n[...] = w - update * (RATE * jnp.maximum(0.001, w_rms) / jnp.maximum(1.0, rms / CLIP))
+    for copy in copies:
+        copy.wait()
 
 
 def optimizer(table, pieces, mid_rows, *state):
     proj, outw, w_in, w_outT, norms, sr, sc, ms, hs, ns = state
     shards, rows, _ = pieces[0].shape
     order = [proj, outw, w_in, w_outT, norms, proj, outw, w_in, w_outT, norms, sr, sc, ms, hs, ns]
+    big = (0, 1, 2, 3, 5, 6, 7, 8)
     outs = pl.pallas_call(
         functools.partial(optimizer_kernel, len(pieces), mid_rows),
         in_specs=[pl.BlockSpec(memory_space=pltpu.SMEM)] + [whole(a) for a in (*pieces, *state)],
+        out_specs=[pl.BlockSpec(memory_space=pl.ANY) if i in big else whole(a) for i, a in enumerate(order)],
         out_shape=[shape(a.shape, F32) for a in order],
-        scratch_shapes=[
+        scratch_shapes=[pltpu.VMEM(order[i].shape, F32) for i in big]
+        + [
+            pltpu.SemaphoreType.DMA((20,)),
             pltpu.VMEM((len(pieces) * shards * mid_rows, 128), F32),
             pltpu.VMEM((len(pieces) * shards * (rows - mid_rows), 128), F32),
         ],
         compiler_params=params(),
-        cost_estimate=cost(8), name="optimizer",
+        cost_estimate=cost(8),
+        name="optimizer",
     )(table, *pieces, *state)
     outs = list(outs)
     for i in (3, 8):
@@ -1032,14 +1066,13 @@
     perm = perm_matrix()
     shards, tables = lax.axis_size("rows"), lax.axis_size("table")
     table = lax.axis_index("table").astype(jnp.int32).reshape(1)
-    wqkvT, woT, vec = first_weights(proj, outw, norms)
-    own = slot_rows(shards, train_count, key_mask, train_order, x, wqkvT, woT, vec)
+    own, wqkvT, woT, vec = slot_rows(shards, train_count, key_mask, train_order, x, proj, outw, norms)
     slots = lax.all_to_all(own, "rows", 0, 0).reshape((-1,) + own.shape[2:])
     w_in, _ = lax.optimization_barrier((w_in, own))
     wqkvI, wo, *ws = other_weights(proj, outw, w_in, w_outT)
-    ht, ct, *saved = feature_forward(x, cot, (wqkvT, woT, vec, perm))
-    wkv2, wkv2T, *ws = ws
-    yt, g1t, back, *mids = item_and_dense(table, ht, ct, slots, perm, (*ws, wkv2, wkv2T), vec, mid_rows, tables)
+    wkv2, wkv2T, wq2, *ws = ws
+    ht, ct, qt, *saved = feature_forward(x, cot, (wqkvT, woT, vec, perm, wq2))
+    yt, g1t, back, *mids = item_and_dense(table, ht, qt, ct, slots, perm, (*ws, wkv2, wkv2T), vec, mid_rows, tables)
     back = lax.all_to_all(back.reshape(own.shape), "rows", 0, 0)
     mids = table_sums(tables, mids)
     cg, y, *accs = feature_backward(x, saved, g1t, yt, wqkvI, wo, vec, perm)

time: 226 us -> 215 us (0.951)
  Pallas kernels: 156 us -> 147 us
    pallas_call x3 -> x2, Pallas kernels: 105 us -> 93.5 us  [the longest x1 63.2 us: item_and_dense(): pl.pallas_call(functools.partial(item_kernel, RW, keys, tables, OFF, AO,...]
  transfers between devices with their start and end apart: 11 -> 11, of which waited for: 5 -> 6; matrix products, arithmetic and copies ran while one was open for 0% -> 0% of each run, Pallas kernels for 27% -> 28%
where the time goes in v2:
time: 215 us
  Pallas kernels  147 us (68%)
  blocking collectives  28.8 us (13%)
  waiting for transfers between devices  18.1 us (8%)
  starting transfers between devices  17.1 us (8%)
  local copies, waits for them, and re-layouts  2.47 us (1%)
    pallas_call x1, Pallas kernels, item_and_dense(): pl.pallas_call(functools.partial(item_kernel, RW, keys, tables, OFF, AO,...  63.2 us
    pallas_call x1, Pallas kernels, feature_backward(): pl.pallas_call(functools.partial(backward_kernel, R, OFF, YO), grid=(rows...  30.4 us
    pallas_call x1, Pallas kernels, feature_forward(): pl.pallas_call(functools.partial(forward_kernel, R, OFF), grid=(rows // R...  27.1 us
    all_to_all x1, blocking collectives, sum_rows(): parts = lax.all_to_all(parts, 'rows', 0, 0)  15.2 us
    all_to_all x1, blocking collectives, gather_all(): own = lax.all_to_all(copies, 'rows', 0, 0)  13.6 us
    pallas_call x1, Pallas kernels, optimizer(): pl.pallas_call(functools.partial(optimizer_kernel, len(pieces), mid_rows)...  7.97 us
    all_to_all x1, starting transfers between devices, on_device(): slots = lax.all_to_all(own, 'rows', 0, 0).reshape((-1,) + own.shape[2:])  7.26 us
    pallas_call x1, Pallas kernels, slots_backward(): pl.pallas_call(functools.partial(slots_back_kernel, SL, tables), grid=(1,...  6.04 us
  transfers between devices with their start and end apart: 11, of which 6 were waited for; matrix products, arithmetic and copies ran while one was open for 0% of the time, Pallas kernels for 28%

profile of v2, /device:TPU:0, one launch (start us, length us, event | category | flops | bytes accessed | tf_op | source)
XLA Modules:
  0.0 214.7 jit_solution(9900198882809515341)
XLA Ops:
  1.3 4.6 %slot_rows.1 = (bf16[8,2,120,384]{3,2,1,0:T(8,128)(2,1)}, bf16[576,256]{1,0:T(8,128)(2,1)}, bf16[192,256]{1,0:T(8,128)(2,1)}, f32[6,192,128]{2,1,0:T(8,128)}) custom-call(s32[1]{0:T(128)S(6)} %copy.35.count_ref, s32[1,4]{1,0:T(1,128)} %mask_ref.1, s32[1,4]{1,0:T(1,128)} %order_ref.1, bf16[64,192,119]{2,1,0:T(8,128)(2,1)} %bitcast.19, ...), custom_call_target="tpu_custom_call" | custom-call | flops 6600000000 | bytes 6000000 | tf_op jit(solution)/shard_map/slot_rows/pallas_call | solution.py:257
  5.9 7.3 %all-to-all-start = ((bf16[8,2,120,384]{3,2,1,0:T(8,128)(2,1)}), bf16[8,2,120,384]{3,2,1,0:T(8,128)(2,1)S(1)}, u32[]{:S(2)}, u32[]{:S(2)}) async-start(bf16[8,2,120,384]{3,2,1,0:T(8,128)(2,1)} %get-tuple-element.84), calls=%async_computation | async-start | bytes 2949120 | tf_op jit(solution)/shard_map/all_to_all | solution.py:1070
  13.1 3.4 %other_weights.1 = (bf16[192,768]{1,0:T(8,128)(2,1)}, bf16[192,256]{1,0:T(8,128)(2,1)}, bf16[256,512]{1,0:T(8,128)(2,1)}, bf16[512,256]{1,0:T(8,128)(2,1)}, bf16...) custom-call(f32[6,192,192]{2,1,0:T(8,128)} %refs_5_.1, ...), custom_call_target="tpu_custom_call" | custom-call | flops 4400000000 | bytes 4000000 | tf_op jit(solution)/shard_map/other_weights/pallas_call | solution.py:170
  16.5 27.1 %feature_forward.1 = (bf16[128,64,256]{2,1,0:T(8,128)(2,1)}, bf16[128,64,256]{2,1,0:T(8,128)(2,1)}, bf16[128,64,256]{2,1,0:T(8,128)(2,1)}, bf16[64,208,128]{2,1,...) custom-call(bf16[64,192,119]{2,1,0:T(8,128)(2,1)} %bitcast.20, ...), custom_call_target="tpu_custom_call" | custom-call | flops 39600001024 | bytes 36000000 | tf_op jit(solution)/shard_map/feature_forward/pallas_call | solution.py:331
  43.7 4.4 %all-to-all-done = bf16[8,2,120,384]{3,2,1,0:T(8,128)(2,1)S(1)} async-done(((bf16[8,2,120,384]{3,2,1,0:T(8,128)(2,1)}), bf16[8,2,120,384]{3,2,1,0:T(8,128)(2,1)S(1)}, u32[]{:S(2)}, u32[]{:S(2)}) %all-to-all-start) | async-done | bytes 1474592 | tf_op jit(solution)/shard_map/all_to_all | solution.py:1070
  48.0 0.0 copy-start
  48.0 1.1 copy-done
  49.1 63.2 %item_and_dense.1 = (bf16[120,64,256]{2,1,0:T(8,128)(2,1)}, bf16[120,64,256]{2,1,0:T(8,128)(2,1)}, bf16[16,120,384]{2,1,0:T(8,128)(2,1)}, bf16[896,128]{1,0:T(8,...) custom-call(s32[1]{0:T(128)} %bitcast.6.table_ref.refs_0_, ...), custom_call_target="tpu_custom_call" | custom-call | flops 72600002560 | bytes 66000000 | tf_op jit(solution)/shard_map/item_and_dense/pallas_call | solution.py:642
  112.3 4.5 %all-to-all-start.1 = ((bf16[8,2,120,384]{3,2,1,0:T(8,128)(2,1)}), bf16[8,2,120,384]{3,2,1,0:T(8,128)(2,1)}, u32[]{:S(2)}, u32[]{:S(2)}) async-start(bf16[8,2,120,384]{3,2,1,0:T(8,128)(2,1)} %bitcast.23), calls=%async_computation.1 | async-start | bytes 2949120 | tf_op jit(solution)/shard_map/all_to_all | solution.py:1076
  116.8 0.1 collective-permute-start
  116.9 1.6 collective-permute-start.1
  118.5 0.3 collective-permute-start.2
  118.8 30.4 %feature_backward.1 = (f32[64,192,119]{2,1,0:T(8,128)}, bf16[64,192,119]{2,1,0:T(8,128)(2,1)}, f32[576,192]{1,0:T(8,128)}, f32[192,192]{1,0:T(8,128)}, f32[2,192,128]{2,1,0:T(8,128)}) custom-call(bf16[64,192,119]{2,1,0:T(8,128)(2,1)} %bitcast.21, bf16[64,208,128]{2,1,0:T(8,128)(2,1)} %get-tuple-element.87.n_ref, ...), custom_call_target="tpu_custom_call" | custom-call | flops 263999995904 | bytes 240000000 | tf_op jit(solution)/shard_map/feature_backward/pallas_call | solution.py:772
  149.2 0.0 collective-permute-done.refs_1_
  149.2 0.0 collective-permute-done.1.refs_2_
  149.2 0.0 collective-permute-done.2.refs_3_
  149.2 2.1 all-to-all-done.1.slot_ref
  151.3 6.0 %slots_backward.1 = (f32[64,192,119]{2,1,0:T(8,128)}, bf16[320,128]{1,0:T(8,128)(2,1)}, bf16[320,128]{1,0:T(8,128)(2,1)}, bf16[320,128]{1,0:T(8,128)(2,1)}, bf16[320,128]{1,0:T(8,128)(2,1)}) custom-call(s32[1]{0:T(128)} %bitcast.6.table_ref.refs_0_, bf16[64,192,119]{2,1,0:T(8,128)(2,1)} %bitcast.22, ...), custom_call_target="tpu_custom_call", output_to_operand_aliasing={{0}: (8, {})} | custom-call | flops 8800000000 | bytes 8000000 | tf_op jit(solution)/shard_map/slots_backward/pallas_call | solution.py:826
  157.3 0.0 collective-permute-start.3
  157.3 1.6 collective-permute-start.4
  158.9 0.3 collective-permute-start.5
  159.2 0.0 collective-permute-done.3.refs_5_
  159.2 0.0 copy-start.5
  159.2 3.5 %collective-permute-done.4.refs_6_ = bf16[320,128]{1,0:T(8,128)(2,1)S(1)} collective-permute-done((bf16[320,128]{1,0:T(8,128)(2,1)}, bf16[320,128]{1,0:T(8,128)(2,1)S(1)}, u32[]{:S(2)}, u32[]{:S(2)}) %collective-permute-start.4) | collective-permute-done | bytes 81952 | tf_op jit(solution)/shard_map/ppermute | solution.py:849
  162.7 0.0 copy-start.6
  162.7 1.2 collective-permute-done.5.refs_7_
  163.9 0.0 copy-start.7
  163.9 0.0 copy-done.5
  163.9 0.0 copy-done.6
  163.9 0.6 copy-done.7
  164.5 2.2 %join_tables.1 = bf16[8,152,128]{2,1,0:T(8,128)(2,1)} custom-call(bf16[896,128]{1,0:T(8,128)(2,1)} %get-tuple-element.122.refs_0_, bf16[896,128]{1,0:T(8,128)(2,1)} %collective-permute-done.refs_1_, bf16[896,128]{1,0:T(8,128)(2,1)} %collective-permute-done.1.refs_2_, bf16[896,128]{1,0:T(8,128)(2,1)} %collective-permute-done.2.refs_3_, ...), custom_call_target="tpu_custom_call" | custom-call | flops 2200000000 | bytes 2000000 | tf_op jit(solution)/shard_map/join_tables/pallas_call | solution.py:868
  166.7 15.2 %all_to_all.20.parts_ref = bf16[8,152,128]{2,1,0:T(8,128)(2,1)} all-to-all(bf16[8,152,128]{2,1,0:T(8,128)(2,1)} %join_tables.1), channel_id=1, replica_groups=mesh['table'=4,'rows'=8] {'rows'}, dimensions={0} | all-to-all | bytes 622592 | tf_op jit(solution)/shard_map/all_to_all | solution.py:887
  182.0 1.7 sum_rows.1
  183.7 13.6 %all_to_all.21.refs_1_ = bf16[8,152,128]{2,1,0:T(8,128)(2,1)S(1)} all-to-all(bf16[8,152,128]{2,1,0:T(8,128)(2,1)} %sum_rows.1), channel_id=1, replica_groups=mesh['table'=4,'rows'=8] {'rows'}, dimensions={0} | all-to-all | bytes 622592 | tf_op jit(solution)/shard_map/all_to_all | solution.py:900
  197.3 0.0 copy-start.1
  197.3 1.5 collective-permute-start.7
  198.8 0.0 collective-permute-start.6
  198.8 5.4 %collective-permute-done.7.refs_3_ = bf16[8,152,128]{2,1,0:T(8,128)(2,1)S(1)} collective-permute-done((bf16[8,152,128]{2,1,0:T(8,128)(2,1)S(1)}, bf16[8,152,128]{2,1,0:T(8,128)(2,1)S(1)}, u32[]{:S(2)}, u32[]{:S(2)}) %collective-permute-start.7) | collective-permute-done | bytes 311328 | tf_op jit(solution)/shard_map/ppermute | solution.py:903
  204.2 0.0 copy-start.2
  204.2 0.0 collective-permute-start.8
  204.2 0.0 collective-permute-done.6.refs_2_
  204.2 0.0 copy-start.3
  204.2 1.6 collective-permute-done.8.refs_4_
  205.8 0.0 copy-done.1
  205.8 0.0 copy-done.2
  205.8 0.0 copy-done.3
  205.8 0.0 copy-start.4
  205.8 0.7 copy-done.4
  206.5 8.0 %optimizer.1 = (f32[6,192,192]{2,1,0:T(8,128)}, f32[2,192,192]{2,1,0:T(8,128)}, f32[192,768]{1,0:T(8,128)}, f32[192,768]{1,0:T(8,128)}, f32[6,192]{1,0:T(8,128)}...) custom-call(s32[1]{0:T(128)} %bitcast.6.table_ref.refs_0_, ...), custom_call_target="tpu_custom_call" | custom-call | flops 8800000000 | bytes 8000000 | tf_op jit(solution)/shard_map/optimizer/pallas_call | solution.py:1035
Async XLA Ops:
  5.9 42.1 %all-to-all-start = ((bf16[8,2,120,384]{3,2,1,0:T(8,128)(2,1)}), bf16[8,2,120,384]{3,2,1,0:T(8,128)(2,1)S(1)}, u32[]{:S(2)}, u32[]{:S(2)}) async-start(bf16[8,2,120,384]{3,2,1,0:T(8,128)(2,1)} %get-tuple-element.84), calls=%async_computation | async-start | bytes 2949120 | tf_op jit(solution)/shard_map/all_to_all | solution.py:1070
  48.0 1.1 copy-start
  112.3 39.0 %all-to-all-start.1 = ((bf16[8,2,120,384]{3,2,1,0:T(8,128)(2,1)}), bf16[8,2,120,384]{3,2,1,0:T(8,128)(2,1)}, u32[]{:S(2)}, u32[]{:S(2)}) async-start(bf16[8,2,120,384]{3,2,1,0:T(8,128)(2,1)} %bitcast.23), calls=%async_computation.1 | async-start | bytes 2949120 | tf_op jit(solution)/shard_map/all_to_all | solution.py:1076
  116.8 32.3 %collective-permute-start = (bf16[896,128]{1,0:T(8,128)(2,1)}, bf16[896,128]{1,0:T(8,128)(2,1)}, u32[]{:S(2)}, u32[]{:S(2)}) collective-permute-start(bf16[896,128]{1,0:T(8,128)(2,1)} %get-tuple-element.112), channel_id=1, source_target_pairs={{0,8},{8,0},{16,24},{24,16},{1,9},{9,1},{17,25},{25,17},{2,10},{10... | collective-permute-start | bytes 688136 | tf_op jit(solution)/shard_map/ppermute | solution.py:849
  116.9 32.3 %collective-permute-start.1 = (bf16[896,128]{1,0:T(8,128)(2,1)}, bf16[896,128]{1,0:T(8,128)(2,1)}, u32[]{:S(2)}, u32[]{:S(2)}) collective-permute-start(bf16[896,128]{1,0:T(8,128)(2,1)} %get-tuple-element.113), channel_id=1, source_target_pairs={{0,16},{8,24},{16,0},{24,8},{1,17},{9,25},{17,1},{25,9},{2,18},{10... | collective-permute-start | bytes 688136 | tf_op jit(solution)/shard_map/ppermute | solution.py:849
  118.5 30.7 %collective-permute-start.2 = (bf16[896,128]{1,0:T(8,128)(2,1)}, bf16[896,128]{1,0:T(8,128)(2,1)}, u32[]{:S(2)}, u32[]{:S(2)}) collective-permute-start(bf16[896,128]{1,0:T(8,128)(2,1)} %get-tuple-element.114), channel_id=1, source_target_pairs={{0,24},{8,16},{16,8},{24,0},{1,25},{9,17},{17,9},{25,1},{2,26},{10... | collective-permute-start | bytes 688136 | tf_op jit(solution)/shard_map/ppermute | solution.py:849
  157.3 1.9 collective-permute-start.3
  157.3 5.3 %collective-permute-start.4 = (bf16[320,128]{1,0:T(8,128)(2,1)}, bf16[320,128]{1,0:T(8,128)(2,1)S(1)}, u32[]{:S(2)}, u32[]{:S(2)}) collective-permute-start(bf16[320,128]{1,0:T(8,128)(2,1)} %get-tuple-element.128), channel_id=1, source_target_pairs={{0,16},{8,24},{16,0},{24,8},{1,17},{9,25},{17,1},{25,9},{2,18},{10... | collective-permute-start | bytes 245768 | tf_op jit(solution)/shard_map/ppermute | solution.py:849
  158.9 4.9 %collective-permute-start.5 = (bf16[320,128]{1,0:T(8,128)(2,1)}, bf16[320,128]{1,0:T(8,128)(2,1)S(1)}, u32[]{:S(2)}, u32[]{:S(2)}) collective-permute-start(bf16[320,128]{1,0:T(8,128)(2,1)} %get-tuple-element.129), channel_id=1, source_target_pairs={{0,24},{8,16},{16,8},{24,0},{1,25},{9,17},{17,9},{25,1},{2,26},{10... | collective-permute-start | bytes 245768 | tf_op jit(solution)/shard_map/ppermute | solution.py:849
  159.2 4.7 %copy-start.5 = (bf16[320,128]{1,0:T(8,128)(2,1)}, bf16[320,128]{1,0:T(8,128)(2,1)S(1)}, u32[]{:S(2)}) copy-start(bf16[320,128]{1,0:T(8,128)(2,1)S(1)} %collective-permute-done.3.refs_5_) | copy-start | bytes 245764
  162.7 1.2 copy-start.6
  163.9 0.6 copy-start.7
  197.3 8.5 %copy-start.1 = (bf16[8,152,128]{2,1,0:T(8,128)(2,1)}, bf16[8,152,128]{2,1,0:T(8,128)(2,1)S(1)}, u32[]{:S(2)}) copy-start(bf16[8,152,128]{2,1,0:T(8,128)(2,1)S(1)} %all_to_all.21.refs_1_) | copy-start | bytes 933892
  197.3 6.9 %collective-permute-start.7 = (bf16[8,152,128]{2,1,0:T(8,128)(2,1)S(1)}, bf16[8,152,128]{2,1,0:T(8,128)(2,1)S(1)}, u32[]{:S(2)}, u32[]{:S(2)}) collective-permute-start(bf16[8,152,128]{2,1,0:T(8,128)(2,1)S(1)} %all_to_all.21.refs_1_), channel_id=1, source_target_pairs={{0,16},{8,24},{16,0},{24,8},{1,17},{9,25},{17,1},{25,9},{2,18},{10... | collective-permute-start | bytes 933896 | tf_op jit(solution)/shard_map/ppermute | solution.py:903
  198.8 5.4 %collective-permute-start.6 = (bf16[8,152,128]{2,1,0:T(8,128)(2,1)S(1)}, bf16[8,152,128]{2,1,0:T(8,128)(2,1)S(1)}, u32[]{:S(2)}, u32[]{:S(2)}) collective-permute-start(bf16[8,152,128]{2,1,0:T(8,128)(2,1)S(1)} %all_to_all.21.refs_1_), channel_id=1, source_target_pairs={{0,8},{8,0},{16,24},{24,16},{1,9},{9,1},{17,25},{25,17},{2,10},{10... | collective-permute-start | bytes 933896 | tf_op jit(solution)/shard_map/ppermute | solution.py:904
  204.2 1.6 copy-start.2
  204.2 1.6 collective-permute-start.8
  204.2 1.6 copy-start.3
  205.8 0.7 copy-start.4

commit v3 on v2

--- a/solution.py
+++ b/solution.py
@@ -17,6 +17,7 @@
 STEP = 3
 CLIP = 0.3
 RATE = 0.5
+WV = 0
 FB = 8
 SCALE = E**-0.5
 SCALE2 = SCALE * 1.4426950408889634
@@ -868,7 +869,7 @@
     return pl.pallas_call(
         functools.partial(join_kernel, len(mids)),
         out_shape=shape((shards, rows, 128)),
-        compiler_params=params(),
+        compiler_params=params(16),
         cost_estimate=cost(2),
         name="join_tables",
     )(*mids, *tails)
@@ -888,7 +889,7 @@
     return pl.pallas_call(
         sum_kernel,
         out_shape=shape(parts.shape),
-        compiler_params=params(),
+        compiler_params=params(16),
         cost_estimate=cost(2),
         name="sum_rows",
     )(parts)
@@ -940,15 +941,8 @@
 
 def optimizer_steps(
     proj_ref, outw_ref, in_ref, hid_ref, norm_ref, sr_ref, sc_ref, mm_ref, mh_ref, ns_ref,
-    proj_gx, out_gx, in_gx, hid_gx, norm_g, proj_nx, out_nx, in_nx, hid_nx, norm_n, sr_n, sc_n, mm_n, mh_n, ns_n,
-    proj_g, out_g, in_g, hid_g, proj_n, out_n, in_n, hid_n, sems, mid_ref, tail_ref,
+    proj_g, out_g, in_g, hid_g, norm_g, proj_n, out_n, in_n, hid_n, norm_n, sr_n, sc_n, mm_n, mh_n, ns_n, mid_ref, tail_ref,
 ):
-    copies = []
-
-    def send(a, b):
-        copies.append(pltpu.make_async_copy(a, b, sems.at[len(copies)]))
-        copies[-1].start()
-
     decay = 1.0 - STEP ** (-0.8)
 
     def stats(grad, col_old, row_old):
@@ -961,53 +955,46 @@
     def scaled(grad, col, row, mean):
         return grad * lax.rsqrt(col * (1.0 / mean)) * lax.rsqrt(row)
 
-    def square_pair(ref, at):
-        both = ref[at + 2 * D : at + 3 * D].astype(F32)
-        a = jnp.concatenate([ref[at : at + D].astype(F32), both[:, 0:64]], 1)
-        b = jnp.concatenate([ref[at + D : at + 2 * D].astype(F32), both[:, 64:128]], 1)
-        return a, b
-
-    wq, wk = square_pair(tail_ref, 0)
-    wv, wo = square_pair(tail_ref, PAIR)
-    wq2, wo2 = square_pair(mid_ref, 12 * D)
-    wk2, wv2 = square_pair(mid_ref, 12 * D + PAIR)
-    for i, grad in enumerate((wq, wk, wv, wq2, wk2, wv2, wo, wo2)):
+    def square_step(i, ref, at, first):
         g_ref, n_ref, w_ref, j = (proj_g, proj_n, proj_ref, i) if i < 6 else (out_g, out_n, outw_ref, i - 6)
-        gx, nx = (proj_gx, proj_nx) if i < 6 else (out_gx, out_nx)
+        low = ref[at : at + D] if first else ref[at + D : at + 2 * D]
+        high = ref[at + 2 * D : at + 3 * D]
+        grad = jnp.concatenate([low, high[:, 0:64] if first else high[:, 64:128]], 1)
         g_ref[j] = grad
-        send(g_ref.at[j], gx.at[j])
+        yield
         col, row = stats(grad, to_col(sr_ref[i : i + 1, :]), sc_ref[i : i + 1, :])
         sr_n[i : i + 1, :] = to_row(col)
         sc_n[i : i + 1, :] = row
+        yield
         mean = jnp.sum(col, 0, keepdims=True) * (1.0 / D)
+        update = scaled(grad, col, row, mean)
+        yield
         w = w_ref[j]
-        n_ref[j] = w - clipped(scaled(grad, col, row, mean), w, D * D)
-        send(n_ref.at[j], nx.at[j])
-
-    def wide(at):
-        return jnp.concatenate([mid_ref[at + D * j : at + D * j + D].astype(F32) for j in range(6)], 1)
-
-    grad = wide(0)
-    in_g[...] = grad
-    send(in_g, in_gx)
-    col, row = stats(grad, to_col(mm_ref[0:1, :]), mh_ref[0:1, :])
-    mm_n[0:1, :] = to_row(col)
-    mh_n[0:1, :] = row
-    mean = jnp.sum(col, 0, keepdims=True) * (1.0 / D)
-    w = in_ref[...]
-    in_n[...] = w - clipped(scaled(grad, col, row, mean), w, D * FF)
-    send(in_n, in_nx)
-    grad = wide(6 * D)
-    hid_g[...] = grad
-    send(hid_g, hid_gx)
-    col, row = stats(grad, to_col(mm_ref[1:2, :]), mh_ref[1:2, :])
-    mm_n[1:2, :] = to_row(col)
-    mh_n[1:2, :] = row
-    mean = jnp.sum(row, 1, keepdims=True) * (1.0 / FF)
-    w = hid_ref[...]
-    update = grad * lax.rsqrt(col) * lax.rsqrt(row * (1.0 / mean))
-    hid_n[...] = w - clipped(update, w, D * FF)
-    send(hid_n, hid_nx)
+        n_ref[j] = w - clipped(update, w, D * D)
+        yield
+
+    def wide_step(i, at, w_ref, g_ref, n_ref):
+        for j in range(6):
+            g_ref[:, 128 * j : 128 * j + 128] = mid_ref[at + D * j : at + D * j + D]
+            yield
+        grad = g_ref[...]
+        col, row = stats(grad, to_col(mm_ref[i : i + 1, :]), mh_ref[i : i + 1, :])
+        mm_n[i : i + 1, :] = to_row(col)
+        mh_n[i : i + 1, :] = row
+        yield
+        mean = jnp.sum(col, 0, keepdims=True) * (1.0 / D) if i == 0 else jnp.sum(row, 1, keepdims=True) * (1.0 / FF)
+        update = scaled(grad, col, row, mean)
+        yield
+        w = w_ref[...]
+        n_ref[...] = w - clipped(update, w, D * FF)
+        yield
+
+    steps = [wide_step(0, 0, in_ref, in_g, in_n), wide_step(1, 6 * D, hid_ref, hid_g, hid_n)]
+    places = ((0, tail_ref, 0, True), (1, tail_ref, 0, False), (2, tail_ref, PAIR, True), (6, tail_ref, PAIR, False))
+    places += ((3, mid_ref, 12 * D, True), (7, mid_ref, 12 * D, False))
+    places += ((4, mid_ref, 12 * D + PAIR, True), (5, mid_ref, 12 * D + PAIR, False))
+    steps += [square_step(*a) for a in places]
+    weave([(g, WV * i, 1) for i, g in enumerate(steps)])
 
     pieces = []
     for ref, at, count in ((tail_ref, 2 * PAIR, 2), (mid_ref, 12 * D + 2 * PAIR, 4)):
@@ -1023,29 +1010,22 @@
     w = norm_ref[...]
     w_rms = jnp.sqrt(jnp.sum(w * w, 1, keepdims=True) * (1.0 / D))
     norm_n[...] = w - update * (RATE * jnp.maximum(0.001, w_rms) / jnp.maximum(1.0, rms / CLIP))
-    for copy in copies:
-        copy.wait()
 
 
 def optimizer(table, pieces, mid_rows, *state):
     proj, outw, w_in, w_outT, norms, sr, sc, ms, hs, ns = state
     shards, rows, _ = pieces[0].shape
     order = [proj, outw, w_in, w_outT, norms, proj, outw, w_in, w_outT, norms, sr, sc, ms, hs, ns]
-    big = (0, 1, 2, 3, 5, 6, 7, 8)
     outs = pl.pallas_call(
         functools.partial(optimizer_kernel, len(pieces), mid_rows),
         in_specs=[pl.BlockSpec(memory_space=pltpu.SMEM)] + [whole(a) for a in (*pieces, *state)],
-        out_specs=[pl.BlockSpec(memory_space=pl.ANY) if i in big else whole(a) for i, a in enumerate(order)],
         out_shape=[shape(a.shape, F32) for a in order],
-        scratch_shapes=[pltpu.VMEM(order[i].shape, F32) for i in big]
-        + [
-            pltpu.SemaphoreType.DMA((20,)),
+        scratch_shapes=[
             pltpu.VMEM((len(pieces) * shards * mid_rows, 128), F32),
             pltpu.VMEM((len(pieces) * shards * (rows - mid_rows), 128), F32),
         ],
-        compiler_params=params(),
-        cost_estimate=cost(8),
-        name="optimizer",
+        compiler_params=params(28),
+        cost_estimate=cost(8), name="optimizer",
     )(table, *pieces, *state)
     outs = list(outs)
     for i in (3, 8):

time: 215 us -> 209 us (0.972)
  Pallas kernels: 147 us -> 142 us
    pallas_call x1, Pallas kernels: 7.97 us -> 5.53 us  [optimizer(): pl.pallas_call(functools.partial(optimizer_kernel, len(pieces), mid_rows)...]
  transfers between devices with their start and end apart: 11 -> 11, of which waited for: 6 -> 6; matrix products, arithmetic and copies ran while one was open for 0% -> 0% of each run, Pallas kernels for 28% -> 29%
where the time goes in v3:
time: 209 us; the launch traced here: 208 us
  Pallas kernels  142 us (68%)
  blocking collectives  27.9 us (13%)
  waiting for transfers between devices  18.2 us (9%)
  starting transfers between devices  16.9 us (8%)
    pallas_call x1, Pallas kernels, item_and_dense(): pl.pallas_call(functools.partial(item_kernel, RW, keys, tables, OFF, AO,...  63.2 us
    pallas_call x1, Pallas kernels, feature_backward(): pl.pallas_call(functools.partial(backward_kernel, R, OFF, YO), grid=(rows...  30.4 us
    pallas_call x1, Pallas kernels, feature_forward(): pl.pallas_call(functools.partial(forward_kernel, R, OFF), grid=(rows // R...  27.1 us
    all_to_all x1, blocking collectives, sum_rows(): parts = lax.all_to_all(parts, 'rows', 0, 0)  14.5 us
    all_to_all x1, blocking collectives, gather_all(): own = lax.all_to_all(copies, 'rows', 0, 0)  13.4 us
    all_to_all x1, starting transfers between devices, on_device(): slots = lax.all_to_all(own, 'rows', 0, 0).reshape((-1,) + own.shape[2:])  7.26 us
    pallas_call x1, Pallas kernels, slots_backward(): pl.pallas_call(functools.partial(slots_back_kernel, SL, tables), grid=(1,...  6.08 us
    ppermute x1, waiting for transfers between devices, gather_all(): lax.ppermute(own, 'table', [(t, (t // 2 + s) % ny * 2 + t % 2) for t in r...  5.56 us
  transfers between devices with their start and end apart: 11, of which 6 were waited for; matrix products, arithmetic and copies ran while one was open for 0% of the time, Pallas kernels for 29%

profile of v3, /device:TPU:0, one launch (start us, length us, event | category | flops | bytes accessed | tf_op | source)
XLA Modules:
  0.0 208.3 jit_solution(12118456831521241595)
XLA Ops:
  1.3 4.6 %slot_rows.1 = (bf16[8,2,120,384]{3,2,1,0:T(8,128)(2,1)}, bf16[576,256]{1,0:T(8,128)(2,1)}, bf16[192,256]{1,0:T(8,128)(2,1)}, f32[6,192,128]{2,1,0:T(8,128)}) custom-call(s32[1]{0:T(128)S(6)} %copy.35.count_ref, s32[1,4]{1,0:T(1,128)} %mask_ref.1, s32[1,4]{1,0:T(1,128)} %order_ref.1, bf16[64,192,119]{2,1,0:T(8,128)(2,1)} %bitcast.21, ...), custom_call_target="tpu_custom_call" | custom-call | flops 6600000000 | bytes 6000000 | tf_op jit(solution)/shard_map/slot_rows/pallas_call | solution.py:258
  5.9 7.3 %all-to-all-start = ((bf16[8,2,120,384]{3,2,1,0:T(8,128)(2,1)}), bf16[8,2,120,384]{3,2,1,0:T(8,128)(2,1)S(1)}, u32[]{:S(2)}, u32[]{:S(2)}) async-start(bf16[8,2,120,384]{3,2,1,0:T(8,128)(2,1)} %get-tuple-element.84), calls=%async_computation | async-start | bytes 2949120 | tf_op jit(solution)/shard_map/all_to_all | solution.py:1050
  13.1 3.4 %other_weights.1 = (bf16[192,768]{1,0:T(8,128)(2,1)}, bf16[192,256]{1,0:T(8,128)(2,1)}, bf16[256,512]{1,0:T(8,128)(2,1)}, bf16[512,256]{1,0:T(8,128)(2,1)}, bf16...) custom-call(f32[6,192,192]{2,1,0:T(8,128)} %refs_5_.1, ...), custom_call_target="tpu_custom_call" | custom-call | flops 4400000000 | bytes 4000000 | tf_op jit(solution)/shard_map/other_weights/pallas_call | solution.py:171
  16.5 27.1 %feature_forward.1 = (bf16[128,64,256]{2,1,0:T(8,128)(2,1)}, bf16[128,64,256]{2,1,0:T(8,128)(2,1)}, bf16[128,64,256]{2,1,0:T(8,128)(2,1)}, bf16[64,208,128]{2,1,...) custom-call(bf16[64,192,119]{2,1,0:T(8,128)(2,1)} %bitcast.22, ...), custom_call_target="tpu_custom_call" | custom-call | flops 39600001024 | bytes 36000000 | tf_op jit(solution)/shard_map/feature_forward/pallas_call | solution.py:332
  43.7 4.3 %all-to-all-done = bf16[8,2,120,384]{3,2,1,0:T(8,128)(2,1)S(1)} async-done(((bf16[8,2,120,384]{3,2,1,0:T(8,128)(2,1)}), bf16[8,2,120,384]{3,2,1,0:T(8,128)(2,1)S(1)}, u32[]{:S(2)}, u32[]{:S(2)}) %all-to-all-start) | async-done | bytes 1474592 | tf_op jit(solution)/shard_map/all_to_all | solution.py:1050
  48.0 0.0 copy-start.12
  48.0 1.1 copy-done.12
  49.1 63.2 %item_and_dense.1 = (bf16[120,64,256]{2,1,0:T(8,128)(2,1)}, bf16[120,64,256]{2,1,0:T(8,128)(2,1)}, bf16[16,120,384]{2,1,0:T(8,128)(2,1)}, bf16[896,128]{1,0:T(8,...) custom-call(s32[1]{0:T(128)} %bitcast.6.table_ref.refs_0_, ...), custom_call_target="tpu_custom_call" | custom-call | flops 72600002560 | bytes 66000000 | tf_op jit(solution)/shard_map/item_and_dense/pallas_call | solution.py:643
  112.3 4.5 %all-to-all-start.1 = ((bf16[8,2,120,384]{3,2,1,0:T(8,128)(2,1)}), bf16[8,2,120,384]{3,2,1,0:T(8,128)(2,1)}, u32[]{:S(2)}, u32[]{:S(2)}) async-start(bf16[8,2,120,384]{3,2,1,0:T(8,128)(2,1)} %bitcast.25), calls=%async_computation.1 | async-start | bytes 2949120 | tf_op jit(solution)/shard_map/all_to_all | solution.py:1056
  116.9 0.1 collective-permute-start
  117.0 1.6 collective-permute-start.1
  118.6 0.3 collective-permute-start.2
  118.8 30.4 %feature_backward.1 = (f32[64,192,119]{2,1,0:T(8,128)}, bf16[64,192,119]{2,1,0:T(8,128)(2,1)}, f32[576,192]{1,0:T(8,128)}, f32[192,192]{1,0:T(8,128)}, f32[2,192,128]{2,1,0:T(8,128)}) custom-call(bf16[64,192,119]{2,1,0:T(8,128)(2,1)} %bitcast.23, bf16[64,208,128]{2,1,0:T(8,128)(2,1)} %get-tuple-element.87.n_ref, ...), custom_call_target="tpu_custom_call" | custom-call | flops 263999995904 | bytes 240000000 | tf_op jit(solution)/shard_map/feature_backward/pallas_call | solution.py:773
  149.3 0.0 collective-permute-done.refs_1_
  149.3 0.0 collective-permute-done.1.refs_2_
  149.3 0.0 collective-permute-done.2.refs_3_
  149.3 2.0 all-to-all-done.1.slot_ref
  151.3 0.0 copy-start.11
  151.3 6.1 %slots_backward.1 = (f32[64,192,119]{2,1,0:T(8,128)}, bf16[320,128]{1,0:T(8,128)(2,1)}, bf16[320,128]{1,0:T(8,128)(2,1)}, bf16[320,128]{1,0:T(8,128)(2,1)}, bf16[320,128]{1,0:T(8,128)(2,1)}) custom-call(s32[1]{0:T(128)} %bitcast.6.table_ref.refs_0_, bf16[64,192,119]{2,1,0:T(8,128)(2,1)} %bitcast.24, ...), custom_call_target="tpu_custom_call", output_to_operand_aliasing={{0}: (8, {})} | custom-call | flops 8800000000 | bytes 8000000 | tf_op jit(solution)/shard_map/slots_backward/pallas_call | solution.py:827
  157.4 0.0 collective-permute-start.3
  157.4 1.6 collective-permute-start.4
  159.0 0.3 collective-permute-start.5
  159.3 0.0 collective-permute-done.3.refs_5_
  159.3 3.5 %collective-permute-done.4.refs_6_ = bf16[320,128]{1,0:T(8,128)(2,1)S(1)} collective-permute-done((bf16[320,128]{1,0:T(8,128)(2,1)}, bf16[320,128]{1,0:T(8,128)(2,1)S(1)}, u32[]{:S(2)}, u32[]{:S(2)}) %collective-permute-start.4) | collective-permute-done | bytes 81952 | tf_op jit(solution)/shard_map/ppermute | solution.py:850
  162.7 1.2 collective-permute-done.5.refs_7_
  163.9 0.0 copy-done.11
  163.9 0.0 copy-start.4
  163.9 0.9 copy-done.4
  164.8 1.3 join_tables.1
  166.1 14.5 %all_to_all.20.parts_ref = bf16[8,152,128]{2,1,0:T(8,128)(2,1)S(1)} all-to-all(bf16[8,152,128]{2,1,0:T(8,128)(2,1)S(1)} %join_tables.1), channel_id=1, replica_groups=mesh['table'=4,'rows'=8] {'rows'}, dimensions={0} | all-to-all | bytes 622592 | tf_op jit(solution)/shard_map/all_to_all | solution.py:888
  180.7 0.0 copy-start
  180.7 0.0 copy-start.1
  180.7 0.0 copy-start.2
  180.7 0.0 copy-start.3
  180.7 0.0 copy-start.5
  180.7 0.0 copy-start.6
  180.7 0.0 copy-start.7
  180.7 0.0 copy-start.8
  180.7 0.0 copy-start.9
  180.7 0.0 copy-start.10
  180.8 0.1 sum_rows.1
  180.8 13.4 %all_to_all.21.refs_1_ = bf16[8,152,128]{2,1,0:T(8,128)(2,1)S(1)} all-to-all(bf16[8,152,128]{2,1,0:T(8,128)(2,1)S(1)} %sum_rows.1), channel_id=1, replica_groups=mesh['table'=4,'rows'=8] {'rows'}, dimensions={0} | all-to-all | bytes 622592 | tf_op jit(solution)/shard_map/all_to_all | solution.py:901
  194.2 1.3 collective-permute-start.7
  195.5 0.0 collective-permute-start.6
  195.5 5.6 %collective-permute-done.7.refs_3_ = bf16[8,152,128]{2,1,0:T(8,128)(2,1)S(1)} collective-permute-done((bf16[8,152,128]{2,1,0:T(8,128)(2,1)S(1)}, bf16[8,152,128]{2,1,0:T(8,128)(2,1)S(1)}, u32[]{:S(2)}, u32[]{:S(2)}) %collective-permute-start.7) | collective-permute-done | bytes 311328 | tf_op jit(solution)/shard_map/ppermute | solution.py:904
  201.1 0.0 collective-permute-start.8
  201.1 0.0 collective-permute-done.6.refs_2_
  201.1 1.6 collective-permute-done.8.refs_4_
  202.7 0.0 copy-done
  202.7 0.0 copy-done.1
  202.7 0.0 copy-done.2
  202.7 0.0 copy-done.3
  202.7 0.0 copy-done.5
  202.7 0.0 copy-done.6
  202.8 0.0 copy-done.7
  202.8 0.0 copy-done.8
  202.8 0.0 copy-done.9
  202.8 0.0 copy-done.10
  202.8 5.5 %optimizer.1 = (f32[6,192,192]{2,1,0:T(8,128)}, f32[2,192,192]{2,1,0:T(8,128)}, f32[192,768]{1,0:T(8,128)}, f32[192,768]{1,0:T(8,128)}, f32[6,192]{1,0:T(8,128)}...) custom-call(s32[1]{0:T(128)} %bitcast.6.table_ref.refs_0_, ...), custom_call_target="tpu_custom_call" | custom-call | flops 8800000000 | bytes 8000000 | tf_op jit(solution)/shard_map/optimizer/pallas_call | solution.py:1019
Async XLA Ops:
  5.9 42.1 %all-to-all-start = ((bf16[8,2,120,384]{3,2,1,0:T(8,128)(2,1)}), bf16[8,2,120,384]{3,2,1,0:T(8,128)(2,1)S(1)}, u32[]{:S(2)}, u32[]{:S(2)}) async-start(bf16[8,2,120,384]{3,2,1,0:T(8,128)(2,1)} %get-tuple-element.84), calls=%async_computation | async-start | bytes 2949120 | tf_op jit(solution)/shard_map/all_to_all | solution.py:1050
  48.0 1.1 copy-start.12
  112.3 39.0 %all-to-all-start.1 = ((bf16[8,2,120,384]{3,2,1,0:T(8,128)(2,1)}), bf16[8,2,120,384]{3,2,1,0:T(8,128)(2,1)}, u32[]{:S(2)}, u32[]{:S(2)}) async-start(bf16[8,2,120,384]{3,2,1,0:T(8,128)(2,1)} %bitcast.25), calls=%async_computation.1 | async-start | bytes 2949120 | tf_op jit(solution)/shard_map/all_to_all | solution.py:1056
  116.9 32.4 %collective-permute-start = (bf16[896,128]{1,0:T(8,128)(2,1)}, bf16[896,128]{1,0:T(8,128)(2,1)}, u32[]{:S(2)}, u32[]{:S(2)}) collective-permute-start(bf16[896,128]{1,0:T(8,128)(2,1)} %get-tuple-element.112), channel_id=1, source_target_pairs={{0,8},{8,0},{16,24},{24,16},{1,9},{9,1},{17,25},{25,17},{2,10},{10... | collective-permute-start | bytes 688136 | tf_op jit(solution)/shard_map/ppermute | solution.py:850
  117.0 32.3 %collective-permute-start.1 = (bf16[896,128]{1,0:T(8,128)(2,1)}, bf16[896,128]{1,0:T(8,128)(2,1)}, u32[]{:S(2)}, u32[]{:S(2)}) collective-permute-start(bf16[896,128]{1,0:T(8,128)(2,1)} %get-tuple-element.113), channel_id=1, source_target_pairs={{0,16},{8,24},{16,0},{24,8},{1,17},{9,25},{17,1},{25,9},{2,18},{10... | collective-permute-start | bytes 688136 | tf_op jit(solution)/shard_map/ppermute | solution.py:850
  118.6 30.7 %collective-permute-start.2 = (bf16[896,128]{1,0:T(8,128)(2,1)}, bf16[896,128]{1,0:T(8,128)(2,1)}, u32[]{:S(2)}, u32[]{:S(2)}) collective-permute-start(bf16[896,128]{1,0:T(8,128)(2,1)} %get-tuple-element.114), channel_id=1, source_target_pairs={{0,24},{8,16},{16,8},{24,0},{1,25},{9,17},{17,9},{25,1},{2,26},{10... | collective-permute-start | bytes 688136 | tf_op jit(solution)/shard_map/ppermute | solution.py:850
  151.3 12.6 %copy-start.11 = (bf16[896,128]{1,0:T(8,128)(2,1)S(1)}, bf16[896,128]{1,0:T(8,128)(2,1)}, u32[]{:S(2)}) copy-start(bf16[896,128]{1,0:T(8,128)(2,1)} %get-tuple-element.122.refs_0_) | copy-start | bytes 688132
  157.4 1.9 collective-permute-start.3
  157.4 5.3 %collective-permute-start.4 = (bf16[320,128]{1,0:T(8,128)(2,1)}, bf16[320,128]{1,0:T(8,128)(2,1)S(1)}, u32[]{:S(2)}, u32[]{:S(2)}) collective-permute-start(bf16[320,128]{1,0:T(8,128)(2,1)} %get-tuple-element.128), channel_id=1, source_target_pairs={{0,16},{8,24},{16,0},{24,8},{1,17},{9,25},{17,1},{25,9},{2,18},{10... | collective-permute-start | bytes 245768 | tf_op jit(solution)/shard_map/ppermute | solution.py:850
  159.0 4.9 %collective-permute-start.5 = (bf16[320,128]{1,0:T(8,128)(2,1)}, bf16[320,128]{1,0:T(8,128)(2,1)S(1)}, u32[]{:S(2)}, u32[]{:S(2)}) collective-permute-start(bf16[320,128]{1,0:T(8,128)(2,1)} %get-tuple-element.129), channel_id=1, source_target_pairs={{0,24},{8,16},{16,8},{24,0},{1,25},{9,17},{17,9},{25,1},{2,26},{10... | collective-permute-start | bytes 245768 | tf_op jit(solution)/shard_map/ppermute | solution.py:850
  163.9 0.9 copy-start.4
  180.7 22.0 %copy-start = (f32[6,192,192]{2,1,0:T(8,128)S(1)}, f32[6,192,192]{2,1,0:T(8,128)}, u32[]{:S(2)}) copy-start(f32[6,192,192]{2,1,0:T(8,128)} %refs_5_.1) | copy-start | bytes 2654212
  180.7 22.0 %copy-start.1 = (f32[192,768]{1,0:T(8,128)S(1)}, f32[192,768]{1,0:T(8,128)}, u32[]{:S(2)}) copy-start(f32[192,768]{1,0:T(8,128)} %refs_7_.1) | copy-start | bytes 1769476
  180.7 22.0 %copy-start.2 = (f32[768,192]{0,1:T(8,128)S(1)}, f32[768,192]{0,1:T(8,128)}, u32[]{:S(2)}) copy-start(f32[768,192]{0,1:T(8,128)} %param.24) | copy-start | bytes 1769476
  180.7 22.1 %copy-start.3 = (f32[2,192,192]{2,1,0:T(8,128)S(1)}, f32[2,192,192]{2,1,0:T(8,128)}, u32[]{:S(2)}) copy-start(f32[2,192,192]{2,1,0:T(8,128)} %refs_6_.1) | copy-start | bytes 884740
  180.7 22.1 %copy-start.5 = (f32[6,192]{1,0:T(8,128)S(1)}, f32[6,192]{1,0:T(8,128)}, u32[]{:S(2)}) copy-start(f32[6,192]{1,0:T(8,128)} %refs_9_.1) | copy-start | bytes 13828
  180.7 22.1 %copy-start.6 = (f32[8,192]{1,0:T(8,128)S(1)}, f32[8,192]{1,0:T(8,128)}, u32[]{:S(2)}) copy-start(f32[8,192]{1,0:T(8,128)} %refs_10_.1) | copy-start | bytes 18436
  180.7 22.1 %copy-start.7 = (f32[8,192]{1,0:T(8,128)S(1)}, f32[8,192]{1,0:T(8,128)}, u32[]{:S(2)}) copy-start(f32[8,192]{1,0:T(8,128)} %refs_11_.1) | copy-start | bytes 18436
  180.7 22.1 %copy-start.8 = (f32[6,192]{1,0:T(8,128)S(1)}, f32[6,192]{1,0:T(8,128)}, u32[]{:S(2)}) copy-start(f32[6,192]{1,0:T(8,128)} %refs_14_.1) | copy-start | bytes 13828
  180.7 22.0 %copy-start.9 = (f32[2,768]{1,0:T(2,128)S(1)}, f32[2,768]{1,0:T(2,128)}, u32[]{:S(2)}) copy-start(f32[2,768]{1,0:T(2,128)} %refs_13_.1) | copy-start | bytes 18436
  180.7 22.0 %copy-start.10 = (f32[2,192]{1,0:T(2,128)S(1)}, f32[2,192]{1,0:T(2,128)}, u32[]{:S(2)}) copy-start(f32[2,192]{1,0:T(2,128)} %refs_12_.1) | copy-start | bytes 4612
  194.2 6.9 %collective-permute-start.7 = (bf16[8,152,128]{2,1,0:T(8,128)(2,1)S(1)}, bf16[8,152,128]{2,1,0:T(8,128)(2,1)S(1)}, u32[]{:S(2)}, u32[]{:S(2)}) collective-permute-start(bf16[8,152,128]{2,1,0:T(8,128)(2,1)S(1)} %all_to_all.21.refs_1_), channel_id=1, source_target_pairs={{0,16},{8,24},{16,0},{24,8},{1,17},{9,25},{17,1},{25,9},{2,18},{10... | collective-permute-start | bytes 933896 | tf_op jit(solution)/shard_map/ppermute | solution.py:904
  195.5 5.6 %collective-permute-start.6 = (bf16[8,152,128]{2,1,0:T(8,128)(2,1)S(1)}, bf16[8,152,128]{2,1,0:T(8,128)(2,1)S(1)}, u32[]{:S(2)}, u32[]{:S(2)}) collective-permute-start(bf16[8,152,128]{2,1,0:T(8,128)(2,1)S(1)} %all_to_all.21.refs_1_), channel_id=1, source_target_pairs={{0,8},{8,0},{16,24},{24,16},{1,9},{9,1},{17,25},{25,17},{2,10},{10... | collective-permute-start | bytes 933896 | tf_op jit(solution)/shard_map/ppermute | solution.py:905
  201.1 1.6 collective-permute-start.8

commit v4 on v3

--- a/solution.py
+++ b/solution.py
@@ -18,7 +18,6 @@
 CLIP = 0.3
 RATE = 0.5
 WV = 0
-FB = 8
 SCALE = E**-0.5
 SCALE2 = SCALE * 1.4426950408889634
 C0 = 0.7978845608028654
@@ -378,7 +377,7 @@
 
 
 def item_kernel(
-    RW, keys, tables, OFF, AO, AS, WP, CC, WC, table_ref, ht_ref, next_ref, q_ref, qnext_ref, ct_ref, slot_ref, perm_ref, wqT_ref, woI_ref, wo_ref, w1T_ref, w1_ref, w2T_ref, w2_ref,
+    FB, RW, keys, tables, OFF, AO, AS, WP, CC, WC, table_ref, ht_ref, next_ref, q_ref, qnext_ref, ct_ref, slot_ref, perm_ref, wqT_ref, woI_ref, wo_ref, w1T_ref, w1_ref, w2T_ref, w2_ref,
     wkv_ref, wkvT_ref, vec_ref, y_ref, g1_ref, back_ref, *rest
 ):
     piece_refs, rest = rest[:tables], rest[tables:]
@@ -629,9 +628,10 @@
         hand_out(table_ref, pack_ref, piece_refs)
 
 
-def item_and_dense(table, ht, qt, ct, slots, perm, ws, vec, packed, tables, OFF=0, AO=2, AS=6, WP=4, CC=384, WC=192):
+def item_and_dense(table, ht, qt, ct, slots, perm, ws, vec, packed, tables, OFF=0, CC=384, WC=192):
     RW = ht.shape[1]
     keys = 2 * slots.shape[0]
+    FB, AO, AS, WP = (20, 2, 2, 2) if keys <= 32 else (8, 2, 6, 4)
     M = FB * RW
     cells = pl.BlockSpec((FB, RW, DP), lambda i: (i, 0, 0))
     accs = [(D, DP), (D, DP), (FF, D), (FF, D), (4, D, 128), (DP, 2 * DP), (keys, 128), (packed, 128)]
@@ -641,7 +641,7 @@
     flat = [slots, perm, *ws, vec]
     outs = [shape((FS, RW, DP))] * 2 + [shape(slots.shape)] + [shape((packed // tables, 128))] * tables
     return pl.pallas_call(
-        functools.partial(item_kernel, RW, keys, tables, OFF, AO, AS, WP, CC, WC),
+        functools.partial(item_kernel, FB, RW, keys, tables, OFF, AO, AS, WP, CC, WC),
         grid=(FS // FB,),
         in_specs=[pl.BlockSpec(memory_space=pltpu.SMEM), cells, ahead, cells, ahead, cells] + [whole(a) for a in flat],
         out_specs=[cells, cells] + [whole(a) for a in outs[2:]],

time: 209 us -> 203 us (0.971)
  Pallas kernels: 142 us -> 136 us
    pallas_call x1, Pallas kernels: 63.2 us -> 57.8 us  [item_and_dense(): pl.pallas_call(functools.partial(item_kernel, FB, RW, keys, tables, OFF,...]
  transfers between devices with their start and end apart: 11 -> 11, of which waited for: 6 -> 6; matrix products, arithmetic and copies ran while one was open for 0% -> 0% of each run, Pallas kernels for 29% -> 30%
where the time goes in v4:
time: 203 us
  Pallas kernels  136 us (67%)
  blocking collectives  28 us (14%)
  waiting for transfers between devices  18.3 us (9%)
  starting transfers between devices  16.7 us (8%)
  local copies, waits for them, and re-layouts  2.05 us (1%)
    pallas_call x1, Pallas kernels, item_and_dense(): pl.pallas_call(functools.partial(item_kernel, FB, RW, keys, tables, OFF,...  57.8 us
    pallas_call x1, Pallas kernels, feature_backward(): pl.pallas_call(functools.partial(backward_kernel, R, OFF, YO), grid=(rows...  30.4 us
    pallas_call x1, Pallas kernels, feature_forward(): pl.pallas_call(functools.partial(forward_kernel, R, OFF), grid=(rows // R...  27.1 us
    all_to_all x1, blocking collectives, sum_rows(): parts = lax.all_to_all(parts, 'rows', 0, 0)  14.6 us
    all_to_all x1, blocking collectives, gather_all(): own = lax.all_to_all(copies, 'rows', 0, 0)  13.4 us
    all_to_all x1, starting transfers between devices, on_device(): slots = lax.all_to_all(own, 'rows', 0, 0).reshape((-1,) + own.shape[2:])  7.26 us
    pallas_call x1, Pallas kernels, slots_backward(): pl.pallas_call(functools.partial(slots_back_kernel, SL, tables), grid=(1,...  6.07 us
    ppermute x1, waiting for transfers between devices, gather_all(): lax.ppermute(own, 'table', [(t, (t // 2 + s) % ny * 2 + t % 2) for t in r...  5.54 us
  transfers between devices with their start and end apart: 11, of which 6 were waited for; matrix products, arithmetic and copies ran while one was open for 0% of the time, Pallas kernels for 30%

profile of v4, /device:TPU:0, one launch (start us, length us, event | category | flops | bytes accessed | tf_op | source)
XLA Modules:
  0.0 202.9 jit_solution(2425604063058384140)
XLA Ops:
  1.3 4.6 %slot_rows.1 = (bf16[8,2,120,384]{3,2,1,0:T(8,128)(2,1)}, bf16[576,256]{1,0:T(8,128)(2,1)}, bf16[192,256]{1,0:T(8,128)(2,1)}, f32[6,192,128]{2,1,0:T(8,128)}) custom-call(s32[1]{0:T(128)S(6)} %copy.35.count_ref, s32[1,4]{1,0:T(1,128)} %mask_ref.1, s32[1,4]{1,0:T(1,128)} %order_ref.1, bf16[64,192,119]{2,1,0:T(8,128)(2,1)} %bitcast.21, ...), custom_call_target="tpu_custom_call" | custom-call | flops 6600000000 | bytes 6000000 | tf_op jit(solution)/shard_map/slot_rows/pallas_call | solution.py:257
  5.9 7.3 %all-to-all-start = ((bf16[8,2,120,384]{3,2,1,0:T(8,128)(2,1)}), bf16[8,2,120,384]{3,2,1,0:T(8,128)(2,1)S(1)}, u32[]{:S(2)}, u32[]{:S(2)}) async-start(bf16[8,2,120,384]{3,2,1,0:T(8,128)(2,1)} %get-tuple-element.84), calls=%async_computation | async-start | bytes 2949120 | tf_op jit(solution)/shard_map/all_to_all | solution.py:1050
  13.1 3.4 %other_weights.1 = (bf16[192,768]{1,0:T(8,128)(2,1)}, bf16[192,256]{1,0:T(8,128)(2,1)}, bf16[256,512]{1,0:T(8,128)(2,1)}, bf16[512,256]{1,0:T(8,128)(2,1)}, bf16...) custom-call(f32[6,192,192]{2,1,0:T(8,128)} %refs_5_.1, ...), custom_call_target="tpu_custom_call" | custom-call | flops 4400000000 | bytes 4000000 | tf_op jit(solution)/shard_map/other_weights/pallas_call | solution.py:170
  16.5 27.1 %feature_forward.1 = (bf16[128,64,256]{2,1,0:T(8,128)(2,1)}, bf16[128,64,256]{2,1,0:T(8,128)(2,1)}, bf16[128,64,256]{2,1,0:T(8,128)(2,1)}, bf16[64,208,128]{2,1,...) custom-call(bf16[64,192,119]{2,1,0:T(8,128)(2,1)} %bitcast.22, ...), custom_call_target="tpu_custom_call" | custom-call | flops 39600001024 | bytes 36000000 | tf_op jit(solution)/shard_map/feature_forward/pallas_call | solution.py:331
  43.7 4.3 %all-to-all-done = bf16[8,2,120,384]{3,2,1,0:T(8,128)(2,1)S(1)} async-done(((bf16[8,2,120,384]{3,2,1,0:T(8,128)(2,1)}), bf16[8,2,120,384]{3,2,1,0:T(8,128)(2,1)S(1)}, u32[]{:S(2)}, u32[]{:S(2)}) %all-to-all-start) | async-done | bytes 1474592 | tf_op jit(solution)/shard_map/all_to_all | solution.py:1050
  48.0 0.0 copy-start.12
  48.0 1.1 copy-done.12
  49.1 57.8 %item_and_dense.1 = (bf16[120,64,256]{2,1,0:T(8,128)(2,1)}, bf16[120,64,256]{2,1,0:T(8,128)(2,1)}, bf16[16,120,384]{2,1,0:T(8,128)(2,1)}, bf16[896,128]{1,0:T(8,...) custom-call(s32[1]{0:T(128)} %bitcast.6.table_ref.refs_0_, ...), custom_call_target="tpu_custom_call" | custom-call | flops 72600002560 | bytes 66000000 | tf_op jit(solution)/shard_map/item_and_dense/pallas_call | solution.py:643
  106.9 4.3 %all-to-all-start.1 = ((bf16[8,2,120,384]{3,2,1,0:T(8,128)(2,1)}), bf16[8,2,120,384]{3,2,1,0:T(8,128)(2,1)}, u32[]{:S(2)}, u32[]{:S(2)}) async-start(bf16[8,2,120,384]{3,2,1,0:T(8,128)(2,1)} %bitcast.25), calls=%async_computation.1 | async-start | bytes 2949120 | tf_op jit(solution)/shard_map/all_to_all | solution.py:1056
  111.2 0.1 collective-permute-start
  111.3 1.6 collective-permute-start.1
  112.9 0.3 collective-permute-start.2
  113.2 30.4 %feature_backward.1 = (f32[64,192,119]{2,1,0:T(8,128)}, bf16[64,192,119]{2,1,0:T(8,128)(2,1)}, f32[576,192]{1,0:T(8,128)}, f32[192,192]{1,0:T(8,128)}, f32[2,192,128]{2,1,0:T(8,128)}) custom-call(bf16[64,192,119]{2,1,0:T(8,128)(2,1)} %bitcast.23, bf16[64,208,128]{2,1,0:T(8,128)(2,1)} %get-tuple-element.87.n_ref, ...), custom_call_target="tpu_custom_call" | custom-call | flops 263999995904 | bytes 240000000 | tf_op jit(solution)/shard_map/feature_backward/pallas_call | solution.py:773
  143.6 0.0 collective-permute-done.refs_1_
  143.6 0.0 collective-permute-done.1.refs_2_
  143.7 0.0 collective-permute-done.2.refs_3_
  143.7 2.1 %all-to-all-done.1.slot_ref = bf16[8,2,120,384]{3,2,1,0:T(8,128)(2,1)} async-done(((bf16[8,2,120,384]{3,2,1,0:T(8,128)(2,1)}), bf16[8,2,120,384]{3,2,1,0:T(8,128)(2,1)}, u32[]{:S(2)}, u32[]{:S(2)}) %all-to-all-start.1) | async-done | bytes 1474592 | tf_op jit(solution)/shard_map/all_to_all | solution.py:1056
  145.8 0.0 copy-start.11
  145.8 6.1 %slots_backward.1 = (f32[64,192,119]{2,1,0:T(8,128)}, bf16[320,128]{1,0:T(8,128)(2,1)}, bf16[320,128]{1,0:T(8,128)(2,1)}, bf16[320,128]{1,0:T(8,128)(2,1)}, bf16[320,128]{1,0:T(8,128)(2,1)}) custom-call(s32[1]{0:T(128)} %bitcast.6.table_ref.refs_0_, bf16[64,192,119]{2,1,0:T(8,128)(2,1)} %bitcast.24, ...), custom_call_target="tpu_custom_call", output_to_operand_aliasing={{0}: (8, {})} | custom-call | flops 8800000000 | bytes 8000000 | tf_op jit(solution)/shard_map/slots_backward/pallas_call | solution.py:827
  151.9 0.0 collective-permute-start.3
  151.9 1.6 collective-permute-start.4
  153.5 0.3 collective-permute-start.5
  153.7 0.0 collective-permute-done.3.refs_5_
  153.7 3.5 %collective-permute-done.4.refs_6_ = bf16[320,128]{1,0:T(8,128)(2,1)S(1)} collective-permute-done((bf16[320,128]{1,0:T(8,128)(2,1)}, bf16[320,128]{1,0:T(8,128)(2,1)S(1)}, u32[]{:S(2)}, u32[]{:S(2)}) %collective-permute-start.4) | collective-permute-done | bytes 81952 | tf_op jit(solution)/shard_map/ppermute | solution.py:850
  157.2 1.2 collective-permute-done.5.refs_7_
  158.4 0.0 copy-done.11
  158.4 0.0 copy-start.4
  158.4 0.9 copy-done.4
  159.3 1.3 join_tables.1
  160.6 14.6 %all_to_all.20.parts_ref = bf16[8,152,128]{2,1,0:T(8,128)(2,1)S(1)} all-to-all(bf16[8,152,128]{2,1,0:T(8,128)(2,1)S(1)} %join_tables.1), channel_id=1, replica_groups=mesh['table'=4,'rows'=8] {'rows'}, dimensions={0} | all-to-all | bytes 622592 | tf_op jit(solution)/shard_map/all_to_all | solution.py:888
  175.2 0.0 copy-start
  175.2 0.0 copy-start.1
  175.2 0.0 copy-start.2
  175.2 0.0 copy-start.3
  175.3 0.0 copy-start.5
  175.3 0.0 copy-start.6
  175.3 0.0 copy-start.7
  175.3 0.0 copy-start.8
  175.3 0.0 copy-start.9
  175.3 0.0 copy-start.10
  175.3 0.1 sum_rows.1
  175.4 13.4 %all_to_all.21.refs_1_ = bf16[8,152,128]{2,1,0:T(8,128)(2,1)S(1)} all-to-all(bf16[8,152,128]{2,1,0:T(8,128)(2,1)S(1)} %sum_rows.1), channel_id=1, replica_groups=mesh['table'=4,'rows'=8] {'rows'}, dimensions={0} | all-to-all | bytes 622592 | tf_op jit(solution)/shard_map/all_to_all | solution.py:901
  188.8 1.4 collective-permute-start.7
  190.1 0.0 collective-permute-start.6
  190.1 5.5 %collective-permute-done.7.refs_3_ = bf16[8,152,128]{2,1,0:T(8,128)(2,1)S(1)} collective-permute-done((bf16[8,152,128]{2,1,0:T(8,128)(2,1)S(1)}, bf16[8,152,128]{2,1,0:T(8,128)(2,1)S(1)}, u32[]{:S(2)}, u32[]{:S(2)}) %collective-permute-start.7) | collective-permute-done | bytes 311328 | tf_op jit(solution)/shard_map/ppermute | solution.py:904
  195.7 0.0 collective-permute-start.8
  195.7 0.0 collective-permute-done.6.refs_2_
  195.7 1.6 collective-permute-done.8.refs_4_
  197.3 0.0 copy-done
  197.3 0.0 copy-done.1
  197.3 0.0 copy-done.2
  197.3 0.0 copy-done.3
  197.3 0.0 copy-done.5
  197.3 0.0 copy-done.6
  197.3 0.0 copy-done.7
  197.3 0.0 copy-done.8
  197.3 0.0 copy-done.9
  197.4 0.0 copy-done.10
  197.4 5.5 %optimizer.1 = (f32[6,192,192]{2,1,0:T(8,128)}, f32[2,192,192]{2,1,0:T(8,128)}, f32[192,768]{1,0:T(8,128)}, f32[192,768]{1,0:T(8,128)}, f32[6,192]{1,0:T(8,128)}...) custom-call(s32[1]{0:T(128)} %bitcast.6.table_ref.refs_0_, ...), custom_call_target="tpu_custom_call" | custom-call | flops 8800000000 | bytes 8000000 | tf_op jit(solution)/shard_map/optimizer/pallas_call | solution.py:1019
Async XLA Ops:
  5.9 42.1 %all-to-all-start = ((bf16[8,2,120,384]{3,2,1,0:T(8,128)(2,1)}), bf16[8,2,120,384]{3,2,1,0:T(8,128)(2,1)S(1)}, u32[]{:S(2)}, u32[]{:S(2)}) async-start(bf16[8,2,120,384]{3,2,1,0:T(8,128)(2,1)} %get-tuple-element.84), calls=%async_computation | async-start | bytes 2949120 | tf_op jit(solution)/shard_map/all_to_all | solution.py:1050
  48.0 1.1 copy-start.12
  106.9 38.9 %all-to-all-start.1 = ((bf16[8,2,120,384]{3,2,1,0:T(8,128)(2,1)}), bf16[8,2,120,384]{3,2,1,0:T(8,128)(2,1)}, u32[]{:S(2)}, u32[]{:S(2)}) async-start(bf16[8,2,120,384]{3,2,1,0:T(8,128)(2,1)} %bitcast.25), calls=%async_computation.1 | async-start | bytes 2949120 | tf_op jit(solution)/shard_map/all_to_all | solution.py:1056
  111.2 32.4 %collective-permute-start = (bf16[896,128]{1,0:T(8,128)(2,1)}, bf16[896,128]{1,0:T(8,128)(2,1)}, u32[]{:S(2)}, u32[]{:S(2)}) collective-permute-start(bf16[896,128]{1,0:T(8,128)(2,1)} %get-tuple-element.112), channel_id=1, source_target_pairs={{0,8},{8,0},{16,24},{24,16},{1,9},{9,1},{17,25},{25,17},{2,10},{10... | collective-permute-start | bytes 688136 | tf_op jit(solution)/shard_map/ppermute | solution.py:850
  111.3 32.3 %collective-permute-start.1 = (bf16[896,128]{1,0:T(8,128)(2,1)}, bf16[896,128]{1,0:T(8,128)(2,1)}, u32[]{:S(2)}, u32[]{:S(2)}) collective-permute-start(bf16[896,128]{1,0:T(8,128)(2,1)} %get-tuple-element.113), channel_id=1, source_target_pairs={{0,16},{8,24},{16,0},{24,8},{1,17},{9,25},{17,1},{25,9},{2,18},{10... | collective-permute-start | bytes 688136 | tf_op jit(solution)/shard_map/ppermute | solution.py:850
  112.9 30.7 %collective-permute-start.2 = (bf16[896,128]{1,0:T(8,128)(2,1)}, bf16[896,128]{1,0:T(8,128)(2,1)}, u32[]{:S(2)}, u32[]{:S(2)}) collective-permute-start(bf16[896,128]{1,0:T(8,128)(2,1)} %get-tuple-element.114), channel_id=1, source_target_pairs={{0,24},{8,16},{16,8},{24,0},{1,25},{9,17},{17,9},{25,1},{2,26},{10... | collective-permute-start | bytes 688136 | tf_op jit(solution)/shard_map/ppermute | solution.py:850
  145.8 12.6 %copy-start.11 = (bf16[896,128]{1,0:T(8,128)(2,1)S(1)}, bf16[896,128]{1,0:T(8,128)(2,1)}, u32[]{:S(2)}) copy-start(bf16[896,128]{1,0:T(8,128)(2,1)} %get-tuple-element.122.refs_0_) | copy-start | bytes 688132
  151.9 1.9 collective-permute-start.3
  151.9 5.3 %collective-permute-start.4 = (bf16[320,128]{1,0:T(8,128)(2,1)}, bf16[320,128]{1,0:T(8,128)(2,1)S(1)}, u32[]{:S(2)}, u32[]{:S(2)}) collective-permute-start(bf16[320,128]{1,0:T(8,128)(2,1)} %get-tuple-element.128), channel_id=1, source_target_pairs={{0,16},{8,24},{16,0},{24,8},{1,17},{9,25},{17,1},{25,9},{2,18},{10... | collective-permute-start | bytes 245768 | tf_op jit(solution)/shard_map/ppermute | solution.py:850
  153.5 4.9 %collective-permute-start.5 = (bf16[320,128]{1,0:T(8,128)(2,1)}, bf16[320,128]{1,0:T(8,128)(2,1)S(1)}, u32[]{:S(2)}, u32[]{:S(2)}) collective-permute-start(bf16[320,128]{1,0:T(8,128)(2,1)} %get-tuple-element.129), channel_id=1, source_target_pairs={{0,24},{8,16},{16,8},{24,0},{1,25},{9,17},{17,9},{25,1},{2,26},{10... | collective-permute-start | bytes 245768 | tf_op jit(solution)/shard_map/ppermute | solution.py:850
  158.4 0.9 copy-start.4
  175.2 22.0 %copy-start = (f32[6,192,192]{2,1,0:T(8,128)S(1)}, f32[6,192,192]{2,1,0:T(8,128)}, u32[]{:S(2)}) copy-start(f32[6,192,192]{2,1,0:T(8,128)} %refs_5_.1) | copy-start | bytes 2654212
  175.2 22.0 %copy-start.1 = (f32[192,768]{1,0:T(8,128)S(1)}, f32[192,768]{1,0:T(8,128)}, u32[]{:S(2)}) copy-start(f32[192,768]{1,0:T(8,128)} %refs_7_.1) | copy-start | bytes 1769476
  175.2 22.0 %copy-start.2 = (f32[768,192]{0,1:T(8,128)S(1)}, f32[768,192]{0,1:T(8,128)}, u32[]{:S(2)}) copy-start(f32[768,192]{0,1:T(8,128)} %param.24) | copy-start | bytes 1769476
  175.2 22.1 %copy-start.3 = (f32[2,192,192]{2,1,0:T(8,128)S(1)}, f32[2,192,192]{2,1,0:T(8,128)}, u32[]{:S(2)}) copy-start(f32[2,192,192]{2,1,0:T(8,128)} %refs_6_.1) | copy-start | bytes 884740
  175.3 22.1 %copy-start.5 = (f32[6,192]{1,0:T(8,128)S(1)}, f32[6,192]{1,0:T(8,128)}, u32[]{:S(2)}) copy-start(f32[6,192]{1,0:T(8,128)} %refs_9_.1) | copy-start | bytes 13828
  175.3 22.1 %copy-start.6 = (f32[8,192]{1,0:T(8,128)S(1)}, f32[8,192]{1,0:T(8,128)}, u32[]{:S(2)}) copy-start(f32[8,192]{1,0:T(8,128)} %refs_10_.1) | copy-start | bytes 18436
  175.3 22.1 %copy-start.7 = (f32[8,192]{1,0:T(8,128)S(1)}, f32[8,192]{1,0:T(8,128)}, u32[]{:S(2)}) copy-start(f32[8,192]{1,0:T(8,128)} %refs_11_.1) | copy-start | bytes 18436
  175.3 22.1 %copy-start.8 = (f32[6,192]{1,0:T(8,128)S(1)}, f32[6,192]{1,0:T(8,128)}, u32[]{:S(2)}) copy-start(f32[6,192]{1,0:T(8,128)} %refs_14_.1) | copy-start | bytes 13828
  175.3 22.0 %copy-start.9 = (f32[2,768]{1,0:T(2,128)S(1)}, f32[2,768]{1,0:T(2,128)}, u32[]{:S(2)}) copy-start(f32[2,768]{1,0:T(2,128)} %refs_13_.1) | copy-start | bytes 18436
  175.3 22.0 %copy-start.10 = (f32[2,192]{1,0:T(2,128)S(1)}, f32[2,192]{1,0:T(2,128)}, u32[]{:S(2)}) copy-start(f32[2,192]{1,0:T(2,128)} %refs_12_.1) | copy-start | bytes 4612
  188.8 6.9 %collective-permute-start.7 = (bf16[8,152,128]{2,1,0:T(8,128)(2,1)S(1)}, bf16[8,152,128]{2,1,0:T(8,128)(2,1)S(1)}, u32[]{:S(2)}, u32[]{:S(2)}) collective-permute-start(bf16[8,152,128]{2,1,0:T(8,128)(2,1)S(1)} %all_to_all.21.refs_1_), channel_id=1, source_target_pairs={{0,16},{8,24},{16,0},{24,8},{1,17},{9,25},{17,1},{25,9},{2,18},{10... | collective-permute-start | bytes 933896 | tf_op jit(solution)/shard_map/ppermute | solution.py:904
  190.1 5.6 %collective-permute-start.6 = (bf16[8,152,128]{2,1,0:T(8,128)(2,1)S(1)}, bf16[8,152,128]{2,1,0:T(8,128)(2,1)S(1)}, u32[]{:S(2)}, u32[]{:S(2)}) collective-permute-start(bf16[8,152,128]{2,1,0:T(8,128)(2,1)S(1)} %all_to_all.21.refs_1_), channel_id=1, source_target_pairs={{0,8},{8,0},{16,24},{24,16},{1,9},{9,1},{17,25},{25,17},{2,10},{10... | collective-permute-start | bytes 933896 | tf_op jit(solution)/shard_map/ppermute | solution.py:905
  195.7 1.6 collective-permute-start.8

commit v5 on v4

--- a/solution.py
+++ b/solution.py
@@ -628,7 +628,7 @@
         hand_out(table_ref, pack_ref, piece_refs)
 
 
-def item_and_dense(table, ht, qt, ct, slots, perm, ws, vec, packed, tables, OFF=0, CC=384, WC=192):
+def item_and_dense(table, ht, qt, ct, slots, perm, ws, vec, packed, tables, OFF=0, CC=384, WC=384):
     RW = ht.shape[1]
     keys = 2 * slots.shape[0]
     FB, AO, AS, WP = (20, 2, 2, 2) if keys <= 32 else (8, 2, 6, 4)

time: 203 us -> 204 us (level)
  no operation moved by 1% of the time
where the time goes in v5:
time: 204 us; the launch traced here: 203 us
  Pallas kernels  137 us (67%)
  blocking collectives  28 us (14%)
  waiting for transfers between devices  18.4 us (9%)
  starting transfers between devices  16.7 us (8%)
  local copies, waits for them, and re-layouts  2.05 us (1%)
    pallas_call x1, Pallas kernels, item_and_dense(): pl.pallas_call(functools.partial(item_kernel, FB, RW, keys, tables, OFF,...  58.3 us
    pallas_call x1, Pallas kernels, feature_backward(): pl.pallas_call(functools.partial(backward_kernel, R, OFF, YO), grid=(rows...  30.4 us
    pallas_call x1, Pallas kernels, feature_forward(): pl.pallas_call(functools.partial(forward_kernel, R, OFF), grid=(rows // R...  27.1 us
    all_to_all x1, blocking collectives, sum_rows(): parts = lax.all_to_all(parts, 'rows', 0, 0)  14.6 us
    all_to_all x1, blocking collectives, gather_all(): own = lax.all_to_all(copies, 'rows', 0, 0)  13.4 us
    all_to_all x1, starting transfers between devices, on_device(): slots = lax.all_to_all(own, 'rows', 0, 0).reshape((-1,) + own.shape[2:])  7.26 us
    pallas_call x1, Pallas kernels, slots_backward(): pl.pallas_call(functools.partial(slots_back_kernel, SL, tables), grid=(1,...  6.07 us
    ppermute x1, waiting for transfers between devices, gather_all(): lax.ppermute(own, 'table', [(t, (t // 2 + s) % ny * 2 + t % 2) for t in r...  5.56 us
  transfers between devices with their start and end apart: 11, of which 6 were waited for; matrix products, arithmetic and copies ran while one was open for 0% of the time, Pallas kernels for 30%

profile of v5, /device:TPU:0, one launch (start us, length us, event | category | flops | bytes accessed | tf_op | source)
XLA Modules:
  0.0 203.4 jit_solution(2610959241629964842)
XLA Ops:
  1.3 4.6 %slot_rows.1 = (bf16[8,2,120,384]{3,2,1,0:T(8,128)(2,1)}, bf16[576,256]{1,0:T(8,128)(2,1)}, bf16[192,256]{1,0:T(8,128)(2,1)}, f32[6,192,128]{2,1,0:T(8,128)}) custom-call(s32[1]{0:T(128)S(6)} %copy.35.count_ref, s32[1,4]{1,0:T(1,128)} %mask_ref.1, s32[1,4]{1,0:T(1,128)} %order_ref.1, bf16[64,192,119]{2,1,0:T(8,128)(2,1)} %bitcast.21, ...), custom_call_target="tpu_custom_call" | custom-call | flops 6600000000 | bytes 6000000 | tf_op jit(solution)/shard_map/slot_rows/pallas_call | solution.py:257
  5.9 7.3 %all-to-all-start = ((bf16[8,2,120,384]{3,2,1,0:T(8,128)(2,1)}), bf16[8,2,120,384]{3,2,1,0:T(8,128)(2,1)S(1)}, u32[]{:S(2)}, u32[]{:S(2)}) async-start(bf16[8,2,120,384]{3,2,1,0:T(8,128)(2,1)} %get-tuple-element.84), calls=%async_computation | async-start | bytes 2949120 | tf_op jit(solution)/shard_map/all_to_all | solution.py:1050
  13.1 3.4 %other_weights.1 = (bf16[192,768]{1,0:T(8,128)(2,1)}, bf16[192,256]{1,0:T(8,128)(2,1)}, bf16[256,512]{1,0:T(8,128)(2,1)}, bf16[512,256]{1,0:T(8,128)(2,1)}, bf16...) custom-call(f32[6,192,192]{2,1,0:T(8,128)} %refs_5_.1, ...), custom_call_target="tpu_custom_call" | custom-call | flops 4400000000 | bytes 4000000 | tf_op jit(solution)/shard_map/other_weights/pallas_call | solution.py:170
  16.5 27.1 %feature_forward.1 = (bf16[128,64,256]{2,1,0:T(8,128)(2,1)}, bf16[128,64,256]{2,1,0:T(8,128)(2,1)}, bf16[128,64,256]{2,1,0:T(8,128)(2,1)}, bf16[64,208,128]{2,1,...) custom-call(bf16[64,192,119]{2,1,0:T(8,128)(2,1)} %bitcast.22, ...), custom_call_target="tpu_custom_call" | custom-call | flops 39600001024 | bytes 36000000 | tf_op jit(solution)/shard_map/feature_forward/pallas_call | solution.py:331
  43.7 4.3 %all-to-all-done = bf16[8,2,120,384]{3,2,1,0:T(8,128)(2,1)S(1)} async-done(((bf16[8,2,120,384]{3,2,1,0:T(8,128)(2,1)}), bf16[8,2,120,384]{3,2,1,0:T(8,128)(2,1)S(1)}, u32[]{:S(2)}, u32[]{:S(2)}) %all-to-all-start) | async-done | bytes 1474592 | tf_op jit(solution)/shard_map/all_to_all | solution.py:1050
  48.0 0.0 copy-start.12
  48.0 1.1 copy-done.12
  49.1 58.3 %item_and_dense.1 = (bf16[120,64,256]{2,1,0:T(8,128)(2,1)}, bf16[120,64,256]{2,1,0:T(8,128)(2,1)}, bf16[16,120,384]{2,1,0:T(8,128)(2,1)}, bf16[896,128]{1,0:T(8,...) custom-call(s32[1]{0:T(128)} %bitcast.6.table_ref.refs_0_, ...), custom_call_target="tpu_custom_call" | custom-call | flops 72600002560 | bytes 66000000 | tf_op jit(solution)/shard_map/item_and_dense/pallas_call | solution.py:643
  107.4 4.3 %all-to-all-start.1 = ((bf16[8,2,120,384]{3,2,1,0:T(8,128)(2,1)}), bf16[8,2,120,384]{3,2,1,0:T(8,128)(2,1)}, u32[]{:S(2)}, u32[]{:S(2)}) async-start(bf16[8,2,120,384]{3,2,1,0:T(8,128)(2,1)} %bitcast.25), calls=%async_computation.1 | async-start | bytes 2949120 | tf_op jit(solution)/shard_map/all_to_all | solution.py:1056
  111.7 0.1 collective-permute-start
  111.8 1.6 collective-permute-start.1
  113.4 0.3 collective-permute-start.2
  113.7 30.4 %feature_backward.1 = (f32[64,192,119]{2,1,0:T(8,128)}, bf16[64,192,119]{2,1,0:T(8,128)(2,1)}, f32[576,192]{1,0:T(8,128)}, f32[192,192]{1,0:T(8,128)}, f32[2,192,128]{2,1,0:T(8,128)}) custom-call(bf16[64,192,119]{2,1,0:T(8,128)(2,1)} %bitcast.23, bf16[64,208,128]{2,1,0:T(8,128)(2,1)} %get-tuple-element.87.n_ref, ...), custom_call_target="tpu_custom_call" | custom-call | flops 263999995904 | bytes 240000000 | tf_op jit(solution)/shard_map/feature_backward/pallas_call | solution.py:773
  144.1 0.0 collective-permute-done.refs_1_
  144.1 0.0 collective-permute-done.1.refs_2_
  144.1 0.0 collective-permute-done.2.refs_3_
  144.2 2.1 %all-to-all-done.1.slot_ref = bf16[8,2,120,384]{3,2,1,0:T(8,128)(2,1)} async-done(((bf16[8,2,120,384]{3,2,1,0:T(8,128)(2,1)}), bf16[8,2,120,384]{3,2,1,0:T(8,128)(2,1)}, u32[]{:S(2)}, u32[]{:S(2)}) %all-to-all-start.1) | async-done | bytes 1474592 | tf_op jit(solution)/shard_map/all_to_all | solution.py:1056
  146.3 0.0 copy-start.11
  146.3 6.1 %slots_backward.1 = (f32[64,192,119]{2,1,0:T(8,128)}, bf16[320,128]{1,0:T(8,128)(2,1)}, bf16[320,128]{1,0:T(8,128)(2,1)}, bf16[320,128]{1,0:T(8,128)(2,1)}, bf16[320,128]{1,0:T(8,128)(2,1)}) custom-call(s32[1]{0:T(128)} %bitcast.6.table_ref.refs_0_, bf16[64,192,119]{2,1,0:T(8,128)(2,1)} %bitcast.24, ...), custom_call_target="tpu_custom_call", output_to_operand_aliasing={{0}: (8, {})} | custom-call | flops 8800000000 | bytes 8000000 | tf_op jit(solution)/shard_map/slots_backward/pallas_call | solution.py:827
  152.4 0.0 collective-permute-start.3
  152.4 1.6 collective-permute-start.4
  154.0 0.3 collective-permute-start.5
  154.2 0.0 collective-permute-done.3.refs_5_
  154.2 3.5 %collective-permute-done.4.refs_6_ = bf16[320,128]{1,0:T(8,128)(2,1)S(1)} collective-permute-done((bf16[320,128]{1,0:T(8,128)(2,1)}, bf16[320,128]{1,0:T(8,128)(2,1)S(1)}, u32[]{:S(2)}, u32[]{:S(2)}) %collective-permute-start.4) | collective-permute-done | bytes 81952 | tf_op jit(solution)/shard_map/ppermute | solution.py:850
  157.7 1.2 collective-permute-done.5.refs_7_
  158.9 0.0 copy-done.11
  158.9 0.0 copy-start.4
  158.9 0.9 copy-done.4
  159.8 1.3 join_tables.1
  161.1 14.6 %all_to_all.20.parts_ref = bf16[8,152,128]{2,1,0:T(8,128)(2,1)S(1)} all-to-all(bf16[8,152,128]{2,1,0:T(8,128)(2,1)S(1)} %join_tables.1), channel_id=1, replica_groups=mesh['table'=4,'rows'=8] {'rows'}, dimensions={0} | all-to-all | bytes 622592 | tf_op jit(solution)/shard_map/all_to_all | solution.py:888
  175.7 0.0 copy-start
  175.8 0.0 copy-start.1
  175.8 0.0 copy-start.2
  175.8 0.0 copy-start.3
  175.8 0.0 copy-start.5
  175.8 0.0 copy-start.6
  175.8 0.0 copy-start.7
  175.8 0.0 copy-start.8
  175.8 0.0 copy-start.9
  175.8 0.0 copy-start.10
  175.8 0.1 sum_rows.1
  175.9 13.4 %all_to_all.21.refs_1_ = bf16[8,152,128]{2,1,0:T(8,128)(2,1)S(1)} all-to-all(bf16[8,152,128]{2,1,0:T(8,128)(2,1)S(1)} %sum_rows.1), channel_id=1, replica_groups=mesh['table'=4,'rows'=8] {'rows'}, dimensions={0} | all-to-all | bytes 622592 | tf_op jit(solution)/shard_map/all_to_all | solution.py:901
  189.3 1.3 collective-permute-start.7
  190.6 0.0 collective-permute-start.6
  190.6 5.6 %collective-permute-done.7.refs_3_ = bf16[8,152,128]{2,1,0:T(8,128)(2,1)S(1)} collective-permute-done((bf16[8,152,128]{2,1,0:T(8,128)(2,1)S(1)}, bf16[8,152,128]{2,1,0:T(8,128)(2,1)S(1)}, u32[]{:S(2)}, u32[]{:S(2)}) %collective-permute-start.7) | collective-permute-done | bytes 311328 | tf_op jit(solution)/shard_map/ppermute | solution.py:904
  196.2 0.0 collective-permute-start.8
  196.2 0.0 collective-permute-done.6.refs_2_
  196.2 1.6 collective-permute-done.8.refs_4_
  197.8 0.0 copy-done
  197.8 0.0 copy-done.1
  197.8 0.0 copy-done.2
  197.8 0.0 copy-done.3
  197.8 0.0 copy-done.5
  197.8 0.0 copy-done.6
  197.8 0.0 copy-done.7
  197.8 0.0 copy-done.8
  197.9 0.0 copy-done.9
  197.9 0.0 copy-done.10
  197.9 5.5 %optimizer.1 = (f32[6,192,192]{2,1,0:T(8,128)}, f32[2,192,192]{2,1,0:T(8,128)}, f32[192,768]{1,0:T(8,128)}, f32[192,768]{1,0:T(8,128)}, f32[6,192]{1,0:T(8,128)}...) custom-call(s32[1]{0:T(128)} %bitcast.6.table_ref.refs_0_, ...), custom_call_target="tpu_custom_call" | custom-call | flops 8800000000 | bytes 8000000 | tf_op jit(solution)/shard_map/optimizer/pallas_call | solution.py:1019
Async XLA Ops:
  5.9 42.1 %all-to-all-start = ((bf16[8,2,120,384]{3,2,1,0:T(8,128)(2,1)}), bf16[8,2,120,384]{3,2,1,0:T(8,128)(2,1)S(1)}, u32[]{:S(2)}, u32[]{:S(2)}) async-start(bf16[8,2,120,384]{3,2,1,0:T(8,128)(2,1)} %get-tuple-element.84), calls=%async_computation | async-start | bytes 2949120 | tf_op jit(solution)/shard_map/all_to_all | solution.py:1050
  48.0 1.1 copy-start.12
  107.4 38.9 %all-to-all-start.1 = ((bf16[8,2,120,384]{3,2,1,0:T(8,128)(2,1)}), bf16[8,2,120,384]{3,2,1,0:T(8,128)(2,1)}, u32[]{:S(2)}, u32[]{:S(2)}) async-start(bf16[8,2,120,384]{3,2,1,0:T(8,128)(2,1)} %bitcast.25), calls=%async_computation.1 | async-start | bytes 2949120 | tf_op jit(solution)/shard_map/all_to_all | solution.py:1056
  111.7 32.4 %collective-permute-start = (bf16[896,128]{1,0:T(8,128)(2,1)}, bf16[896,128]{1,0:T(8,128)(2,1)}, u32[]{:S(2)}, u32[]{:S(2)}) collective-permute-start(bf16[896,128]{1,0:T(8,128)(2,1)} %get-tuple-element.112), channel_id=1, source_target_pairs={{0,8},{8,0},{16,24},{24,16},{1,9},{9,1},{17,25},{25,17},{2,10},{10... | collective-permute-start | bytes 688136 | tf_op jit(solution)/shard_map/ppermute | solution.py:850
  111.8 32.3 %collective-permute-start.1 = (bf16[896,128]{1,0:T(8,128)(2,1)}, bf16[896,128]{1,0:T(8,128)(2,1)}, u32[]{:S(2)}, u32[]{:S(2)}) collective-permute-start(bf16[896,128]{1,0:T(8,128)(2,1)} %get-tuple-element.113), channel_id=1, source_target_pairs={{0,16},{8,24},{16,0},{24,8},{1,17},{9,25},{17,1},{25,9},{2,18},{10... | collective-permute-start | bytes 688136 | tf_op jit(solution)/shard_map/ppermute | solution.py:850
  113.4 30.7 %collective-permute-start.2 = (bf16[896,128]{1,0:T(8,128)(2,1)}, bf16[896,128]{1,0:T(8,128)(2,1)}, u32[]{:S(2)}, u32[]{:S(2)}) collective-permute-start(bf16[896,128]{1,0:T(8,128)(2,1)} %get-tuple-element.114), channel_id=1, source_target_pairs={{0,24},{8,16},{16,8},{24,0},{1,25},{9,17},{17,9},{25,1},{2,26},{10... | collective-permute-start | bytes 688136 | tf_op jit(solution)/shard_map/ppermute | solution.py:850
  146.3 12.6 %copy-start.11 = (bf16[896,128]{1,0:T(8,128)(2,1)S(1)}, bf16[896,128]{1,0:T(8,128)(2,1)}, u32[]{:S(2)}) copy-start(bf16[896,128]{1,0:T(8,128)(2,1)} %get-tuple-element.122.refs_0_) | copy-start | bytes 688132
  152.4 1.9 collective-permute-start.3
  152.4 5.3 %collective-permute-start.4 = (bf16[320,128]{1,0:T(8,128)(2,1)}, bf16[320,128]{1,0:T(8,128)(2,1)S(1)}, u32[]{:S(2)}, u32[]{:S(2)}) collective-permute-start(bf16[320,128]{1,0:T(8,128)(2,1)} %get-tuple-element.128), channel_id=1, source_target_pairs={{0,16},{8,24},{16,0},{24,8},{1,17},{9,25},{17,1},{25,9},{2,18},{10... | collective-permute-start | bytes 245768 | tf_op jit(solution)/shard_map/ppermute | solution.py:850
  154.0 4.9 %collective-permute-start.5 = (bf16[320,128]{1,0:T(8,128)(2,1)}, bf16[320,128]{1,0:T(8,128)(2,1)S(1)}, u32[]{:S(2)}, u32[]{:S(2)}) collective-permute-start(bf16[320,128]{1,0:T(8,128)(2,1)} %get-tuple-element.129), channel_id=1, source_target_pairs={{0,24},{8,16},{16,8},{24,0},{1,25},{9,17},{17,9},{25,1},{2,26},{10... | collective-permute-start | bytes 245768 | tf_op jit(solution)/shard_map/ppermute | solution.py:850
  158.9 0.9 copy-start.4
  175.7 22.0 %copy-start = (f32[6,192,192]{2,1,0:T(8,128)S(1)}, f32[6,192,192]{2,1,0:T(8,128)}, u32[]{:S(2)}) copy-start(f32[6,192,192]{2,1,0:T(8,128)} %refs_5_.1) | copy-start | bytes 2654212
  175.8 22.0 %copy-start.1 = (f32[192,768]{1,0:T(8,128)S(1)}, f32[192,768]{1,0:T(8,128)}, u32[]{:S(2)}) copy-start(f32[192,768]{1,0:T(8,128)} %refs_7_.1) | copy-start | bytes 1769476
  175.8 22.0 %copy-start.2 = (f32[768,192]{0,1:T(8,128)S(1)}, f32[768,192]{0,1:T(8,128)}, u32[]{:S(2)}) copy-start(f32[768,192]{0,1:T(8,128)} %param.24) | copy-start | bytes 1769476
  175.8 22.1 %copy-start.3 = (f32[2,192,192]{2,1,0:T(8,128)S(1)}, f32[2,192,192]{2,1,0:T(8,128)}, u32[]{:S(2)}) copy-start(f32[2,192,192]{2,1,0:T(8,128)} %refs_6_.1) | copy-start | bytes 884740
  175.8 22.1 %copy-start.5 = (f32[6,192]{1,0:T(8,128)S(1)}, f32[6,192]{1,0:T(8,128)}, u32[]{:S(2)}) copy-start(f32[6,192]{1,0:T(8,128)} %refs_9_.1) | copy-start | bytes 13828
  175.8 22.1 %copy-start.6 = (f32[8,192]{1,0:T(8,128)S(1)}, f32[8,192]{1,0:T(8,128)}, u32[]{:S(2)}) copy-start(f32[8,192]{1,0:T(8,128)} %refs_10_.1) | copy-start | bytes 18436
  175.8 22.1 %copy-start.7 = (f32[8,192]{1,0:T(8,128)S(1)}, f32[8,192]{1,0:T(8,128)}, u32[]{:S(2)}) copy-start(f32[8,192]{1,0:T(8,128)} %refs_11_.1) | copy-start | bytes 18436
  175.8 22.1 %copy-start.8 = (f32[6,192]{1,0:T(8,128)S(1)}, f32[6,192]{1,0:T(8,128)}, u32[]{:S(2)}) copy-start(f32[6,192]{1,0:T(8,128)} %refs_14_.1) | copy-start | bytes 13828
  175.8 22.0 %copy-start.9 = (f32[2,768]{1,0:T(2,128)S(1)}, f32[2,768]{1,0:T(2,128)}, u32[]{:S(2)}) copy-start(f32[2,768]{1,0:T(2,128)} %refs_13_.1) | copy-start | bytes 18436
  175.8 22.0 %copy-start.10 = (f32[2,192]{1,0:T(2,128)S(1)}, f32[2,192]{1,0:T(2,128)}, u32[]{:S(2)}) copy-start(f32[2,192]{1,0:T(2,128)} %refs_12_.1) | copy-start | bytes 4612
  189.3 6.9 %collective-permute-start.7 = (bf16[8,152,128]{2,1,0:T(8,128)(2,1)S(1)}, bf16[8,152,128]{2,1,0:T(8,128)(2,1)S(1)}, u32[]{:S(2)}, u32[]{:S(2)}) collective-permute-start(bf16[8,152,128]{2,1,0:T(8,128)(2,1)S(1)} %all_to_all.21.refs_1_), channel_id=1, source_target_pairs={{0,16},{8,24},{16,0},{24,8},{1,17},{9,25},{17,1},{25,9},{2,18},{10... | collective-permute-start | bytes 933896 | tf_op jit(solution)/shard_map/ppermute | solution.py:904
  190.6 5.6 %collective-permute-start.6 = (bf16[8,152,128]{2,1,0:T(8,128)(2,1)S(1)}, bf16[8,152,128]{2,1,0:T(8,128)(2,1)S(1)}, u32[]{:S(2)}, u32[]{:S(2)}) collective-permute-start(bf16[8,152,128]{2,1,0:T(8,128)(2,1)S(1)} %all_to_all.21.refs_1_), channel_id=1, source_target_pairs={{0,8},{8,0},{16,24},{24,16},{1,9},{9,1},{17,25},{25,17},{2,10},{10... | collective-permute-start | bytes 933896 | tf_op jit(solution)/shard_map/ppermute | solution.py:905
  196.2 1.6 collective-permute-start.8
